TPU v7x, 32 devices: a whole 2x2x4 slice. The times are simulated.
32 devices in a mesh: row: 2 (over y), col: 4 (over z), leaf: 4 (over x, core).
Axes of the slice: x: 2, y: 2, z: 4, core: 2. Of those that a mesh axis runs over, the one named last changes fastest.
Arguments:
- rhs_leaf: float32 [4, 8192, 128], P('leaf', 'row'), may hold values from -6 to 6
- rhs_mid: float32 [2, 8192, 128], P(None, 'row'), may hold values from -6 to 6
- rhs_root: float32 [8192, 128], P('row'), may hold values from -6 to 6
- inverse_leaf: bfloat16 [4, 8192, 8192], P('leaf', 'col', 'row'), may hold values from -3 to 3, as said below
- inverse_mid: bfloat16 [2, 8192, 8192], P(None, ('col', 'leaf'), 'row'), may hold values from -3 to 3, as said below
- inverse_root: bfloat16 [8192, 8192], P(('col', 'leaf'), 'row'), may hold values from -3 to 3, as said below
- factor_leaf_mid: bfloat16 [4, 8192, 8192], P('leaf', 'row', 'col'), may hold values from -0.0625 to 0.0625
- factor_leaf_root: bfloat16 [4, 8192, 8192], P('leaf', 'row', 'col'), may hold values from -0.0625 to 0.0625
- factor_mid_root: bfloat16 [2, 8192, 8192], P(None, 'row', ('col', 'leaf')), may hold values from -0.0625 to 0.0625
- pattern_leaf_mid: int32 [4, 32, 32], P('leaf', 'row', 'col'), may hold values 0 or 1
- pattern_leaf_root: int32 [4, 32, 32], P('leaf', 'row', 'col'), may hold values 0 or 1
- pattern_mid_root: int32 [2, 32, 32], P(None, 'row', ('col', 'leaf')), may hold values 0 or 1
Outputs:
- solve_leaf: float32 [4, 8192, 128], P('leaf', 'row')
- solve_mid: float32 [2, 8192, 128], P(None, 'row')
- solve_root: float32 [8192, 128], P('row')
- forward_root: float32 [8192, 128], P(('col', 'leaf'))
Inputs may be any that keep to these rules, and one draw needn't show every extreme that they name: `inverse_leaf`: lower triangular, with a positive diagonal. `inverse_mid`: lower triangular, with a positive diagonal. `inverse_root`: lower triangular, with a positive diagonal.
All inputs are finite; a program needn't handle non-finite values. No bound on the sum of `pattern_leaf_mid` or of `pattern_leaf_root` or of `pattern_mid_root` on one device may be relied on, other than what follows from the above.
Results may differ from a plain program's by a relative error of at most 0.018.
Values sent between devices are 32-bit elements; how exact they have to be, the bound alone decides.
No kernel may reach another device: no remote copies, remote signals or barrier semaphores. Data moves between devices by JAX's collectives and lax.ppermute only.
A program may use at most 256 MiB of HBM per device.

v0:
```python
import jax
import jax.numpy as jnp
from jax import lax
from jax.sharding import PartitionSpec as P


def masked_blocks(matrix, pattern):
    leading, row_count, col_count = matrix.shape
    block_rows = pattern.shape[1]
    block_cols = pattern.shape[2]
    tiles = matrix.reshape(
        leading, block_rows, row_count // block_rows, block_cols, col_count // block_cols
    )
    keeper = pattern.astype(matrix.dtype)[:, :, None, :, None]
    return (tiles * keeper).reshape(leading, row_count, col_count)


def row_total(partial_sum):
    return lax.psum(partial_sum, "row")


def branch_total(partial_sum):
    return lax.psum(partial_sum, ("col", "leaf"))


def shards(
    rhs_leaf,
    rhs_mid,
    rhs_root,
    inverse_leaf,
    inverse_mid,
    inverse_root,
    factor_leaf_mid,
    factor_leaf_root,
    factor_mid_root,
    pattern_leaf_mid,
    pattern_leaf_root,
    pattern_mid_root,
):
    leaf_mid = masked_blocks(factor_leaf_mid, pattern_leaf_mid)[0]
    leaf_root = masked_blocks(factor_leaf_root, pattern_leaf_root)[0]
    mid_root = masked_blocks(factor_mid_root, pattern_mid_root)
    leaf_inverse = inverse_leaf[0]
    owner_mid = lax.axis_index("leaf") // 2
    forward_leaf = row_total(
        jnp.dot(leaf_inverse, rhs_leaf[0].astype(jnp.bfloat16), preferred_element_type=jnp.float32)[
            None
        ]
    )
    leaf_half = forward_leaf[0].astype(jnp.bfloat16)
    to_mid = jnp.dot(leaf_mid, leaf_half, preferred_element_type=jnp.float32)
    to_root = jnp.dot(leaf_root, leaf_half, preferred_element_type=jnp.float32)
    selector = (jnp.arange(2) == owner_mid).astype(jnp.float32)[:, None, None]
    mid_terms = lax.psum(selector * to_mid[None], ("col", "leaf"))
    residue_mid = rhs_mid - mid_terms
    forward_mid = row_total(
        jnp.einsum(
            "pij,pjk->pik",
            inverse_mid,
            residue_mid.astype(jnp.bfloat16),
            preferred_element_type=jnp.float32,
        )
    )
    mid_half = forward_mid.astype(jnp.bfloat16)
    root_partial = to_root + jnp.einsum(
        "pij,pjk->ik", mid_root, mid_half, preferred_element_type=jnp.float32
    )
    residue_root = rhs_root - branch_total(root_partial)
    forward_root = row_total(
        jnp.dot(
            inverse_root, residue_root.astype(jnp.bfloat16), preferred_element_type=jnp.float32
        )[None]
    )
    root_half = forward_root[0].astype(jnp.bfloat16)
    solve_root = branch_total(
        jnp.einsum("ji,jk->ik", inverse_root, root_half, preferred_element_type=jnp.float32)
    )
    root_back = solve_root.astype(jnp.bfloat16)
    corrected_mid = forward_mid - row_total(
        jnp.einsum("pji,jk->pik", mid_root, root_back, preferred_element_type=jnp.float32)
    )
    solve_mid = branch_total(
        jnp.einsum(
            "pji,pjk->pik",
            inverse_mid,
            corrected_mid.astype(jnp.bfloat16),
            preferred_element_type=jnp.float32,
        )
    )
    mid_back = lax.dynamic_index_in_dim(solve_mid, owner_mid, 0, keepdims=False).astype(
        jnp.bfloat16
    )
    back_partial = jnp.einsum("ji,jk->ik", leaf_mid, mid_back, preferred_element_type=jnp.float32)
    back_partial = back_partial + jnp.einsum(
        "ji,jk->ik", leaf_root, root_back, preferred_element_type=jnp.float32
    )
    corrected_leaf = forward_leaf - row_total(back_partial[None])
    leaf_terms = jnp.einsum(
        "ji,jk->ik",
        leaf_inverse,
        corrected_leaf[0].astype(jnp.bfloat16),
        preferred_element_type=jnp.float32,
    )
    solve_leaf = lax.psum(leaf_terms, "col")[None]
    return (solve_leaf, solve_mid, solve_root, forward_root[0])


def solution(mesh):
    return jax.shard_map(
        shards,
        mesh=mesh,
        in_specs=(
            P("leaf", "row", None),
            P(None, "row", None),
            P("row", None),
            P("leaf", "col", "row"),
            P(None, ("col", "leaf"), "row"),
            P(("col", "leaf"), "row"),
            P("leaf", "row", "col"),
            P("leaf", "row", "col"),
            P(None, "row", ("col", "leaf")),
            P("leaf", "row", "col"),
            P("leaf", "row", "col"),
            P(None, "row", ("col", "leaf")),
        ),
        out_specs=(
            P("leaf", "row", None),
            P(None, "row", None),
            P("row", None),
            P(("col", "leaf"), None),
        ),
        check_vma=False,
    )
```

profile of v0, /device:TPU:8, one launch (start us, length us, event | category | flops | bytes accessed | tf_op | source)
XLA Modules:
  0.0 774.9 jit_solution(16371570130385999379)
XLA Ops:
  7.2 0.0 all-reduce.11.cloned.1.call-start
  7.2 11.9 %fusion.18 = f32[1,2048,128]{2,1,0:T(8,128)} fusion(bf16[1,2048,4096]{2,1,0:T(8,128)(2,1)} %param.15, f32[1,4096,128]{2,1,0:T(8,128)} %param.12), kind=kOutput, calls=%fused_computation.21 | convolution fusion | flops 2148007936 | bytes 19922944 | tf_op jit(solution)/shard_map/dot_general | solution.py:46
  19.1 0.0 all-reduce.13.cloned.1.call-start
  19.2 0.1 copy.16
  19.3 5.9 mul.66
  25.2 25.8 %mul.67 = bf16[1,4096,2048]{2,1,0:T(8,128)(2,1)} reshape(bf16[16,256,8,256]{3,2,1,0:T(8,128)(2,1)} %mul.66) | data formatting | bytes 33554432 | tf_op jit(solution)/shard_map/mul | solution.py:15
  51.0 9.5 %all-reduce.11.cloned.1.call-done = f32[1,2048,128]{2,1,0:T(8,128)} async-done(((f32[1,2048,128]{2,1,0:T(8,128)}), f32[1,2048,128]{2,1,0:T(8,128)}) %all-reduce.11.cloned.1.call-update) | async-done | bytes 1048592 | tf_op jit(solution)/shard_map/psum | solution.py:19
  60.5 13.3 %fusion.5 = f32[4096,128]{1,0:T(8,128)S(1)} fusion(bf16[1,4096,2048]{2,1,0:T(8,128)(2,1)} %param.18, bf16[1,4096,2048]{2,1,0:T(8,128)(2,1)} %mul.67, f32[1,2048,128]{2,1,0:T(8,128)} %all-reduce.11.cloned.1.call-done), kind=kOutput, calls=%fused_computation.6 | convolution fusion | flops 2156134400 | bytes 36700160 | tf_op jit(solution)/shard_map/dot_general | solution.py:51
  73.8 2.4 broadcast_multiply_fusion
  76.2 0.0 all-reduce.15.cloned.1.call-start
  76.3 0.1 copy.19
  76.4 6.0 mul.77
  82.4 25.8 %mul.78 = bf16[1,4096,2048]{2,1,0:T(8,128)(2,1)} reshape(bf16[16,256,8,256]{3,2,1,0:T(8,128)(2,1)} %mul.77) | data formatting | bytes 33554432 | tf_op jit(solution)/shard_map/mul | solution.py:15
  108.2 0.1 copy.18
  108.3 6.6 mul.73
  114.9 14.1 %mul.74 = bf16[2,4096,512]{2,1,0:T(8,128)(2,1)} reshape(bf16[2,16,256,2,256]{4,3,2,1,0:T(2,128)(2,1)} %mul.73) | data formatting | bytes 16777216 | tf_op jit(solution)/shard_map/mul | solution.py:15
  129.1 9.8 %mul.75 = bf16[2,4096,512]{2,1,0:T(8,128)(2,1)} multiply(bf16[2,4096,512]{2,1,0:T(8,128)(2,1)} %param.20, bf16[2,4096,512]{2,1,0:T(8,128)(2,1)} %mul.74) | non-fusion elementwise | flops 4194304 | bytes 25165824 | tf_op jit(solution)/shard_map/mul | solution.py:15
  138.8 48.8 %all-reduce.13.cloned.1.call-done = f32[2,4096,128]{2,1,0:T(8,128)} async-done(((f32[2,4096,128]{2,1,0:T(8,128)}), f32[2,4096,128]{2,1,0:T(8,128)}) %all-reduce.13.cloned.1.call-update) | async-done | bytes 4194320 | tf_op jit(solution)/shard_map/psum | solution.py:54
  187.6 9.5 %fusion.28 = f32[2,512,128]{1,2,0:T(8,128)} fusion(bf16[2,512,4096]{2,1,0:T(8,128)(2,1)} %param.16, f32[2,4096,128]{2,1,0:T(8,128)} %param.13, f32[2,4096,128]{2,1,0:T(8,128)} %all-reduce.13.cloned.1.call-done), kind=kOutput, calls=%fused_computation.28 | convolution fusion | flops 1075838976 | bytes 17301504 | tf_op jit(solution)/shard_map/pij,pjk->pik/dot_general | solution.py:57
  197.2 0.2 all-reduce.17.cloned.1.call-start
  197.4 13.2 %fusion.1 = f32[4096,128]{1,0:T(8,128)S(1)} fusion(bf16[1,4096,2048]{2,1,0:T(8,128)(2,1)} %param.19, bf16[1,4096,2048]{2,1,0:T(8,128)(2,1)} %mul.78, f32[1,2048,128]{2,1,0:T(8,128)S(1)} %copy-done.1), kind=kOutput, calls=%fused_computation.2 | convolution fusion | flops 2156134400 | bytes 36700160 | tf_op jit(solution)/shard_map/dot_general | solution.py:52
  210.7 14.5 %all-reduce.15.cloned.1.call-done = f32[2,512,128]{1,2,0:T(8,128)} async-done(((f32[2,512,128]{1,2,0:T(8,128)}), f32[2,512,128]{1,2,0:T(8,128)}) %all-reduce.15.cloned.1.call-update) | async-done | bytes 524304 | tf_op jit(solution)/shard_map/psum | solution.py:19
  225.1 7.1 fusion.17
  232.3 0.0 all-reduce.19.cloned.1.call-start
  232.3 98.0 %all-reduce.17.cloned.1.call-done = f32[4096,128]{1,0:T(8,128)} async-done(((f32[4096,128]{1,0:T(8,128)}), f32[4096,128]{1,0:T(8,128)}) %all-reduce.17.cloned.1.call-update) | async-done | bytes 2097168 | tf_op jit(solution)/shard_map/psum | solution.py:23
  330.3 5.7 convolution_bitcast_fusion.3
  336.0 0.0 all-reduce.21.cloned.1.call-start
  336.0 22.4 %all-reduce.19.cloned.1.call-done = f32[512,128]{0,1:T(8,128)} async-done(((f32[512,128]{0,1:T(8,128)}), f32[512,128]{0,1:T(8,128)}) %all-reduce.19.cloned.1.call-update) | async-done | bytes 262160 | tf_op jit(solution)/shard_map/psum | solution.py:19
  358.5 4.3 convolution_bitcast_fusion.1
  362.8 0.0 all-reduce.23.cloned.1.call-start
  362.9 98.0 %all-reduce.21.cloned.1.call-done = f32[4096,128]{0,1:T(8,128)} async-done(((f32[4096,128]{0,1:T(8,128)}), f32[4096,128]{0,1:T(8,128)}) %all-reduce.21.cloned.1.call-update) | async-done | bytes 2097168 | tf_op jit(solution)/shard_map/psum | solution.py:23
  460.8 6.1 fusion.31
  466.9 0.0 all-reduce.25.cloned.1.call-start
  467.0 27.8 %all-reduce.23.cloned.1.call-done = f32[2,512,128]{1,2,0:T(8,128)} async-done(((f32[2,512,128]{1,2,0:T(8,128)}), f32[2,512,128]{1,2,0:T(8,128)}) %all-reduce.23.cloned.1.call-update) | async-done | bytes 524304 | tf_op jit(solution)/shard_map/psum | solution.py:19
  494.8 6.8 convolution_bitcast_fusion
  501.7 0.3 all-reduce.27.cloned.1.call-start
  502.0 16.5 %copy.25 = bf16[512,8,8,256]{3,1,2,0:T(8,128)(2,1)} copy(bf16[512,8,8,256]{3,2,1,0:T(8,128)(2,1)} %bitcast.78) | data formatting | bytes 33554432
  518.5 14.7 %fusion = f32[2048,128]{1,0:T(8,128)} fusion(bf16[4096,2048]{1,0:T(8,128)(2,1)} %bitcast.79, bf16[1,4096,2048]{2,1,0:T(8,128)(2,1)} %param.19, f32[4096,128]{0,1:T(8,128)S(1)} %copy-done), kind=kOutput, calls=%fused_computation.1 | convolution fusion | flops 2156396544 | bytes 36700160 | tf_op jit(solution)/shard_map/ji,jk->ik/dot_general | solution.py:94
  533.2 79.9 %all-reduce.25.cloned.1.call-done = f32[2,4096,128]{1,2,0:T(8,128)} async-done(((f32[2,4096,128]{1,2,0:T(8,128)}), f32[2,4096,128]{1,2,0:T(8,128)}) %all-reduce.25.cloned.1.call-update) | async-done | bytes 4194320 | tf_op jit(solution)/shard_map/psum | solution.py:23
  613.1 17.5 %fusion.24 = f32[1,2048,128]{2,1,0:T(8,128)} fusion(f32[2048,128]{1,0:T(8,128)} %fusion, bf16[1,4096,2048]{2,1,0:T(8,128)(2,1)} %param.18, bf16[1,4096,2048]{2,1,0:T(8,128)(2,1)} %mul.67, f32[2,4096,128]{1,2,0:T(8,128)} %all-reduce.25.cloned.1.call-done, s32[]{:T(128)S(6)} %select_n.10), kind=kOutput, calls=%fused_computation.23 | convolution fusion | flops 2156134400 | bytes 36700164 | tf_op jit(solution)/shard_map/ji,jk->ik/dot_general | solution.py:93
  630.7 0.3 all-reduce.29.cloned.1.call-start
  631.0 39.1 %all-reduce.27.cloned.1.call-done = f32[1,2048,128]{2,1,0:T(8,128)} async-done(((f32[1,2048,128]{2,1,0:T(8,128)}), f32[1,2048,128]{2,1,0:T(8,128)}) %all-reduce.27.cloned.1.call-update) | async-done | bytes 1048592 | tf_op jit(solution)/shard_map/psum | solution.py:19
  670.1 9.8 %fusion.14 = f32[1,4096,128]{1,2,0:T(8,128)} fusion(bf16[1,2048,4096]{2,1,0:T(8,128)(2,1)} %param.15, f32[1,2048,128]{2,1,0:T(8,128)S(1)} %copy-done.1, f32[1,2048,128]{2,1,0:T(8,128)} %all-reduce.27.cloned.1.call-done), kind=kOutput, calls=%fused_computation.16 | convolution fusion | flops 2148007936 | bytes 20971520 | tf_op jit(solution)/shard_map/ji,jk->ik/dot_general | solution.py:98
  679.9 0.8 copy.23
  680.7 1.8 copy.22
  682.5 5.6 copy.21
  688.2 77.0 %all-reduce.29.cloned.1.call-done = f32[1,4096,128]{1,2,0:T(8,128)} async-done(((f32[1,4096,128]{1,2,0:T(8,128)}), f32[1,4096,128]{1,2,0:T(8,128)}) %all-reduce.29.cloned.1.call-update) | async-done | bytes 2097168 | tf_op jit(solution)/shard_map/psum | solution.py:104
  765.2 2.9 copy.20
  (28 shorter events, 0.2 us)
Async XLA Ops:
  7.2 12.0 %copy-start.4 = (s32[1,16,8]{1,2,0:T(8,128)S(1)}, s32[1,16,8]{1,2,0:T(8,128)}, u32[]{:S(2)}) copy-start(s32[1,16,8]{1,2,0:T(8,128)} %param.21) | copy-start | bytes 1540
  7.2 53.3 %all-reduce.11.cloned.1.call-start = ((), (), s32[]{:S(2)}) async-start(), calls=%async_computation | async-start | bytes 2097152 | tf_op jit(solution)/shard_map/psum | solution.py:19
  19.1 168.5 %all-reduce.13.cloned.1.call-start = ((), (), s32[]{:S(2)}) async-start(), calls=%async_computation.1 | async-start | bytes 8388608 | tf_op jit(solution)/shard_map/psum | solution.py:54
  73.8 2.4 copy-start.5
  76.2 148.9 %all-reduce.15.cloned.1.call-start = ((), (), s32[]{:S(2)}) async-start(), calls=%async_computation.2 | async-start | bytes 1048576 | tf_op jit(solution)/shard_map/psum | solution.py:19
  82.4 25.8 %copy-start.6 = (s32[2,16,2]{1,2,0:T(2,128)S(1)}, s32[2,16,2]{1,2,0:T(2,128)}, u32[]{:S(2)}) copy-start(s32[2,16,2]{1,2,0:T(2,128)} %param.23) | copy-start | bytes 772
  138.8 58.6 %copy-start.1 = (f32[1,2048,128]{2,1,0:T(8,128)S(1)}, f32[1,2048,128]{2,1,0:T(8,128)}, u32[]{:S(2)}) copy-start(f32[1,2048,128]{2,1,0:T(8,128)} %all-reduce.11.cloned.1.call-done) | copy-start | bytes 3145732
  197.2 133.1 %all-reduce.17.cloned.1.call-start = ((), (), s32[]{:S(2)}) async-start(), calls=%async_computation.3 | async-start | bytes 4194304 | tf_op jit(solution)/shard_map/psum | solution.py:23
  232.3 126.2 %all-reduce.19.cloned.1.call-start = ((), (), s32[]{:S(2)}) async-start(), calls=%async_computation.4 | async-start | bytes 524288 | tf_op jit(solution)/shard_map/psum | solution.py:19
  336.0 124.9 %all-reduce.21.cloned.1.call-start = ((), (), s32[]{:S(2)}) async-start(), calls=%async_computation.5 | async-start | bytes 4194304 | tf_op jit(solution)/shard_map/psum | solution.py:23
  362.8 132.0 %copy-start.2 = (f32[2,512,128]{1,2,0:T(8,128)S(1)}, f32[2,512,128]{1,2,0:T(8,128)}, u32[]{:S(2)}) copy-start(f32[2,512,128]{1,2,0:T(8,128)} %all-reduce.15.cloned.1.call-done) | copy-start | bytes 1572868
  362.8 132.0 %all-reduce.23.cloned.1.call-start = ((), (), s32[]{:S(2)}) async-start(), calls=%async_computation.6 | async-start | bytes 1048576 | tf_op jit(solution)/shard_map/psum | solution.py:19
  466.9 146.2 %all-reduce.25.cloned.1.call-start = ((), (), s32[]{:S(2)}) async-start(), calls=%async_computation.7 | async-start | bytes 8388608 | tf_op jit(solution)/shard_map/psum | solution.py:23
  501.7 168.4 %all-reduce.27.cloned.1.call-start = ((), (), s32[]{:S(2)}) async-start(), calls=%async_computation.8 | async-start | bytes 2097152 | tf_op jit(solution)/shard_map/psum | solution.py:19
  502.0 16.5 %copy-start = (f32[4096,128]{0,1:T(8,128)S(1)}, f32[4096,128]{0,1:T(8,128)}, u32[]{:S(2)}) copy-start(f32[4096,128]{0,1:T(8,128)} %all-reduce.21.cloned.1.call-done) | copy-start | bytes 6291460
  630.6 49.2 %copy-start.3 = (f32[512,128]{0,1:T(8,128)S(1)}, f32[512,128]{0,1:T(8,128)}, u32[]{:S(2)}) copy-start(f32[512,128]{0,1:T(8,128)} %all-reduce.19.cloned.1.call-done) | copy-start | bytes 786436
  630.7 134.5 %all-reduce.29.cloned.1.call-start = ((), (), s32[]{:S(2)}) async-start(), calls=%async_computation.9 | async-start | bytes 4194304 | tf_op jit(solution)/shard_map/psum | solution.py:104
Sparse Core Ops, SparseCore 0:
  19.2 41.2 all-reduce.10
  76.3 111.2 all-reduce.12
  197.3 27.8 all-reduce.14
  232.4 97.8 all-reduce.16
  336.1 22.2 all-reduce.18
  362.9 97.8 all-reduce.20
  467.1 27.7 all-reduce.22
  501.8 111.2 all-reduce.24
  630.8 39.2 all-reduce.26
  680.0 85.0 all-reduce.28
where the time goes:
time: 780 us; the launch traced here: 775 us
  waiting for transfers between devices  515 us (66%)
  matrix products  120 us (15%)
  local copies, waits for them, and re-layouts  112 us (14%)
  between operations  14.3 us (2%)
  other arithmetic  12.1 us (2%)
    psum x3, waiting for transfers between devices, branch_total(): return lax.psum(partial_sum, ('col', 'leaf'))  276 us
    psum x5, waiting for transfers between devices, row_total(): return lax.psum(partial_sum, 'row')  113 us
    mul x8, local copies, waits for them, and re-layouts, masked_blocks(): return (tiles * keeper).reshape(leading, row_count, col_count)  84.5 us
    psum x1, waiting for transfers between devices, shards(): solve_leaf = lax.psum(leaf_terms, 'col')[None]  77 us
    psum x1, waiting for transfers between devices, shards(): mid_terms = lax.psum(selector * to_mid[None], ('col', 'leaf'))  48.8 us
    unnamed x19, local copies, waits for them, and re-layouts  27.7 us
    dot_general x1, matrix products, shards(): jnp.einsum('ji,jk->ik', leaf_mid, mid_back, preferred_element_type=jnp.fl...  17.5 us
  transfers between devices with their start and end apart: 10, of which 10 were waited for; matrix products, arithmetic and copies ran while one was open for 19% of the time, Pallas kernels for 0%

commit v1 on v0

v1 whole, which is shorter than its diff:
```python
import jax
import jax.numpy as jnp
from jax import lax
from jax.sharding import PartitionSpec as P


def masked_blocks(matrix, pattern):
    leading, row_count, col_count = matrix.shape
    block_rows = pattern.shape[1]
    block_cols = pattern.shape[2]
    tiles = matrix.reshape(
        leading, block_rows, row_count // block_rows, block_cols, col_count // block_cols
    )
    keeper = pattern.astype(matrix.dtype)[:, :, None, :, None]
    return (tiles * keeper).reshape(leading, row_count, col_count)


def send_xor(value, axis, size, bit):
    return lax.ppermute(value, axis, [(i, i ^ bit) for i in range(size)])


def pick(blocks, index):
    return lax.dynamic_index_in_dim(blocks, index, 0, keepdims=False)


def scatter_sum(value, axis, size, bits):
    me = lax.axis_index(axis)
    count = len(bits) + 1
    unit = bits[0]
    slot = (me // unit) % count
    blocks = value.reshape((count, value.shape[0] // count) + value.shape[1:])
    total = pick(blocks, slot)
    arrived = [
        send_xor(pick(blocks, slot ^ (bit // unit)), axis, size, bit) for bit in bits
    ]
    for block in arrived:
        total = total + block
    return total


def gather_all(value, axis, size, bits):
    me = lax.axis_index(axis)
    count = len(bits) + 1
    unit = bits[0]
    slot = (me // unit) % count
    out = jnp.zeros((count,) + value.shape, value.dtype)
    out = lax.dynamic_update_index_in_dim(out, value, slot, 0)
    for bit in bits:
        block = send_xor(value, axis, size, bit)
        out = lax.dynamic_update_index_in_dim(out, block, slot ^ (bit // unit), 0)
    return out.reshape((count * value.shape[0],) + value.shape[1:])


def make_shards(sizes):
    rows, cols, leaves = sizes["row"], sizes["col"], sizes["leaf"]
    col_bits = list(range(1, cols))

    def row_total(partial_sum):
        if rows == 2:
            return partial_sum + send_xor(partial_sum, "row", rows, 1)
        return lax.psum(partial_sum, "row")

    def col_scatter(value):
        return scatter_sum(value, "col", cols, col_bits)

    def col_gather(value):
        return gather_all(value, "col", cols, col_bits)

    def leaf_scatter(value, bit):
        return scatter_sum(value, "leaf", leaves, [bit])

    def leaf_gather(value, bit):
        return gather_all(value, "leaf", leaves, [bit])

    def dot(a, b):
        return jnp.dot(a, b, preferred_element_type=jnp.float32)

    def dot_t(a, b):
        return jnp.einsum("ji,jk->ik", a, b, preferred_element_type=jnp.float32)

    def half(a):
        return a.astype(jnp.bfloat16)

    def shards(
        rhs_leaf,
        rhs_mid,
        rhs_root,
        inverse_leaf,
        inverse_mid,
        inverse_root,
        factor_leaf_mid,
        factor_leaf_root,
        factor_mid_root,
        pattern_leaf_mid,
        pattern_leaf_root,
        pattern_mid_root,
    ):
        leaf_mid = masked_blocks(factor_leaf_mid, pattern_leaf_mid)[0]
        leaf_root = masked_blocks(factor_leaf_root, pattern_leaf_root)[0]
        mid_root = masked_blocks(factor_mid_root, pattern_mid_root)
        leaf_inverse = inverse_leaf[0]
        leaf = lax.axis_index("leaf")
        owner = leaf // 2

        forward_leaf = row_total(dot(leaf_inverse, half(rhs_leaf[0])))
        leaf_half = half(forward_leaf)
        to_mid = col_scatter(leaf_scatter(dot(leaf_mid, leaf_half), 1))
        to_root = dot(leaf_root, leaf_half)
        to_mid = leaf_gather(leaf_gather(col_gather(to_mid)[None], 2)[None], 1)
        residue_mid = rhs_mid - jnp.swapaxes(to_mid, 0, 1).reshape(rhs_mid.shape)
        forward_mid = row_total(
            jnp.einsum(
                "pij,pjk->pik", inverse_mid, half(residue_mid), preferred_element_type=jnp.float32
            )
        )
        root_partial = to_root + jnp.einsum(
            "pij,pjk->ik", mid_root, half(forward_mid), preferred_element_type=jnp.float32
        )
        to_root = col_scatter(leaf_scatter(leaf_scatter(root_partial, 1), 2))
        residue_root = rhs_root - leaf_gather(leaf_gather(col_gather(to_root), 2), 1)
        forward_root = row_total(dot(inverse_root, half(residue_root)))

        root_terms = dot_t(inverse_root, half(forward_root))
        root_terms = col_scatter(leaf_scatter(leaf_scatter(root_terms, 1), 2))
        solve_root = leaf_gather(leaf_gather(col_gather(root_terms), 2), 1)
        root_back = half(solve_root)
        corrected_mid = forward_mid - row_total(
            jnp.einsum("pji,jk->pik", mid_root, root_back, preferred_element_type=jnp.float32)
        )
        mid_terms = jnp.einsum(
            "pji,pjk->pik", inverse_mid, half(corrected_mid), preferred_element_type=jnp.float32
        )
        mid_rows = mid_terms.shape[1]
        mid_terms = mid_terms.reshape((2, 2, mid_rows // 2, -1)).swapaxes(0, 1)
        mid_terms = leaf_scatter(mid_terms, 1)[0]
        mid_terms = leaf_scatter(mid_terms, 2)[0]
        mid_own = leaf_gather(col_gather(col_scatter(mid_terms)), 1)
        mid_other = send_xor(mid_own, "leaf", leaves, 2)
        solve_mid = jnp.where(
            owner == 0, jnp.stack([mid_own, mid_other]), jnp.stack([mid_other, mid_own])
        )
        back_partial = dot_t(leaf_mid, half(mid_own)) + dot_t(leaf_root, root_back)
        corrected_leaf = forward_leaf - row_total(back_partial)
        leaf_terms = dot_t(leaf_inverse, half(corrected_leaf))
        solve_leaf = col_gather(col_scatter(leaf_terms))[None]
        return (solve_leaf, solve_mid, solve_root, forward_root)

    return shards


def solution(mesh):
    return jax.shard_map(
        make_shards(dict(mesh.shape)),
        mesh=mesh,
        in_specs=(
            P("leaf", "row", None),
            P(None, "row", None),
            P("row", None),
            P("leaf", "col", "row"),
            P(None, ("col", "leaf"), "row"),
            P(("col", "leaf"), "row"),
            P("leaf", "row", "col"),
            P("leaf", "row", "col"),
            P(None, "row", ("col", "leaf")),
            P("leaf", "row", "col"),
            P("leaf", "row", "col"),
            P(None, "row", ("col", "leaf")),
        ),
        out_specs=(
            P("leaf", "row", None),
            P(None, "row", None),
            P("row", None),
            P(("col", "leaf"), None),
        ),
        check_vma=False,
    )
```

time: 780 us -> 713 us (0.914)
  waiting for transfers between devices: 515 us -> 353 us
  local copies, waits for them, and re-layouts: 112 us -> 180 us
  starting transfers between devices: 1.08 us -> 54.3 us
  matrix products: 120 us -> 94.6 us
  between operations: 14.3 us -> 1.84 us
    psum x10 -> x0, waiting for transfers between devices: 515 us -> none  [the longest x3 276 us: branch_total(): return lax.psum(partial_sum, ('col', 'leaf'))]
    ppermute x0 -> x50, waiting for transfers between devices: none -> 353 us  [send_xor(): return lax.ppermute(value, axis, [(i, i ^ bit) for i in range(size)])]
    ppermute x0 -> x50, starting transfers between devices: none -> 54.3 us  [send_xor(): return lax.ppermute(value, axis, [(i, i ^ bit) for i in range(size)])]
    mul x8 -> x9, local copies, waits for them, and re-layouts: 84.5 us -> 106 us  [masked_blocks(): return (tiles * keeper).reshape(leading, row_count, col_count)]
    dot_general x11, matrix products: 114 us -> 93.2 us  [the longest x4 44.9 us: dot_t(): return jnp.einsum('ji,jk->ik', a, b, preferred_element_type=jnp.float32)]
    reshape x0 -> x4, local copies, waits for them, and re-layouts: none -> 11.7 us  [the longest x1 6.58 us: shards(): mid_terms = mid_terms.reshape((2, 2, mid_rows // 2, -1)).swapaxes(0, 1)]
    another operation x0 -> x10, local copies, waits for them, and re-layouts: none -> 11.5 us
    unnamed x19 -> x54, local copies, waits for them, and re-layouts: 27.7 us -> 36 us
  transfers between devices with their start and end apart: 10 -> 50, of which waited for: 10 -> 43; matrix products, arithmetic and copies ran while one was open for 19% -> 24% of each run, Pallas kernels for 0% -> 0%
where the time goes in v1:
time: 713 us; the launch traced here: 701 us
  waiting for transfers between devices  353 us (50%)
  local copies, waits for them, and re-layouts  180 us (25%)
  matrix products  94.6 us (13%)
  starting transfers between devices  54.3 us (8%)
  other arithmetic  18.6 us (3%)
    ppermute x50, waiting for transfers between devices, send_xor(): return lax.ppermute(value, axis, [(i, i ^ bit) for i in range(size)])  353 us
    mul x9, local copies, waits for them, and re-layouts, masked_blocks(): return (tiles * keeper).reshape(leading, row_count, col_count)  106 us
    ppermute x50, starting transfers between devices, send_xor(): return lax.ppermute(value, axis, [(i, i ^ bit) for i in range(size)])  54.3 us
    dot_general x4, matrix products, dot_t(): return jnp.einsum('ji,jk->ik', a, b, preferred_element_type=jnp.float32)  44.9 us
    dot_general x4, matrix products, dot(): return jnp.dot(a, b, preferred_element_type=jnp.float32)  39.8 us
    unnamed x54, local copies, waits for them, and re-layouts  36 us
  transfers between devices with their start and end apart: 50, of which 43 were waited for; matrix products, arithmetic and copies ran while one was open for 24% of the time, Pallas kernels for 0%

profile of v1, /device:TPU:8, one launch (start us, length us, event | category | flops | bytes accessed | tf_op | source)
XLA Modules:
  0.0 701.5 jit_solution(6733779744477763943)
XLA Ops:
  0.6 8.7 %fusion.7 = f32[2048,128]{1,0:T(8,128)S(1)} fusion(bf16[1,2048,4096]{2,1,0:T(8,128)(2,1)} %param.15, f32[1,4096,128]{2,1,0:T(8,128)} %param.12), kind=kOutput, calls=%fused_computation.8 | convolution fusion | flops 2148007936 | bytes 19922944 | tf_op jit(solution)/shard_map/dot_general | solution.py:76
  11.0 6.0 mul.57
  17.1 25.7 %mul.61 = bf16[2,2048,2048]{2,1,0:T(8,128)(2,1)} reshape(bf16[16,256,8,256]{3,2,1,0:T(8,128)(2,1)} %mul.57) | data formatting | bytes 33554432 | tf_op jit(solution)/shard_map/mul | solution.py:15
  42.9 13.1 %fusion.10 = f32[2,2048,128]{2,1,0:T(8,128)S(1)} fusion(bf16[2,2048,2048]{2,1,0:T(8,128)(2,1)} %bitcast.263, bf16[2,2048,2048]{2,1,0:T(8,128)(2,1)} %mul.61, f32[2048,128]{1,0:T(8,128)S(1)} %add.219), kind=kOutput, calls=%fused_computation.11 | convolution fusion | flops 2156134400 | bytes 36700160 | tf_op jit(solution)/shard_map/dot_general | solution.py:76
  65.9 7.8 %collective-permute-done.2 = f32[512,128]{1,0:T(8,128)S(1)} collective-permute-done((f32[512,128]{1,0:T(8,128)S(1)}, f32[512,128]{1,0:T(8,128)S(1)}, u32[]{:S(2)}, u32[]{:S(2)}) %collective-permute-start.2) | collective-permute-done | bytes 262176 | tf_op jit(solution)/shard_map/ppermute | solution.py:19
  73.7 9.6 %collective-permute-done.3 = f32[512,128]{1,0:T(8,128)S(1)} collective-permute-done((f32[512,128]{1,0:T(8,128)S(1)}, f32[512,128]{1,0:T(8,128)S(1)}, u32[]{:S(2)}, u32[]{:S(2)}) %collective-permute-start.3) | collective-permute-done | bytes 262176 | tf_op jit(solution)/shard_map/ppermute | solution.py:19
  83.4 5.4 collective-permute-done.4
  93.5 6.0 collective-permute-done.5
  99.5 11.5 %collective-permute-done.6 = f32[512,128]{1,0:T(8,128)S(1)} collective-permute-done((f32[512,128]{1,0:T(8,128)S(1)}, f32[512,128]{1,0:T(8,128)S(1)}, u32[]{:S(2)}, u32[]{:S(2)}) %collective-permute-start.6) | collective-permute-done | bytes 262176 | tf_op jit(solution)/shard_map/ppermute | solution.py:19
  111.0 4.3 collective-permute-done.7
  117.1 21.2 %collective-permute-done.8 = f32[1,2048,128]{2,1,0:T(8,128)S(1)} collective-permute-done((f32[1,2048,128]{2,1,0:T(8,128)S(1)}, f32[1,2048,128]{2,1,0:T(8,128)S(1)}, u32[]{:S(2)}, u32[]{:S(2)}) %collective-permute-start.8) | collective-permute-done | bytes 1048608 | tf_op jit(solution)/shard_map/ppermute | solution.py:19
  148.6 6.6 mul.63
  155.2 14.0 %mul.64 = bf16[2,4096,512]{2,1,0:T(8,128)(2,1)} reshape(bf16[2,16,256,2,256]{4,3,2,1,0:T(2,128)(2,1)} %mul.63) | data formatting | bytes 16777216 | tf_op jit(solution)/shard_map/mul | solution.py:15
  171.1 6.4 copy-done
  177.4 9.7 %copy.63 = bf16[512,8,8,256]{3,1,2,0:T(8,128)(2,1)} copy(bf16[512,8,8,256]{3,2,1,0:T(8,128)(2,1)S(1)} %bitcast.259) | data formatting | bytes 33554432
  193.7 16.5 %fusion.16 = f32[4096,128]{1,0:T(8,128)} fusion(f32[4096,128]{1,0:T(8,128)S(1)} %convolution_bitcast_fusion.2, bf16[4096,2048]{1,0:T(8,128)(2,1)} %bitcast.262, bf16[1,4096,2048]{2,1,0:T(8,128)(2,1)} %param.19, f32[2048,128]{1,0:T(8,128)S(1)} %add.219), kind=kOutput, calls=%fused_computation.18 | convolution fusion | flops 2156658688 | bytes 38797312 | tf_op jit(solution)/shard_map/dot_general | solution.py:76
  216.0 12.5 %collective-permute-done.12 = f32[1024,128]{1,0:T(8,128)S(1)} collective-permute-done((f32[1024,128]{1,0:T(8,128)S(1)}, f32[1024,128]{1,0:T(8,128)S(1)}, u32[]{:S(2)}, u32[]{:S(2)}) %collective-permute-start.12) | collective-permute-done | bytes 524320 | tf_op jit(solution)/shard_map/ppermute | solution.py:19
  235.1 5.1 collective-permute-done.14
  249.6 4.7 collective-permute-done.17
  258.9 10.5 %collective-permute-done.19 = f32[1024,128]{1,0:T(8,128)S(1)} collective-permute-done((f32[1024,128]{1,0:T(8,128)S(1)}, f32[1024,128]{1,0:T(8,128)S(1)}, u32[]{:S(2)}, u32[]{:S(2)}) %collective-permute-start.19) | collective-permute-done | bytes 524320 | tf_op jit(solution)/shard_map/ppermute | solution.py:19
  277.6 6.8 collective-permute-done.21
  293.1 12.5 %collective-permute-done.23 = f32[1024,128]{1,0:T(8,128)S(1)} collective-permute-done((f32[1024,128]{1,0:T(8,128)S(1)}, f32[1024,128]{1,0:T(8,128)S(1)}, u32[]{:S(2)}, u32[]{:S(2)}) %collective-permute-start.23) | collective-permute-done | bytes 524320 | tf_op jit(solution)/shard_map/ppermute | solution.py:19
  311.7 6.4 collective-permute-done.25
  327.0 5.1 collective-permute-done.28
  336.6 10.6 %collective-permute-done.30 = f32[1024,128]{1,0:T(8,128)S(1)} collective-permute-done((f32[1024,128]{1,0:T(8,128)S(1)}, f32[1024,128]{1,0:T(8,128)S(1)}, u32[]{:S(2)}, u32[]{:S(2)}) %collective-permute-start.30) | collective-permute-done | bytes 524320 | tf_op jit(solution)/shard_map/ppermute | solution.py:19
  353.1 12.5 %collective-permute-done.32 = f32[2,512,128]{1,2,0:T(8,128)S(1)} collective-permute-done((f32[2,512,128]{1,2,0:T(8,128)S(1)}, f32[2,512,128]{1,2,0:T(8,128)S(1)}, u32[]{:S(2)}, u32[]{:S(2)}) %collective-permute-start.32) | collective-permute-done | bytes 524320 | tf_op jit(solution)/shard_map/ppermute | solution.py:19
  368.9 6.6 reshape.146
  375.5 9.8 %constant_dynamic-slice_fusion.1 = (f32[2,1,2048,128]{2,1,3,0:T(1,128)}, f32[2,1,2048,128]{2,1,3,0:T(1,128)}) fusion(f32[2,2,2048,128]{2,1,3,0:T(2,128)} %reshape.146, s32[]{:T(128)S(6)} %select_n.192, s32[]{:T(128)S(6)} %select_n.193), kind=kLoop, calls=%fused_computation.114 | loop fusion | bytes 8388616 | tf_op jit(solution)/shard_map/dynamic-slice.4
  385.3 6.0 copy.62
  391.3 6.0 copy.61
  401.4 24.1 %collective-permute-done.34 = f32[1,2048,128]{2,1,0:T(8,128)S(1)} collective-permute-done((f32[1,2048,128]{2,1,0:T(8,128)S(1)}, f32[1,2048,128]{2,1,0:T(8,128)S(1)}, u32[]{:S(2)}, u32[]{:S(2)}) %collective-permute-start.34) | collective-permute-done | bytes 1048608 | tf_op jit(solution)/shard_map/ppermute | solution.py:19
  429.5 7.1 %collective-permute-done.35 = f32[512,128]{1,0:T(8,128)S(1)} collective-permute-done((f32[512,128]{1,0:T(8,128)S(1)}, f32[512,128]{1,0:T(8,128)S(1)}, u32[]{:S(2)}, u32[]{:S(2)}) %collective-permute-start.35) | collective-permute-done | bytes 262176 | tf_op jit(solution)/shard_map/ppermute | solution.py:19
  436.7 10.9 %collective-permute-done.36 = f32[512,128]{1,0:T(8,128)S(1)} collective-permute-done((f32[512,128]{1,0:T(8,128)S(1)}, f32[512,128]{1,0:T(8,128)S(1)}, u32[]{:S(2)}, u32[]{:S(2)}) %collective-permute-start.36) | collective-permute-done | bytes 262176 | tf_op jit(solution)/shard_map/ppermute | solution.py:19
  447.5 4.3 collective-permute-done.37
  457.4 25.6 %mul.70 = bf16[1,4096,2048]{2,1,0:T(8,128)(2,1)} reshape(bf16[16,256,8,256]{3,2,1,0:T(8,128)(2,1)} %copy-done) | data formatting | bytes 33554432 | tf_op jit(solution)/shard_map/mul | solution.py:15
  483.0 25.8 %mul.58 = bf16[1,4096,2048]{2,1,0:T(8,128)(2,1)} reshape(bf16[16,256,8,256]{3,2,1,0:T(8,128)(2,1)} %mul.57) | data formatting | bytes 33554432 | tf_op jit(solution)/shard_map/mul | solution.py:15
  513.3 8.7 %collective-permute-done.40 = f32[512,128]{1,0:T(8,128)S(1)} collective-permute-done((f32[512,128]{1,0:T(8,128)}, f32[512,128]{1,0:T(8,128)S(1)}, u32[]{:S(2)}, u32[]{:S(2)}) %collective-permute-start.40) | collective-permute-done | bytes 262176 | tf_op jit(solution)/shard_map/ppermute | solution.py:19
  522.7 16.8 %fusion = f32[2048,128]{1,0:T(8,128)} fusion(bf16[4096,128]{1,0:T(8,128)(2,1)} %bitcast.307, bf16[1,4096,2048]{2,1,0:T(8,128)(2,1)} %param.19, bf16[1,4096,2048]{2,1,0:T(8,128)(2,1)} %mul.70), kind=kOutput, calls=%fused_computation | convolution fusion | flops 2155872256 | bytes 35651584 | tf_op jit(solution)/shard_map/ji,jk->ik/dot_general | solution.py:79
  543.4 17.2 %fusion.18 = f32[2048,128]{1,0:T(8,128)} fusion(f32[2048,128]{1,0:T(8,128)} %fusion, bf16[4096,128]{1,0:T(8,128)(2,1)} %bitcast.282, bf16[1,4096,2048]{2,1,0:T(8,128)(2,1)} %param.18, bf16[1,4096,2048]{2,1,0:T(8,128)(2,1)} %mul.58), kind=kOutput, calls=%fused_computation.22 | convolution fusion | flops 2156134400 | bytes 36700160 | tf_op jit(solution)/shard_map/ji,jk->ik/dot_general | solution.py:79
  563.6 22.8 %collective-permute-done.42 = f32[2048,128]{1,0:T(8,128)S(1)} collective-permute-done((f32[2048,128]{1,0:T(8,128)}, f32[2048,128]{1,0:T(8,128)S(1)}, u32[]{:S(2)}, u32[]{:S(2)}) %collective-permute-start.42) | collective-permute-done | bytes 1048608 | tf_op jit(solution)/shard_map/ppermute | solution.py:19
  586.4 10.2 %fusion.13 = f32[4096,128]{0,1:T(8,128)} fusion(bf16[1,2048,4096]{2,1,0:T(8,128)(2,1)} %param.15, f32[2048,128]{1,0:T(8,128)S(1)} %add.219, f32[2048,128]{1,0:T(8,128)} %fusion.18, f32[2048,128]{1,0:T(8,128)S(1)} %collective-permute-done.42), kind=kOutput, calls=%fused_computation.15 | convolution fusion | flops 2148270080 | bytes 22020096 | tf_op jit(solution)/shard_map/ji,jk->ik/dot_general | solution.py:79
  606.0 17.4 %collective-permute-done.43 = f32[1024,128]{1,0:T(8,128)} collective-permute-done((f32[1024,128]{1,0:T(8,128)}, f32[1024,128]{1,0:T(8,128)}, u32[]{:S(2)}, u32[]{:S(2)}) %collective-permute-start.43) | collective-permute-done | bytes 524320 | tf_op jit(solution)/shard_map/ppermute | solution.py:19
  623.4 14.9 %collective-permute-done.44 = f32[1024,128]{1,0:T(8,128)} collective-permute-done((f32[1024,128]{1,0:T(8,128)S(1)}, f32[1024,128]{1,0:T(8,128)}, u32[]{:S(2)}, u32[]{:S(2)}) %collective-permute-start.44) | collective-permute-done | bytes 524320 | tf_op jit(solution)/shard_map/ppermute | solution.py:19
  638.3 12.1 %collective-permute-done.45 = f32[1024,128]{1,0:T(8,128)} collective-permute-done((f32[1024,128]{1,0:T(8,128)S(1)}, f32[1024,128]{1,0:T(8,128)}, u32[]{:S(2)}, u32[]{:S(2)}) %collective-permute-start.45) | collective-permute-done | bytes 524320 | tf_op jit(solution)/shard_map/ppermute | solution.py:19
  655.7 4.6 maximum_select_fusion
  660.3 11.5 %collective-permute-done.46 = f32[1024,128]{1,0:T(8,128)S(1)} collective-permute-done((f32[1024,128]{1,0:T(8,128)S(1)}, f32[1024,128]{1,0:T(8,128)S(1)}, u32[]{:S(2)}, u32[]{:S(2)}) %collective-permute-start.46) | collective-permute-done | bytes 524320 | tf_op jit(solution)/shard_map/ppermute | solution.py:19
  671.8 17.0 %collective-permute-done.47 = f32[1024,128]{1,0:T(8,128)S(1)} collective-permute-done((f32[1024,128]{1,0:T(8,128)S(1)}, f32[1024,128]{1,0:T(8,128)S(1)}, u32[]{:S(2)}, u32[]{:S(2)}) %collective-permute-start.47) | collective-permute-done | bytes 524320 | tf_op jit(solution)/shard_map/ppermute | solution.py:19
  688.9 10.8 %collective-permute-done.48 = f32[1024,128]{1,0:T(8,128)S(1)} collective-permute-done((f32[1024,128]{1,0:T(8,128)S(1)}, f32[1024,128]{1,0:T(8,128)S(1)}, u32[]{:S(2)}, u32[]{:S(2)}) %collective-permute-start.48) | collective-permute-done | bytes 524320 | tf_op jit(solution)/shard_map/ppermute | solution.py:19
  (213 shorter events, 150.2 us)
Async XLA Ops:
  9.4 33.4 %collective-permute-start = (f32[2048,128]{1,0:T(8,128)S(1)}, f32[2048,128]{1,0:T(8,128)S(1)}, u32[]{:S(2)}, u32[]{:S(2)}) collective-permute-start(f32[2048,128]{1,0:T(8,128)S(1)} %fusion.7), channel_id=1, source_target_pairs={{0,16},{16,0},{1,17},{17,1},{2,18},{18,2},{3,19},{19,3},{4,20},{20... | collective-permute-start | bytes 3145736 | tf_op jit(solution)/shard_map/ppermute | solution.py:19
  57.0 3.0 collective-permute-start.1
  62.3 11.4 %collective-permute-start.2 = (f32[512,128]{1,0:T(8,128)S(1)}, f32[512,128]{1,0:T(8,128)S(1)}, u32[]{:S(2)}, u32[]{:S(2)}) collective-permute-start(f32[512,128]{1,0:T(8,128)S(1)} %get-tuple-element.34), channel_id=1, source_target_pairs={{0,4},{4,0},{8,12},{12,8},{1,5},{5,1},{9,13},{13,9},{2,6},{6,2},{1... | collective-permute-start | bytes 786440 | tf_op jit(solution)/shard_map/ppermute | solution.py:19
  62.8 20.5 %collective-permute-start.3 = (f32[512,128]{1,0:T(8,128)S(1)}, f32[512,128]{1,0:T(8,128)S(1)}, u32[]{:S(2)}, u32[]{:S(2)}) collective-permute-start(f32[512,128]{1,0:T(8,128)S(1)} %get-tuple-element.36), channel_id=1, source_target_pairs={{0,8},{4,12},{8,0},{12,4},{1,9},{5,13},{9,1},{13,5},{2,10},{6,14},... | collective-permute-start | bytes 786440 | tf_op jit(solution)/shard_map/ppermute | solution.py:19
  65.4 23.4 %collective-permute-start.4 = (f32[512,128]{1,0:T(8,128)S(1)}, f32[512,128]{1,0:T(8,128)S(1)}, u32[]{:S(2)}, u32[]{:S(2)}) collective-permute-start(f32[512,128]{1,0:T(8,128)S(1)} %get-tuple-element.35), channel_id=1, source_target_pairs={{0,12},{4,8},{8,4},{12,0},{1,13},{5,9},{9,5},{13,1},{2,14},{6,10},... | collective-permute-start | bytes 786440 | tf_op jit(solution)/shard_map/ppermute | solution.py:19
  89.9 9.6 %collective-permute-start.5 = (f32[512,128]{1,0:T(8,128)S(1)}, f32[512,128]{1,0:T(8,128)S(1)}, u32[]{:S(2)}, u32[]{:S(2)}) collective-permute-start(f32[512,128]{1,0:T(8,128)S(1)} %get-tuple-element.25), channel_id=1, source_target_pairs={{0,4},{4,0},{8,12},{12,8},{1,5},{5,1},{9,13},{13,9},{2,6},{6,2},{1... | collective-permute-start | bytes 786440 | tf_op jit(solution)/shard_map/ppermute | solution.py:19
  90.0 21.0 %collective-permute-start.6 = (f32[512,128]{1,0:T(8,128)S(1)}, f32[512,128]{1,0:T(8,128)S(1)}, u32[]{:S(2)}, u32[]{:S(2)}) collective-permute-start(f32[512,128]{1,0:T(8,128)S(1)} %get-tuple-element.25), channel_id=1, source_target_pairs={{0,8},{4,12},{8,0},{12,4},{1,9},{5,13},{9,1},{13,5},{2,10},{6,14},... | collective-permute-start | bytes 786440 | tf_op jit(solution)/shard_map/ppermute | solution.py:19
  93.0 22.3 %collective-permute-start.7 = (f32[512,128]{1,0:T(8,128)S(1)}, f32[512,128]{1,0:T(8,128)S(1)}, u32[]{:S(2)}, u32[]{:S(2)}) collective-permute-start(f32[512,128]{1,0:T(8,128)S(1)} %get-tuple-element.25), channel_id=1, source_target_pairs={{0,12},{4,8},{8,4},{12,0},{1,13},{5,9},{9,5},{13,1},{2,14},{6,10},... | collective-permute-start | bytes 786440 | tf_op jit(solution)/shard_map/ppermute | solution.py:19
  115.3 23.0 %collective-permute-start.8 = (f32[1,2048,128]{2,1,0:T(8,128)S(1)}, f32[1,2048,128]{2,1,0:T(8,128)S(1)}, u32[]{:S(2)}, u32[]{:S(2)}) collective-permute-start(f32[1,2048,128]{2,1,0:T(8,128)S(1)} %bitcast.283), channel_id=1, source_target_pairs={{0,2},{1,3},{2,0},{3,1},{4,6},{5,7},{6,4},{7,5},{8,10},{9,11},{10,... | collective-permute-start | bytes 3145736 | tf_op jit(solution)/shard_map/ppermute | solution.py:19
  138.4 4.2 collective-permute-start.9
  147.9 42.2 %collective-permute-start.10 = (f32[2,512,128]{1,2,0:T(8,128)S(1)}, f32[2,512,128]{1,2,0:T(8,128)S(1)}, u32[]{:S(2)}, u32[]{:S(2)}) collective-permute-start(f32[2,512,128]{1,2,0:T(8,128)S(1)} %convolution_bitcast_fusion.3), channel_id=1, source_target_pairs={{0,16},{16,0},{1,17},{17,1},{2,18},{18,2},{3,19},{19,3},{4,20},{20... | collective-permute-start | bytes 1572872 | tf_op jit(solution)/shard_map/ppermute | solution.py:19
  211.6 2.7 collective-permute-start.11
  214.5 14.0 %collective-permute-start.12 = (f32[1024,128]{1,0:T(8,128)S(1)}, f32[1024,128]{1,0:T(8,128)S(1)}, u32[]{:S(2)}, u32[]{:S(2)}) collective-permute-start(f32[1024,128]{1,0:T(8,128)S(1)} %dynamic-slice_bitcast_fusion.8), channel_id=1, source_target_pairs={{0,2},{1,3},{2,0},{3,1},{4,6},{5,7},{6,4},{7,5},{8,10},{9,11},{10,... | collective-permute-start | bytes 1572872 | tf_op jit(solution)/shard_map/ppermute | solution.py:19
  228.6 6.5 collective-permute-start.13
  228.7 11.5 %collective-permute-start.14 = (f32[256,128]{1,0:T(8,128)S(1)}, f32[256,128]{1,0:T(8,128)S(1)}, u32[]{:S(2)}, u32[]{:S(2)}) collective-permute-start(f32[256,128]{1,0:T(8,128)S(1)} %get-tuple-element.42), channel_id=1, source_target_pairs={{0,8},{4,12},{8,0},{12,4},{1,9},{5,13},{9,1},{13,5},{2,10},{6,14},... | collective-permute-start | bytes 393224 | tf_op jit(solution)/shard_map/ppermute | solution.py:19
  231.7 11.3 %collective-permute-start.15 = (f32[256,128]{1,0:T(8,128)S(1)}, f32[256,128]{1,0:T(8,128)S(1)}, u32[]{:S(2)}, u32[]{:S(2)}) collective-permute-start(f32[256,128]{1,0:T(8,128)S(1)} %get-tuple-element.41), channel_id=1, source_target_pairs={{0,12},{4,8},{8,4},{12,0},{1,13},{5,9},{9,5},{13,1},{2,14},{6,10},... | collective-permute-start | bytes 393224 | tf_op jit(solution)/shard_map/ppermute | solution.py:19
  243.2 6.4 collective-permute-start.16
  243.3 11.0 %collective-permute-start.17 = (f32[256,128]{1,0:T(8,128)S(1)}, f32[256,128]{1,0:T(8,128)S(1)}, u32[]{:S(2)}, u32[]{:S(2)}) collective-permute-start(f32[256,128]{1,0:T(8,128)S(1)} %get-tuple-element.23), channel_id=1, source_target_pairs={{0,8},{4,12},{8,0},{12,4},{1,9},{5,13},{9,1},{13,5},{2,10},{6,14},... | collective-permute-start | bytes 393224 | tf_op jit(solution)/shard_map/ppermute | solution.py:19
  246.2 11.0 %collective-permute-start.18 = (f32[256,128]{1,0:T(8,128)S(1)}, f32[256,128]{1,0:T(8,128)S(1)}, u32[]{:S(2)}, u32[]{:S(2)}) collective-permute-start(f32[256,128]{1,0:T(8,128)S(1)} %get-tuple-element.23), channel_id=1, source_target_pairs={{0,12},{4,8},{8,4},{12,0},{1,13},{5,9},{9,5},{13,1},{2,14},{6,10},... | collective-permute-start | bytes 393224 | tf_op jit(solution)/shard_map/ppermute | solution.py:19
  257.2 12.2 %collective-permute-start.19 = (f32[1024,128]{1,0:T(8,128)S(1)}, f32[1024,128]{1,0:T(8,128)S(1)}, u32[]{:S(2)}, u32[]{:S(2)}) collective-permute-start(f32[1024,128]{1,0:T(8,128)S(1)} %bitcast.303), channel_id=1, source_target_pairs={{0,2},{1,3},{2,0},{3,1},{4,6},{5,7},{6,4},{7,5},{8,10},{9,11},{10,... | collective-permute-start | bytes 1572872 | tf_op jit(solution)/shard_map/ppermute | solution.py:19
  269.5 2.7 collective-permute-start.20
  276.0 8.4 %collective-permute-start.21 = (f32[512,128]{0,1:T(8,128)S(1)}, f32[512,128]{0,1:T(8,128)S(1)}, u32[]{:S(2)}, u32[]{:S(2)}) collective-permute-start(f32[512,128]{0,1:T(8,128)S(1)} %convolution_bitcast_fusion.4), channel_id=1, source_target_pairs={{0,16},{16,0},{1,17},{17,1},{2,18},{18,2},{3,19},{19,3},{4,20},{20... | collective-permute-start | bytes 786440 | tf_op jit(solution)/shard_map/ppermute | solution.py:19
  291.5 14.0 %collective-permute-start.23 = (f32[1024,128]{1,0:T(8,128)S(1)}, f32[1024,128]{1,0:T(8,128)S(1)}, u32[]{:S(2)}, u32[]{:S(2)}) collective-permute-start(f32[1024,128]{1,0:T(8,128)S(1)} %dynamic-slice_bitcast_fusion.7), channel_id=1, source_target_pairs={{0,2},{1,3},{2,0},{3,1},{4,6},{5,7},{6,4},{7,5},{8,10},{9,11},{10,... | collective-permute-start | bytes 1572872 | tf_op jit(solution)/shard_map/ppermute | solution.py:19
  305.6 6.1 collective-permute-start.24
  305.7 12.4 %collective-permute-start.25 = (f32[256,128]{1,0:T(8,128)S(1)}, f32[256,128]{1,0:T(8,128)S(1)}, u32[]{:S(2)}, u32[]{:S(2)}) collective-permute-start(f32[256,128]{1,0:T(8,128)S(1)} %get-tuple-element.39), channel_id=1, source_target_pairs={{0,8},{4,12},{8,0},{12,4},{1,9},{5,13},{9,1},{13,5},{2,10},{6,14},... | collective-permute-start | bytes 393224 | tf_op jit(solution)/shard_map/ppermute | solution.py:19
  309.7 10.9 %collective-permute-start.26 = (f32[256,128]{1,0:T(8,128)S(1)}, f32[256,128]{1,0:T(8,128)S(1)}, u32[]{:S(2)}, u32[]{:S(2)}) collective-permute-start(f32[256,128]{1,0:T(8,128)S(1)} %get-tuple-element.38), channel_id=1, source_target_pairs={{0,12},{4,8},{8,4},{12,0},{1,13},{5,9},{9,5},{13,1},{2,14},{6,10},... | collective-permute-start | bytes 393224 | tf_op jit(solution)/shard_map/ppermute | solution.py:19
  320.7 6.4 collective-permute-start.27
  320.7 11.4 %collective-permute-start.28 = (f32[256,128]{1,0:T(8,128)S(1)}, f32[256,128]{1,0:T(8,128)S(1)}, u32[]{:S(2)}, u32[]{:S(2)}) collective-permute-start(f32[256,128]{1,0:T(8,128)S(1)} %get-tuple-element.21), channel_id=1, source_target_pairs={{0,8},{4,12},{8,0},{12,4},{1,9},{5,13},{9,1},{13,5},{2,10},{6,14},... | collective-permute-start | bytes 393224 | tf_op jit(solution)/shard_map/ppermute | solution.py:19
  324.0 10.9 %collective-permute-start.29 = (f32[256,128]{1,0:T(8,128)S(1)}, f32[256,128]{1,0:T(8,128)S(1)}, u32[]{:S(2)}, u32[]{:S(2)}) collective-permute-start(f32[256,128]{1,0:T(8,128)S(1)} %get-tuple-element.21), channel_id=1, source_target_pairs={{0,12},{4,8},{8,4},{12,0},{1,13},{5,9},{9,5},{13,1},{2,14},{6,10},... | collective-permute-start | bytes 393224 | tf_op jit(solution)/shard_map/ppermute | solution.py:19
  334.9 12.2 %collective-permute-start.30 = (f32[1024,128]{1,0:T(8,128)S(1)}, f32[1024,128]{1,0:T(8,128)S(1)}, u32[]{:S(2)}, u32[]{:S(2)}) collective-permute-start(f32[1024,128]{1,0:T(8,128)S(1)} %bitcast.305), channel_id=1, source_target_pairs={{0,2},{1,3},{2,0},{3,1},{4,6},{5,7},{6,4},{7,5},{8,10},{9,11},{10,... | collective-permute-start | bytes 1572872 | tf_op jit(solution)/shard_map/ppermute | solution.py:19
  351.5 14.0 %collective-permute-start.32 = (f32[2,512,128]{1,2,0:T(8,128)S(1)}, f32[2,512,128]{1,2,0:T(8,128)S(1)}, u32[]{:S(2)}, u32[]{:S(2)}) collective-permute-start(f32[2,512,128]{1,2,0:T(8,128)S(1)} %fusion.22), channel_id=1, source_target_pairs={{0,16},{16,0},{1,17},{17,1},{2,18},{18,2},{3,19},{19,3},{4,20},{20... | collective-permute-start | bytes 1572872 | tf_op jit(solution)/shard_map/ppermute | solution.py:19
  391.3 6.1 collective-permute-start.33
  399.9 25.6 %collective-permute-start.34 = (f32[1,2048,128]{2,1,0:T(8,128)S(1)}, f32[1,2048,128]{2,1,0:T(8,128)S(1)}, u32[]{:S(2)}, u32[]{:S(2)}) collective-permute-start(f32[1,2048,128]{2,1,0:T(8,128)S(1)} %dynamic-slice_bitcast_fusion), channel_id=1, source_target_pairs={{0,2},{1,3},{2,0},{3,1},{4,6},{5,7},{6,4},{7,5},{8,10},{9,11},{10,... | collective-permute-start | bytes 3145736 | tf_op jit(solution)/shard_map/ppermute | solution.py:19
  425.7 10.9 %collective-permute-start.35 = (f32[512,128]{1,0:T(8,128)S(1)}, f32[512,128]{1,0:T(8,128)S(1)}, u32[]{:S(2)}, u32[]{:S(2)}) collective-permute-start(f32[512,128]{1,0:T(8,128)S(1)} %get-tuple-element.31), channel_id=1, source_target_pairs={{0,4},{4,0},{8,12},{12,8},{1,5},{5,1},{9,13},{13,9},{2,6},{6,2},{1... | collective-permute-start | bytes 786440 | tf_op jit(solution)/shard_map/ppermute | solution.py:19
  425.8 21.7 %collective-permute-start.36 = (f32[512,128]{1,0:T(8,128)S(1)}, f32[512,128]{1,0:T(8,128)S(1)}, u32[]{:S(2)}, u32[]{:S(2)}) collective-permute-start(f32[512,128]{1,0:T(8,128)S(1)} %get-tuple-element.33), channel_id=1, source_target_pairs={{0,8},{4,12},{8,0},{12,4},{1,9},{5,13},{9,1},{13,5},{2,10},{6,14},... | collective-permute-start | bytes 786440 | tf_op jit(solution)/shard_map/ppermute | solution.py:19
  429.5 22.3 %collective-permute-start.37 = (f32[512,128]{1,0:T(8,128)S(1)}, f32[512,128]{1,0:T(8,128)S(1)}, u32[]{:S(2)}, u32[]{:S(2)}) collective-permute-start(f32[512,128]{1,0:T(8,128)S(1)} %get-tuple-element.32), channel_id=1, source_target_pairs={{0,12},{4,8},{8,4},{12,0},{1,13},{5,9},{9,5},{13,1},{2,14},{6,10},... | collective-permute-start | bytes 786440 | tf_op jit(solution)/shard_map/ppermute | solution.py:19
  453.7 56.3 %collective-permute-start.38 = (f32[512,128]{1,0:T(8,128)}, f32[512,128]{1,0:T(8,128)}, u32[]{:S(2)}, u32[]{:S(2)}) collective-permute-start(f32[512,128]{1,0:T(8,128)} %get-tuple-element.19), channel_id=1, source_target_pairs={{0,4},{4,0},{8,12},{12,8},{1,5},{5,1},{9,13},{13,9},{2,6},{6,2},{1... | collective-permute-start | bytes 786440 | tf_op jit(solution)/shard_map/ppermute | solution.py:19
  453.7 57.9 %collective-permute-start.39 = (f32[512,128]{1,0:T(8,128)}, f32[512,128]{1,0:T(8,128)}, u32[]{:S(2)}, u32[]{:S(2)}) collective-permute-start(f32[512,128]{1,0:T(8,128)} %get-tuple-element.19), channel_id=1, source_target_pairs={{0,8},{4,12},{8,0},{12,4},{1,9},{5,13},{9,1},{13,5},{2,10},{6,14},... | collective-permute-start | bytes 786440 | tf_op jit(solution)/shard_map/ppermute | solution.py:19
  510.0 12.0 %collective-permute-start.40 = (f32[512,128]{1,0:T(8,128)}, f32[512,128]{1,0:T(8,128)S(1)}, u32[]{:S(2)}, u32[]{:S(2)}) collective-permute-start(f32[512,128]{1,0:T(8,128)} %get-tuple-element.19), channel_id=1, source_target_pairs={{0,12},{4,8},{8,4},{12,0},{1,13},{5,9},{9,5},{13,1},{2,14},{6,10},... | collective-permute-start | bytes 786440 | tf_op jit(solution)/shard_map/ppermute | solution.py:19
  522.7 18.3 %collective-permute-start.41 = (f32[2048,128]{1,0:T(8,128)}, f32[2048,128]{1,0:T(8,128)}, u32[]{:S(2)}, u32[]{:S(2)}) collective-permute-start(f32[2048,128]{1,0:T(8,128)} %bitcast.87), channel_id=1, source_target_pairs={{0,1},{1,0},{2,3},{3,2},{4,5},{5,4},{6,7},{7,6},{8,9},{9,8},{10,11... | collective-permute-start | bytes 3145736 | tf_op jit(solution)/shard_map/ppermute | solution.py:19
  560.6 25.8 %collective-permute-start.42 = (f32[2048,128]{1,0:T(8,128)}, f32[2048,128]{1,0:T(8,128)S(1)}, u32[]{:S(2)}, u32[]{:S(2)}) collective-permute-start(f32[2048,128]{1,0:T(8,128)} %fusion.18), channel_id=1, source_target_pairs={{0,16},{16,0},{1,17},{17,1},{2,18},{18,2},{3,19},{19,3},{4,20},{20... | collective-permute-start | bytes 3145736 | tf_op jit(solution)/shard_map/ppermute | solution.py:19
  562.1 93.6 %collective-permute-start.49 = (f32[4096,128]{1,0:T(8,128)S(1)}, f32[4096,128]{1,0:T(8,128)}, u32[]{:S(2)}, u32[]{:S(2)}) collective-permute-start(f32[4096,128]{1,0:T(8,128)S(1)} %bitcast.270), channel_id=1, source_target_pairs={{0,2},{1,3},{2,0},{3,1},{4,6},{5,7},{6,4},{7,5},{8,10},{9,11},{10,... | collective-permute-start | bytes 6291464 | tf_op jit(solution)/shard_map/ppermute | solution.py:19
  601.7 21.7 %collective-permute-start.43 = (f32[1024,128]{1,0:T(8,128)}, f32[1024,128]{1,0:T(8,128)}, u32[]{:S(2)}, u32[]{:S(2)}) collective-permute-start(f32[1024,128]{1,0:T(8,128)} %get-tuple-element.28), channel_id=1, source_target_pairs={{0,4},{4,0},{8,12},{12,8},{1,5},{5,1},{9,13},{13,9},{2,6},{6,2},{1... | collective-permute-start | bytes 1572872 | tf_op jit(solution)/shard_map/ppermute | solution.py:19
  601.7 36.6 %collective-permute-start.44 = (f32[1024,128]{1,0:T(8,128)S(1)}, f32[1024,128]{1,0:T(8,128)}, u32[]{:S(2)}, u32[]{:S(2)}) collective-permute-start(f32[1024,128]{1,0:T(8,128)S(1)} %get-tuple-element.30), channel_id=1, source_target_pairs={{0,8},{4,12},{8,0},{12,4},{1,9},{5,13},{9,1},{13,5},{2,10},{6,14},... | collective-permute-start | bytes 1572872 | tf_op jit(solution)/shard_map/ppermute | solution.py:19
  603.4 47.0 %collective-permute-start.45 = (f32[1024,128]{1,0:T(8,128)S(1)}, f32[1024,128]{1,0:T(8,128)}, u32[]{:S(2)}, u32[]{:S(2)}) collective-permute-start(f32[1024,128]{1,0:T(8,128)S(1)} %get-tuple-element.29), channel_id=1, source_target_pairs={{0,12},{4,8},{8,4},{12,0},{1,13},{5,9},{9,5},{13,1},{2,14},{6,10},... | collective-permute-start | bytes 1572872 | tf_op jit(solution)/shard_map/ppermute | solution.py:19
  652.1 19.6 %collective-permute-start.46 = (f32[1024,128]{1,0:T(8,128)S(1)}, f32[1024,128]{1,0:T(8,128)S(1)}, u32[]{:S(2)}, u32[]{:S(2)}) collective-permute-start(f32[1024,128]{1,0:T(8,128)S(1)} %get-tuple-element.17), channel_id=1, source_target_pairs={{0,4},{4,0},{8,12},{12,8},{1,5},{5,1},{9,13},{13,9},{2,6},{6,2},{1... | collective-permute-start | bytes 1572872 | tf_op jit(solution)/shard_map/ppermute | solution.py:19
  652.2 36.6 %collective-permute-start.47 = (f32[1024,128]{1,0:T(8,128)S(1)}, f32[1024,128]{1,0:T(8,128)S(1)}, u32[]{:S(2)}, u32[]{:S(2)}) collective-permute-start(f32[1024,128]{1,0:T(8,128)S(1)} %get-tuple-element.17), channel_id=1, source_target_pairs={{0,8},{4,12},{8,0},{12,4},{1,9},{5,13},{9,1},{13,5},{2,10},{6,14},... | collective-permute-start | bytes 1572872 | tf_op jit(solution)/shard_map/ppermute | solution.py:19
  654.0 45.7 %collective-permute-start.48 = (f32[1024,128]{1,0:T(8,128)S(1)}, f32[1024,128]{1,0:T(8,128)S(1)}, u32[]{:S(2)}, u32[]{:S(2)}) collective-permute-start(f32[1024,128]{1,0:T(8,128)S(1)} %get-tuple-element.17), channel_id=1, source_target_pairs={{0,12},{4,8},{8,4},{12,0},{1,13},{5,9},{9,5},{13,1},{2,14},{6,10},... | collective-permute-start | bytes 1572872 | tf_op jit(solution)/shard_map/ppermute | solution.py:19
  (27 other events, 407.9 us)

commit v2 on v1

v2 whole, which is shorter than its diff:
```python
import functools

import jax
import jax.numpy as jnp
from jax import lax
from jax.experimental import pallas as pl
from jax.experimental.pallas import tpu as pltpu
from jax.sharding import PartitionSpec as P

HALF = jnp.bfloat16
FULL = jnp.float32


def product_kernel(cfg, *refs):
    refs = list(refs)
    tile_p, tile_r, dst, offs, pattern = refs[:5]
    matrix = refs[5]
    at = 6
    terms = refs[at : at + len(cfg["signs"])]
    at += len(cfg["signs"])
    pieces = refs[at : at + cfg["pieces"]]
    at += cfg["pieces"]
    addend = refs[at] if cfg["addend"] else None
    at += 1 if cfg["addend"] else 0
    out = refs[at]
    at += 1
    ordered = refs[at] if cfg["ordered"] else None
    at += 1 if cfg["ordered"] else 0
    vector = refs[at]
    transposed, depth, vectors = cfg["transposed"], cfg["depth"], cfg["vectors"]
    step = pl.program_id(0)

    @pl.when(step == 0)
    def _():
        if pieces:
            target = ordered if transposed else vector
            count = 0
            for piece in pieces:
                size = cfg["piece"]
                for n in range(piece.shape[0] // size):
                    row = pl.multiple_of(offs[count], size)
                    target[pl.ds(row, size), :] = piece[pl.ds(n * size, size), :].astype(
                        target.dtype
                    )
                    count += 1
        chunk = min(512, depth)
        for base in range(0, vectors * depth, chunk):
            if pieces:
                if not transposed:
                    break
                value = ordered[pl.ds(base, chunk), :]
            else:
                value = None
                for term, sign in zip(terms, cfg["signs"]):
                    part = term[pl.ds(base, chunk), :].astype(FULL)
                    if value is None:
                        value = part
                    else:
                        value = value + part if sign > 0 else value - part
            if transposed:
                which, column = base // depth, base % depth
                vector[pl.ds(which * 128, 128), pl.ds(column, chunk)] = value.T.astype(HALF)
            else:
                vector[pl.ds(base, chunk), :] = value.astype(HALF)

    tile, granule, block = cfg["tile"], cfg["granule"], cfg["block"]
    blocks_r, blocks_c, other = cfg["blocks_r"], cfg["blocks_c"], cfg["other"]
    for sub in range(tile // block):
        result = None
        for lead in range(matrix.shape[0]):
            index = lead if cfg["sum_p"] else tile_p[step]
            start = 0
            if vectors > 1:
                stride = 128 if transposed else depth
                start = index * stride
                if not cfg["sum_p"]:
                    start = pl.multiple_of(start, stride)
            if transposed:
                x = vector[pl.ds(start, 128), :]
                a = matrix[lead, :, pl.ds(sub * block, block)]
            else:
                x = vector[pl.ds(start, depth), :]
                a = matrix[lead, pl.ds(sub * block, block), :]
            if cfg["masked"]:
                here = (tile_r[step] * tile + sub * block) // cfg["pattern_block"]
                kept = []
                for n in range(depth // other):
                    if transposed:
                        flag = pattern[(index * blocks_r + n) * blocks_c + here]
                        part = x[:, n * other : (n + 1) * other]
                    else:
                        flag = pattern[(index * blocks_r + here) * blocks_c + n]
                        part = x[n * other : (n + 1) * other, :]
                    kept.append((part.astype(FULL) * flag.astype(FULL)).astype(HALF))
                if len(kept) > 1:
                    x = jnp.concatenate(kept, axis=1 if transposed else 0)
                else:
                    x = kept[0]
            if transposed:
                term = jnp.dot(x, a, preferred_element_type=FULL)
            else:
                term = jnp.dot(a, x, preferred_element_type=FULL)
            result = term if result is None else result + term
        if transposed:
            result = result.T
        for g in range(block // granule):
            row = pl.multiple_of(dst[step * (tile // granule) + sub * (block // granule) + g], granule)
            value = result[g * granule : (g + 1) * granule, :]
            if addend is not None:
                value = value + addend[pl.ds(row, granule), :]
            out[pl.ds(row, granule), :] = value


def product(
    matrix,
    *,
    transposed=False,
    terms=(),
    pieces=(),
    piece=0,
    offs=None,
    tile_p=None,
    tile_r=None,
    tile=None,
    dst=None,
    granule=None,
    pattern=None,
    sum_p=False,
    addend=None,
    ordered=False,
    vectors=1,
):
    lead, rows, cols = matrix.shape
    extent, depth = (cols, rows) if transposed else (rows, cols)
    tiles = tile_r.shape[0]
    out_rows = tiles * tile
    masked = pattern is not None
    block, other, pattern_block = tile, depth, tile
    blocks_r = blocks_c = 1
    if masked:
        blocks_r, blocks_c = pattern.shape[1:]
        pattern_block = extent // (blocks_c if transposed else blocks_r)
        other = depth // (blocks_r if transposed else blocks_c)
        block = min(tile, pattern_block)
        flags = pattern.reshape(-1)
    else:
        flags = jnp.zeros((8,), jnp.int32)
        if transposed:
            block = min(tile, 256)
    granule = min(granule or block, block)
    if dst is None:
        dst = jnp.arange(out_rows // granule, dtype=jnp.int32) * granule
    if offs is None:
        offs = jnp.zeros((8,), jnp.int32)
    if tile_p is None:
        tile_p = jnp.zeros((tiles,), jnp.int32)
    signs = tuple(sign for _, sign in terms)
    term_arrays = [array for array, _ in terms]
    x_rows = vectors * depth
    cfg = dict(
        transposed=transposed, depth=depth, vectors=vectors, signs=signs, pieces=len(pieces),
        piece=piece, addend=addend is not None, ordered=ordered, tile=tile, granule=granule,
        block=block, other=other, pattern_block=pattern_block, blocks_r=blocks_r,
        blocks_c=blocks_c, masked=masked, sum_p=sum_p,
    )
    held = lead if sum_p else 1
    if transposed:
        matrix_block = (held, depth, tile)
        matrix_map = lambda t, tp, tr, *_: (tp[t], 0, tr[t])
    else:
        matrix_block = (held, tile, depth)
        matrix_map = lambda t, tp, tr, *_: (tp[t], tr[t], 0)

    def whole(array):
        return pl.BlockSpec(array.shape, lambda t, *_: (0, 0), pipeline_mode=pl.Buffered(1))

    inputs = term_arrays + list(pieces) + ([addend] if addend is not None else [])
    out_shape = [jax.ShapeDtypeStruct((out_rows, 128), FULL)]
    out_specs = [pl.BlockSpec((out_rows, 128), lambda t, *_: (0, 0))]
    if ordered:
        out_shape.append(jax.ShapeDtypeStruct((x_rows, 128), FULL))
        out_specs.append(pl.BlockSpec((x_rows, 128), lambda t, *_: (0, 0)))
    scratch = (vectors * 128, depth) if transposed else (x_rows, 128)
    matrix_bytes = held * depth * tile * 2
    resident = sum(a.size * a.dtype.itemsize for a in inputs)
    written = sum(s.size * 4 for s in out_shape)
    budget = 2 * matrix_bytes + resident + 2 * written + x_rows * 256 + (12 << 20)
    budget = max(budget, 57 << 20)
    result = pl.pallas_call(
        functools.partial(product_kernel, cfg),
        grid_spec=pltpu.PrefetchScalarGridSpec(
            num_scalar_prefetch=5,
            grid=(tiles,),
            in_specs=[pl.BlockSpec(matrix_block, matrix_map)] + [whole(a) for a in inputs],
            out_specs=out_specs,
            scratch_shapes=[pltpu.VMEM(scratch, HALF)],
        ),
        out_shape=out_shape,
        compiler_params=pltpu.CompilerParams(vmem_limit_bytes=int(budget)),
        cost_estimate=pl.CostEstimate(
            flops=2 * tiles * tile * depth * held * 128,
            bytes_accessed=tiles * matrix_bytes + resident + written,
            transcendentals=0,
        ),
    )(tile_p, tile_r, dst, offs, flags, matrix, *inputs)
    return tuple(result) if ordered else result[0]


def ints(values):
    return jnp.stack([jnp.asarray(v, jnp.int32) for v in values]).reshape(-1)


def make_shards(sizes):
    rows, cols, leaves = sizes["row"], sizes["col"], sizes["leaf"]

    def send(value, axis, bit):
        size = sizes[axis]
        return lax.ppermute(value, axis, [(i, i ^ bit) for i in range(size)])

    def row_terms(part, sign=1):
        if rows == 2:
            return [(part, sign), (send(part, "row", 1), sign)]
        return [(lax.psum(part, "row"), sign)]

    def total(terms):
        value = terms[0][0]
        for term, sign in terms[1:]:
            value = value + term if sign > 0 else value - term
        return value

    def col_reduce(blocks):
        value = blocks[0]
        for k, block in [(k, send(blocks[k], "col", k)) for k in range(1, cols)]:
            value = value + block
        return value

    def col_collect(value):
        return [value] + [send(value, "col", k) for k in range(1, cols)]

    def shards(
        rhs_leaf,
        rhs_mid,
        rhs_root,
        inverse_leaf,
        inverse_mid,
        inverse_root,
        factor_leaf_mid,
        factor_leaf_root,
        factor_mid_root,
        pattern_leaf_mid,
        pattern_leaf_root,
        pattern_mid_root,
    ):
        leaf = lax.axis_index("leaf")
        col = lax.axis_index("col")
        owner = leaf // 2
        parity = leaf % 2
        inverse_root = inverse_root[None]
        full = rhs_root.shape[0]
        split = full // 2
        cut_mid = split // cols
        cut_root = cut_mid // 2
        own = inverse_mid.shape[1]
        unit = full // pattern_leaf_mid.shape[1]

        def tiles(count, start=0):
            return jnp.arange(count, dtype=jnp.int32) + start

        def fit(extent, limit):
            return min(extent, limit)

        def half_start(i, tile):
            return (parity ^ i) * (split // tile)

        def order(sub, granule, with_pair):
            pairs = 2 if with_pair else 1
            spots = []
            for j in range(pairs):
                for k in range(cols):
                    spot = (((j ^ owner) if with_pair else 0) * cols + (k ^ col)) * sub
                    spots += [spot + n * granule for n in range(sub // granule)]
            return ints(spots)

        def pair_sum(make):
            there = make(1)
            arrived = send(there, "leaf", 1)
            return make(0), arrived

        def plane_reduce(here, arrived, cut):
            shape = (2, cols, cut, 128)
            here, arrived = here.reshape(shape), arrived.reshape(shape)
            first = min(max(8, (2 * cut // 3 + 4) // 8 * 8), cut - 8)
            rest = cut - first

            def part(j, k, low, high):
                return here[j, k, low:high] + arrived[j, k, low:high]

            across = send(
                (here[1, :, :first] + arrived[1, :, :first]).reshape(cols * first, 128), "leaf", 2
            )
            moved = [
                send(
                    (here[:, k, first:] + arrived[:, k, first:]).reshape(2 * rest, 128), "col", k
                )
                for k in range(1, cols)
            ]
            near = [
                part(0, k, 0, first) + across[k * first : (k + 1) * first] for k in range(cols)
            ]
            low = col_reduce(near)
            far = part(1, 0, first, cut)
            high = part(0, 0, first, cut)
            for block in moved:
                far = far + block[rest:]
                high = high + block[:rest]
            high = high + send(far, "leaf", 2)
            return jnp.concatenate([low, high])

        def root_reduce(make):
            here, arrived = pair_sum(make)
            return plane_reduce(here, arrived, cut_root)

        def root_collect(value):
            blocks = col_collect(value)
            across = jnp.concatenate([send(b, "leaf", 2) for b in blocks])
            near = jnp.concatenate(blocks)
            gathered = [near, across, send(near, "leaf", 1), send(across, "leaf", 1)]
            spots = [
                (((parity ^ i) * 2 + (owner ^ j)) * cols + (col ^ k)) * cut_root
                for i in range(2)
                for j in range(2)
                for k in range(cols)
            ]
            return gathered, ints(spots)

        tile = fit(inverse_leaf.shape[1], 256)
        leaf_part = product(
            inverse_leaf,
            terms=[(rhs_leaf[0], 1)],
            tile_r=tiles(inverse_leaf.shape[1] // tile),
            tile=tile,
        )
        forward_leaf = row_terms(leaf_part)

        def make_mid(i):
            tile = fit(split, 512)
            granule = min(cut_mid, unit)
            return product(
                factor_leaf_mid,
                terms=forward_leaf,
                pattern=pattern_leaf_mid,
                tile_r=tiles(split // tile, half_start(i, tile)),
                tile=tile,
                granule=granule,
                dst=order(cut_mid, granule, False),
            )

        here, arrived = pair_sum(make_mid)
        summed = here + arrived
        to_mid = col_reduce([summed[k * cut_mid : (k + 1) * cut_mid] for k in range(cols)])
        own_rhs = lax.dynamic_slice(
            rhs_mid, (owner, parity * split + col * cut_mid, 0), (1, cut_mid, 128)
        )[0]
        blocks = col_collect(own_rhs - to_mid)
        across = jnp.concatenate([send(b, "leaf", 2) for b in blocks])
        near = jnp.concatenate(blocks)
        mid_pieces = [near, across, send(near, "leaf", 1), send(across, "leaf", 1)]
        mid_offs = ints(
            [
                (owner ^ j) * full + (parity ^ i) * split + (col ^ k) * cut_mid
                for i in range(2)
                for j in range(2)
                for k in range(cols)
            ]
        )

        def make_leaf_root(i):
            tile = fit(split, 512)
            granule = min(cut_root, unit)
            return product(
                factor_leaf_root,
                terms=forward_leaf,
                pattern=pattern_leaf_root,
                tile_r=tiles(split // tile, half_start(i, tile)),
                tile=tile,
                granule=granule,
                dst=order(cut_root, granule, True),
            )

        leaf_root_parts = [make_leaf_root(0), make_leaf_root(1)]

        tile = fit(own, 256)
        mid_part = product(
            inverse_mid,
            pieces=mid_pieces,
            piece=cut_mid,
            offs=mid_offs,
            vectors=2,
            tile_p=ints([p for p in range(2) for _ in range(own // tile)]),
            tile_r=ints([n for _ in range(2) for n in range(own // tile)]),
            tile=tile,
        )
        forward_mid = row_terms(mid_part)

        def make_root(i):
            tile = fit(split, 1024)
            granule = min(cut_root, unit)
            return product(
                factor_mid_root,
                terms=forward_mid,
                pattern=pattern_mid_root,
                vectors=2,
                sum_p=True,
                tile_r=tiles(split // tile, half_start(i, tile)),
                tile=tile,
                granule=granule,
                dst=order(cut_root, granule, True),
                addend=leaf_root_parts[i],
            )

        to_root = root_reduce(make_root)
        offset = ((parity * 2 + owner) * cols + col) * cut_root
        own_rhs = lax.dynamic_slice(rhs_root, (offset, 0), (cut_root, 128))
        root_pieces, root_offs = root_collect(own_rhs - to_root)
        tile = fit(own, 256)
        root_part = product(
            inverse_root,
            pieces=root_pieces,
            piece=cut_root,
            offs=root_offs,
            tile_r=tiles(own // tile),
            tile=tile,
        )
        root_terms = row_terms(root_part)
        forward_root = total(root_terms)

        def make_back_root(i):
            tile = fit(split, 1024)
            granule = min(cut_root, unit)
            return product(
                inverse_root,
                transposed=True,
                terms=root_terms,
                tile_r=tiles(split // tile, half_start(i, tile)),
                tile=tile,
                granule=granule,
                dst=order(cut_root, granule, True),
            )

        root_pieces, root_offs = root_collect(root_reduce(make_back_root))
        tile = fit(own, 256)
        mid_back, solve_root = product(
            factor_mid_root,
            transposed=True,
            pieces=root_pieces,
            piece=cut_root,
            offs=root_offs,
            pattern=pattern_mid_root,
            tile_p=ints([p for p in range(2) for _ in range(own // tile)]),
            tile_r=ints([n for _ in range(2) for n in range(own // tile)]),
            tile=tile,
            ordered=True,
        )
        corrected_mid = forward_mid + row_terms(mid_back, -1)

        def make_back_mid(i):
            tile = fit(split, 1024)
            granule = min(cut_mid, unit)
            count = split // tile
            return product(
                inverse_mid,
                transposed=True,
                terms=corrected_mid,
                vectors=2,
                tile_p=ints([p for p in range(2) for _ in range(count)]),
                tile_r=jnp.tile(tiles(count, half_start(i, tile)), 2),
                tile=tile,
                granule=granule,
                dst=order(cut_mid, granule, True),
            )

        here, arrived = pair_sum(make_back_mid)
        mid_piece = plane_reduce(here, arrived, cut_mid)
        near = jnp.concatenate(col_collect(mid_piece))
        tile = fit(factor_leaf_root.shape[2], 256)
        leaf_tiles = tiles(factor_leaf_root.shape[2] // tile)
        back_part = product(
            factor_leaf_root,
            transposed=True,
            terms=[(solve_root, 1)],
            pattern=pattern_leaf_root,
            tile_r=leaf_tiles,
            tile=tile,
        )
        back_part, mid_own = product(
            factor_leaf_mid,
            transposed=True,
            pieces=[near, send(near, "leaf", 1)],
            piece=cut_mid,
            offs=ints(
                [(parity ^ i) * split + (col ^ k) * cut_mid for i in range(2) for k in range(cols)]
            ),
            pattern=pattern_leaf_mid,
            tile_r=leaf_tiles,
            tile=tile,
            addend=back_part,
            ordered=True,
        )
        corrected_leaf = total(forward_leaf + row_terms(back_part, -1))
        mid_other = send(mid_own, "leaf", 2)
        solve_mid = jnp.where(
            owner == 0, jnp.stack([mid_own, mid_other]), jnp.stack([mid_other, mid_own])
        )
        cut_leaf = full // cols
        tile = fit(cut_leaf, 512)

        def make_leaf(k):
            count = cut_leaf // tile
            return product(
                inverse_leaf,
                transposed=True,
                terms=[(corrected_leaf, 1)],
                tile_r=tiles(count, (col ^ k) * count),
                tile=tile,
            )

        away = [(k, send(make_leaf(k), "col", k)) for k in range(1, cols)]
        leaf_piece = make_leaf(0)
        for _, block in away:
            leaf_piece = leaf_piece + block
        solve_leaf = jnp.zeros((cols, cut_leaf, 128), FULL)
        for k, block in enumerate(col_collect(leaf_piece)):
            solve_leaf = lax.dynamic_update_index_in_dim(solve_leaf, block, col ^ k, 0)
        return (solve_leaf.reshape(1, full, 128), solve_mid, solve_root, forward_root)

    return shards


def solution(mesh):
    return jax.shard_map(
        make_shards(dict(mesh.shape)),
        mesh=mesh,
        in_specs=(
            P("leaf", "row", None),
            P(None, "row", None),
            P("row", None),
            P("leaf", "col", "row"),
            P(None, ("col", "leaf"), "row"),
            P(("col", "leaf"), "row"),
            P("leaf", "row", "col"),
            P("leaf", "row", "col"),
            P(None, "row", ("col", "leaf")),
            P("leaf", "row", "col"),
            P("leaf", "row", "col"),
            P(None, "row", ("col", "leaf")),
        ),
        out_specs=(
            P("leaf", "row", None),
            P(None, "row", None),
            P("row", None),
            P(("col", "leaf"), None),
        ),
        check_vma=False,
    )
```

time: 713 us -> 551 us (0.77); the launches traced: 701 us -> 550 us
  local copies, waits for them, and re-layouts: 180 us -> 17.5 us
  Pallas kernels: 0 us -> 143 us
  matrix products: 94.6 us -> 0 us
  waiting for transfers between devices: 353 us -> 272 us
  starting transfers between devices: 54.3 us -> 86.3 us
  other arithmetic: 18.6 us -> 30.1 us
    pallas_call x0 -> x20, Pallas kernels: none -> 143 us  [product(): pl.pallas_call(functools.partial(product_kernel, cfg), grid_spec=pltpu.Pr...]
    mul x9 -> x0, local copies, waits for them, and re-layouts: 106 us -> none  [masked_blocks(): return (tiles * keeper).reshape(leading, row_count, col_count)]
    dot_general x12 -> x0, matrix products: 94.6 us -> none  [the longest x4 44.9 us: dot_t(): return jnp.einsum('ji,jk->ik', a, b, preferred_element_type=jnp.float32)]
    ppermute x50 -> x74, waiting for transfers between devices: 353 us -> 272 us  [send(): return lax.ppermute(value, axis, [(i, i ^ bit) for i in range(size)])]
    ppermute x50 -> x74, starting transfers between devices: 54.3 us -> 86.3 us  [send(): return lax.ppermute(value, axis, [(i, i ^ bit) for i in range(size)])]
    unnamed x54 -> x76, local copies, waits for them, and re-layouts: 36 us -> 5.86 us
    add x10 -> x24, other arithmetic: 4.47 us -> 17.4 us  [the longest x8 4.39 us: tiles(): return jnp.arange(count, dtype=jnp.int32) + start]
    reshape x4 -> x3, local copies, waits for them, and re-layouts: 11.7 us -> 2 us  [product(): flags = pattern.reshape(-1)]
  transfers between devices with their start and end apart: 50 -> 74, of which waited for: 43 -> 41; matrix products, arithmetic and copies ran while one was open for 24% -> 5% of each run, Pallas kernels for 0% -> 13%
where the time goes in v2:
time: 551 us; the launch traced here: 550 us
  waiting for transfers between devices  272 us (49%)
  Pallas kernels  143 us (26%)
  starting transfers between devices  86.3 us (16%)
  other arithmetic  30.1 us (5%)
  local copies, waits for them, and re-layouts  17.5 us (3%)
    ppermute x74, waiting for transfers between devices, send(): return lax.ppermute(value, axis, [(i, i ^ bit) for i in range(size)])  272 us
    pallas_call x20, Pallas kernels, product(): pl.pallas_call(functools.partial(product_kernel, cfg), grid_spec=pltpu.Pr...  143 us
    ppermute x74, starting transfers between devices, send(): return lax.ppermute(value, axis, [(i, i ^ bit) for i in range(size)])  86.3 us
  transfers between devices with their start and end apart: 74, of which 41 were waited for; matrix products, arithmetic and copies ran while one was open for 5% of the time, Pallas kernels for 13%

profile of v2, /device:TPU:8, one launch (start us, length us, event | category | flops | bytes accessed | tf_op | source)
XLA Modules:
  0.0 549.8 jit_solution(15054299406383574702)
XLA Ops:
  2.2 13.0 %shard_map.147.refs_6_ = f32[2048,128]{1,0:T(8,128)} custom-call(s32[8]{0:T(128)} %broadcast_11_refs_0__refs_3__refs_4_.2.refs_0_.refs_3_.refs_4_, s32[8]{0:T(128)} %iota.77.refs_1_, s32[8]{0:T(128)} %iota_multiply_fusion.1.refs_2_, s32[8]{0:T(128)} %broadcast_11_refs_0__refs_3__refs_4_.2.refs_0_.refs_3_.refs_4_, ...), custom_call_target="tpu_custom_call" | custom-call | flops 2147483648 | bytes 19922944 | tf_op jit(solution)/shard_map/pallas_call | solution.py:189
  18.6 21.7 %collective-permute-done.refs_7_ = f32[2048,128]{1,0:T(8,128)S(1)} collective-permute-done((f32[2048,128]{1,0:T(8,128)}, f32[2048,128]{1,0:T(8,128)S(1)}, u32[]{:S(2)}, u32[]{:S(2)}) %collective-permute-start) | collective-permute-done | bytes 1048608 | tf_op jit(solution)/shard_map/ppermute | solution.py:218
  41.3 7.9 %shard_map.149 = f32[2048,128]{1,0:T(8,128)} custom-call(s32[4]{0:T(128)} %broadcast_9_refs_0_.2.refs_0_, s32[4]{0:T(128)} %iota_add_fusion.4.refs_1_, s32[8]{0:T(128)} %stack.387.refs_2_, s32[8]{0:T(128)} %broadcast_11_refs_0__refs_3__refs_4_.2.refs_0_.refs_3_.refs_4_, s32[128]{0:T(128)} %reshape.118.refs_4_, bf16[1,4096,2048]{2,1,0:T(8,128)(2,1)} %refs_5_.29, ...), custom_call_target="tpu_custom_call" | custom-call | flops 1073741824 | bytes 11534336 | tf_op jit(solution)/shard_map/pallas_call | solution.py:189
  49.8 7.9 %shard_map.148 = f32[2048,128]{1,0:T(8,128)} custom-call(s32[4]{0:T(128)} %broadcast_9_refs_0_.2.refs_0_, s32[4]{0:T(128)} %iota_add_fusion.5.refs_1_, s32[8]{0:T(128)} %stack.387.refs_2_, s32[8]{0:T(128)} %broadcast_11_refs_0__refs_3__refs_4_.2.refs_0_.refs_3_.refs_4_, s32[128]{0:T(128)} %reshape.118.refs_4_, bf16[1,4096,2048]{2,1,0:T(8,128)(2,1)} %refs_5_.29, ...), custom_call_target="tpu_custom_call" | custom-call | flops 1073741824 | bytes 11534336 | tf_op jit(solution)/shard_map/pallas_call | solution.py:189
  63.2 16.3 %collective-permute-done.4 = f32[512,128]{1,0:T(8,128)S(1)} collective-permute-done((f32[512,128]{1,0:T(8,128)S(1)}, f32[512,128]{1,0:T(8,128)S(1)}, u32[]{:S(2)}, u32[]{:S(2)}) %collective-permute-start.4) | collective-permute-done | bytes 262176 | tf_op jit(solution)/shard_map/ppermute | solution.py:218
  79.5 4.3 collective-permute-done.3
  90.3 7.3 %collective-permute-done.5 = f32[512,128]{1,0:T(8,128)S(1)} collective-permute-done((f32[512,128]{1,0:T(8,128)S(1)}, f32[512,128]{1,0:T(8,128)S(1)}, u32[]{:S(2)}, u32[]{:S(2)}) %collective-permute-start.5) | collective-permute-done | bytes 262176 | tf_op jit(solution)/shard_map/ppermute | solution.py:218
  99.1 7.2 %collective-permute-done.6 = f32[512,128]{1,0:T(8,128)S(1)} collective-permute-done((f32[512,128]{1,0:T(8,128)S(1)}, f32[512,128]{1,0:T(8,128)S(1)}, u32[]{:S(2)}, u32[]{:S(2)}) %collective-permute-start.6) | collective-permute-done | bytes 262176 | tf_op jit(solution)/shard_map/ppermute | solution.py:218
  107.8 3.9 collective-permute-done.7
  113.5 7.1 %collective-permute-done.11 = f32[512,128]{1,0:T(8,128)S(1)} collective-permute-done((f32[512,128]{1,0:T(8,128)S(1)}, f32[512,128]{1,0:T(8,128)S(1)}, u32[]{:S(2)}, u32[]{:S(2)}) %collective-permute-start.11) | collective-permute-done | bytes 262176 | tf_op jit(solution)/shard_map/ppermute | solution.py:218
  123.4 8.4 %shard_map.150.refs_6_ = f32[1024,128]{1,0:T(8,128)} custom-call(s32[4]{0:T(128)} %constant.62.clone.1.refs_0_, s32[4]{0:T(128)} %constant.65.clone.1.refs_1_, s32[4]{0:T(128)} %iota_multiply_fusion.2.refs_2_, s32[16]{0:T(128)} %stack.378.refs_3_, s32[8]{0:T(128)} %broadcast_11_refs_0__refs_3__refs_4_.2.refs_0_.refs_3_.refs_4_, ...), custom_call_target="tpu_custom_call" | custom-call | flops 1073741824 | bytes 13107200 | tf_op jit(solution)/shard_map/pallas_call | solution.py:189
  136.1 7.9 %shard_map.153.refs_8_ = f32[2048,128]{1,0:T(8,128)} custom-call(s32[4]{0:T(128)} %broadcast_9_refs_0_.2.refs_0_, s32[4]{0:T(128)} %iota_add_fusion.4.refs_1_, s32[8]{0:T(128)} %stack.413.refs_2_, s32[8]{0:T(128)} %broadcast_11_refs_0__refs_3__refs_4_.2.refs_0_.refs_3_.refs_4_, s32[128]{0:T(128)} %reshape.120.refs_4_, bf16[1,4096,2048]{2,1,0:T(8,128)(2,1)} %refs_5_.28, ...), custom_call_target="tpu_custom_call" | custom-call | flops 1073741824 | bytes 11534336 | tf_op jit(solution)/shard_map/pallas_call | solution.py:189
  146.8 5.4 shard_map.154
  152.7 7.9 %shard_map.151.refs_8_ = f32[2048,128]{1,0:T(8,128)} custom-call(s32[4]{0:T(128)} %broadcast_9_refs_0_.2.refs_0_, s32[4]{0:T(128)} %iota_add_fusion.5.refs_1_, s32[8]{0:T(128)} %stack.413.refs_2_, s32[8]{0:T(128)} %broadcast_11_refs_0__refs_3__refs_4_.2.refs_0_.refs_3_.refs_4_, s32[128]{0:T(128)} %reshape.120.refs_4_, bf16[1,4096,2048]{2,1,0:T(8,128)(2,1)} %refs_5_.28, ...), custom_call_target="tpu_custom_call" | custom-call | flops 1073741824 | bytes 11534336 | tf_op jit(solution)/shard_map/pallas_call | solution.py:189
  160.6 5.4 shard_map.152
  173.1 5.7 %collective-permute-done.22 = f32[176,128]{1,0:T(8,128)S(1)} collective-permute-done((f32[176,128]{1,0:T(8,128)S(1)}, f32[176,128]{1,0:T(8,128)S(1)}, u32[]{:S(2)}, u32[]{:S(2)}) %collective-permute-start.22) | collective-permute-done | bytes 90144 | tf_op jit(solution)/shard_map/ppermute | solution.py:218
  200.9 5.9 %collective-permute-done.26 = f32[256,128]{1,0:T(8,128)S(1)} collective-permute-done((f32[256,128]{1,0:T(8,128)S(1)}, f32[256,128]{1,0:T(8,128)S(1)}, u32[]{:S(2)}, u32[]{:S(2)}) %collective-permute-start.26) | collective-permute-done | bytes 131104 | tf_op jit(solution)/shard_map/ppermute | solution.py:218
  210.1 4.2 collective-permute-done.29
  219.5 5.1 shard_map.155.refs_6_
  226.1 7.1 %collective-permute-done.33.refs_7_ = f32[512,128]{1,0:T(8,128)S(1)} collective-permute-done((f32[512,128]{1,0:T(8,128)}, f32[512,128]{1,0:T(8,128)S(1)}, u32[]{:S(2)}, u32[]{:S(2)}) %collective-permute-start.33) | collective-permute-done | bytes 262176 | tf_op jit(solution)/shard_map/ppermute | solution.py:218
  233.9 4.0 shard_map.157
  237.9 4.0 shard_map.156
  246.2 4.0 collective-permute-start.40
  255.2 4.0 collective-permute-start.37
  274.6 4.4 collective-permute-done.44
  284.1 4.2 collective-permute-done.48
  293.5 8.0 %shard_map.158 = (f32[1024,128]{1,0:T(8,128)}, f32[4096,128]{1,0:T(8,128)}) custom-call(s32[4]{0:T(128)} %constant.62.clone.1.refs_0_, s32[4]{0:T(128)} %constant.65.clone.1.refs_1_, s32[4]{0:T(128)} %iota_multiply_fusion.2.refs_2_, s32[16]{0:T(128)} %stack.404.refs_3_, s32[64]{0:T(128)} %reshape.119.refs_4_, bf16[2,4096,512]{2,1,0:T(8,128)(2,1)} %refs_5_.25, ...), custom_call_target="tpu_custom_call" | custom-call | flops 1073741824 | bytes 13107200 | tf_op jit(solution)/shard_map/pallas_call | solution.py:189
  304.3 11.4 %collective-permute-done.52.refs_9_ = f32[1024,128]{1,0:T(8,128)S(1)} collective-permute-done((f32[1024,128]{1,0:T(8,128)}, f32[1024,128]{1,0:T(8,128)S(1)}, u32[]{:S(2)}, u32[]{:S(2)}) %collective-permute-start.52) | collective-permute-done | bytes 524320 | tf_op jit(solution)/shard_map/ppermute | solution.py:218
  316.5 6.7 %shard_map.160 = f32[4096,128]{1,0:T(8,128)} custom-call(s32[4]{0:T(128)} %constant.62.clone.1.refs_0_, s32[4]{0:T(128)} %tile.21.refs_1_, s32[16]{0:T(128)} %stack.361.refs_2_, s32[8]{0:T(128)} %broadcast_11_refs_0__refs_3__refs_4_.2.refs_0_.refs_3_.refs_4_, s32[8]{0:T(128)} %broadcast_11_refs_0__refs_3__refs_4_.2.refs_0_.refs_3_.refs_4_, ...), custom_call_target="tpu_custom_call" | custom-call | flops 536870912 | bytes 8388608 | tf_op jit(solution)/shard_map/pallas_call | solution.py:189
  323.8 6.7 %shard_map.159 = f32[4096,128]{1,0:T(8,128)} custom-call(s32[4]{0:T(128)} %constant.62.clone.1.refs_0_, s32[4]{0:T(128)} %tile.9.refs_1_, s32[16]{0:T(128)} %stack.361.refs_2_, s32[8]{0:T(128)} %broadcast_11_refs_0__refs_3__refs_4_.2.refs_0_.refs_3_.refs_4_, s32[8]{0:T(128)} %broadcast_11_refs_0__refs_3__refs_4_.2.refs_0_.refs_3_.refs_4_, ...), custom_call_target="tpu_custom_call" | custom-call | flops 536870912 | bytes 8388608 | tf_op jit(solution)/shard_map/pallas_call | solution.py:189
  336.9 13.1 %collective-permute-done.54 = f32[1376,128]{1,0:T(8,128)S(1)} collective-permute-done((f32[1376,128]{1,0:T(8,128)S(1)}, f32[1376,128]{1,0:T(8,128)S(1)}, u32[]{:S(2)}, u32[]{:S(2)}) %collective-permute-start.54) | collective-permute-done | bytes 704544 | tf_op jit(solution)/shard_map/ppermute | solution.py:218
  355.2 9.1 %collective-permute-done.57 = f32[344,128]{1,0:T(8,128)S(1)} collective-permute-done((f32[344,128]{1,0:T(8,128)S(1)}, f32[344,128]{1,0:T(8,128)S(1)}, u32[]{:S(2)}, u32[]{:S(2)}) %collective-permute-start.57) | collective-permute-done | bytes 176160 | tf_op jit(solution)/shard_map/ppermute | solution.py:218
  370.8 8.8 %collective-permute-done.62 = f32[512,128]{1,0:T(8,128)S(1)} collective-permute-done((f32[512,128]{1,0:T(8,128)S(1)}, f32[512,128]{1,0:T(8,128)S(1)}, u32[]{:S(2)}, u32[]{:S(2)}) %collective-permute-start.62) | collective-permute-done | bytes 262176 | tf_op jit(solution)/shard_map/ppermute | solution.py:218
  379.6 8.6 %collective-permute-done.63 = f32[512,128]{1,0:T(8,128)S(1)} collective-permute-done((f32[512,128]{1,0:T(8,128)S(1)}, f32[512,128]{1,0:T(8,128)S(1)}, u32[]{:S(2)}, u32[]{:S(2)}) %collective-permute-start.63) | collective-permute-done | bytes 262176 | tf_op jit(solution)/shard_map/ppermute | solution.py:218
  388.3 5.6 %collective-permute-done.64 = f32[512,128]{1,0:T(8,128)S(1)} collective-permute-done((f32[512,128]{1,0:T(8,128)S(1)}, f32[512,128]{1,0:T(8,128)S(1)}, u32[]{:S(2)}, u32[]{:S(2)}) %collective-permute-start.64) | collective-permute-done | bytes 262176 | tf_op jit(solution)/shard_map/ppermute | solution.py:218
  395.3 12.2 %shard_map.161.refs_8_ = f32[2048,128]{1,0:T(8,128)} custom-call(s32[8]{0:T(128)} %broadcast_11_refs_0__refs_3__refs_4_.2.refs_0_.refs_3_.refs_4_, s32[8]{0:T(128)} %iota.86.refs_1_, s32[8]{0:T(128)} %iota_multiply_fusion.1.refs_2_, s32[8]{0:T(128)} %broadcast_11_refs_0__refs_3__refs_4_.2.refs_0_.refs_3_.refs_4_, s32[128]{0:T(128)} %reshape.120.refs_4_, ...), custom_call_target="tpu_custom_call" | custom-call | flops 2147483648 | bytes 19922944 | tf_op jit(solution)/shard_map/pallas_call | solution.py:189
  409.0 13.3 %shard_map.162 = (f32[2048,128]{1,0:T(8,128)}, f32[4096,128]{1,0:T(8,128)}) custom-call(s32[8]{0:T(128)} %broadcast_11_refs_0__refs_3__refs_4_.2.refs_0_.refs_3_.refs_4_, s32[8]{0:T(128)} %iota.79.refs_1_, s32[8]{0:T(128)} %iota_multiply_fusion.1.refs_2_, s32[8]{0:T(128)} %stack.344.refs_3_, s32[128]{0:T(128)} %reshape.118.refs_4_, ...), custom_call_target="tpu_custom_call" | custom-call | flops 2147483648 | bytes 23068672 | tf_op jit(solution)/shard_map/pallas_call | solution.py:189
  427.0 20.9 %collective-permute-done.66 = f32[2048,128]{1,0:T(8,128)S(1)} collective-permute-done((f32[2048,128]{1,0:T(8,128)}, f32[2048,128]{1,0:T(8,128)S(1)}, u32[]{:S(2)}, u32[]{:S(2)}) %collective-permute-start.66) | collective-permute-done | bytes 1048608 | tf_op jit(solution)/shard_map/ppermute | solution.py:218
  450.3 4.7 shard_map.166
  456.5 4.7 shard_map.165
  461.2 4.8 shard_map.164
  469.2 4.7 shard_map.163
  473.9 14.5 %collective-permute-done.69 = f32[1024,128]{1,0:T(8,128)S(1)} collective-permute-done((f32[1024,128]{1,0:T(8,128)}, f32[1024,128]{1,0:T(8,128)S(1)}, u32[]{:S(2)}, u32[]{:S(2)}) %collective-permute-start.69) | collective-permute-done | bytes 524320 | tf_op jit(solution)/shard_map/ppermute | solution.py:218
  488.4 10.3 %collective-permute-done.68 = f32[1024,128]{1,0:T(8,128)S(1)} collective-permute-done((f32[1024,128]{1,0:T(8,128)}, f32[1024,128]{1,0:T(8,128)S(1)}, u32[]{:S(2)}, u32[]{:S(2)}) %collective-permute-start.68) | collective-permute-done | bytes 524320 | tf_op jit(solution)/shard_map/ppermute | solution.py:218
  502.9 4.7 maximum_select_fusion
  507.6 15.8 %collective-permute-done.70 = f32[1024,128]{1,0:T(8,128)S(1)} collective-permute-done((f32[1024,128]{1,0:T(8,128)S(1)}, f32[1024,128]{1,0:T(8,128)S(1)}, u32[]{:S(2)}, u32[]{:S(2)}) %collective-permute-start.70) | collective-permute-done | bytes 524320 | tf_op jit(solution)/shard_map/ppermute | solution.py:218
  523.4 13.8 %collective-permute-done.71 = f32[1024,128]{1,0:T(8,128)S(1)} collective-permute-done((f32[1024,128]{1,0:T(8,128)S(1)}, f32[1024,128]{1,0:T(8,128)S(1)}, u32[]{:S(2)}, u32[]{:S(2)}) %collective-permute-start.71) | collective-permute-done | bytes 524320 | tf_op jit(solution)/shard_map/ppermute | solution.py:218
  537.3 11.2 %collective-permute-done.72 = f32[1024,128]{1,0:T(8,128)S(1)} collective-permute-done((f32[1024,128]{1,0:T(8,128)S(1)}, f32[1024,128]{1,0:T(8,128)S(1)}, u32[]{:S(2)}, u32[]{:S(2)}) %collective-permute-start.72) | collective-permute-done | bytes 524320 | tf_op jit(solution)/shard_map/ppermute | solution.py:218
  (266 shorter events, 150.7 us)
Async XLA Ops:
  15.2 25.1 %collective-permute-start = (f32[2048,128]{1,0:T(8,128)}, f32[2048,128]{1,0:T(8,128)S(1)}, u32[]{:S(2)}, u32[]{:S(2)}) collective-permute-start(f32[2048,128]{1,0:T(8,128)} %shard_map.147.refs_6_), channel_id=1, source_target_pairs={{0,16},{16,0},{1,17},{17,1},{2,18},{18,2},{3,19},{19,3},{4,20},{20... | collective-permute-start | bytes 3145736 | tf_op jit(solution)/shard_map/ppermute | solution.py:218
  59.1 20.4 %collective-permute-start.4 = (f32[512,128]{1,0:T(8,128)S(1)}, f32[512,128]{1,0:T(8,128)S(1)}, u32[]{:S(2)}, u32[]{:S(2)}) collective-permute-start(f32[512,128]{1,0:T(8,128)S(1)} %get-tuple-element.41), channel_id=1, source_target_pairs={{0,12},{4,8},{8,4},{12,0},{1,13},{5,9},{9,5},{13,1},{2,14},{6,10},... | collective-permute-start | bytes 786440 | tf_op jit(solution)/shard_map/ppermute | solution.py:218
  60.7 23.1 %collective-permute-start.3 = (f32[512,128]{1,0:T(8,128)S(1)}, f32[512,128]{1,0:T(8,128)S(1)}, u32[]{:S(2)}, u32[]{:S(2)}) collective-permute-start(f32[512,128]{1,0:T(8,128)S(1)} %get-tuple-element.42), channel_id=1, source_target_pairs={{0,8},{4,12},{8,0},{12,4},{1,9},{5,13},{9,1},{13,5},{2,10},{6,14},... | collective-permute-start | bytes 786440 | tf_op jit(solution)/shard_map/ppermute | solution.py:218
  61.8 22.0 %collective-permute-start.2 = (f32[512,128]{1,0:T(8,128)S(1)}, f32[512,128]{1,0:T(8,128)S(1)}, u32[]{:S(2)}, u32[]{:S(2)}) collective-permute-start(f32[512,128]{1,0:T(8,128)S(1)} %get-tuple-element.40), channel_id=1, source_target_pairs={{0,4},{4,0},{8,12},{12,8},{1,5},{5,1},{9,13},{13,9},{2,6},{6,2},{1... | collective-permute-start | bytes 786440 | tf_op jit(solution)/shard_map/ppermute | solution.py:218
  84.8 12.8 %collective-permute-start.5 = (f32[512,128]{1,0:T(8,128)S(1)}, f32[512,128]{1,0:T(8,128)S(1)}, u32[]{:S(2)}, u32[]{:S(2)}) collective-permute-start(f32[512,128]{1,0:T(8,128)S(1)} %fusion.2), channel_id=1, source_target_pairs={{0,4},{4,0},{8,12},{12,8},{1,5},{5,1},{9,13},{13,9},{2,6},{6,2},{1... | collective-permute-start | bytes 786440 | tf_op jit(solution)/shard_map/ppermute | solution.py:218
  87.2 19.1 %collective-permute-start.6 = (f32[512,128]{1,0:T(8,128)S(1)}, f32[512,128]{1,0:T(8,128)S(1)}, u32[]{:S(2)}, u32[]{:S(2)}) collective-permute-start(f32[512,128]{1,0:T(8,128)S(1)} %fusion.2), channel_id=1, source_target_pairs={{0,8},{4,12},{8,0},{12,4},{1,9},{5,13},{9,1},{13,5},{2,10},{6,14},... | collective-permute-start | bytes 786440 | tf_op jit(solution)/shard_map/ppermute | solution.py:218
  88.3 23.3 %collective-permute-start.7 = (f32[512,128]{1,0:T(8,128)S(1)}, f32[512,128]{1,0:T(8,128)S(1)}, u32[]{:S(2)}, u32[]{:S(2)}) collective-permute-start(f32[512,128]{1,0:T(8,128)S(1)} %fusion.2), channel_id=1, source_target_pairs={{0,12},{4,8},{8,4},{12,0},{1,13},{5,9},{9,5},{13,1},{2,14},{6,10},... | collective-permute-start | bytes 786440 | tf_op jit(solution)/shard_map/ppermute | solution.py:218
  88.8 24.5 %collective-permute-start.8 = (f32[512,128]{1,0:T(8,128)S(1)}, f32[512,128]{1,0:T(8,128)S(1)}, u32[]{:S(2)}, u32[]{:S(2)}) collective-permute-start(f32[512,128]{1,0:T(8,128)S(1)} %fusion.2), channel_id=1, source_target_pairs={{0,2},{1,3},{2,0},{3,1},{4,6},{5,7},{6,4},{7,5},{8,10},{9,11},{10,... | collective-permute-start | bytes 786440 | tf_op jit(solution)/shard_map/ppermute | solution.py:218
  97.6 15.8 %collective-permute-start.9 = (f32[512,128]{1,0:T(8,128)S(1)}, f32[512,128]{1,0:T(8,128)S(1)}, u32[]{:S(2)}, u32[]{:S(2)}) collective-permute-start(f32[512,128]{1,0:T(8,128)S(1)} %collective-permute-done.5), channel_id=1, source_target_pairs={{0,2},{1,3},{2,0},{3,1},{4,6},{5,7},{6,4},{7,5},{8,10},{9,11},{10,... | collective-permute-start | bytes 786440 | tf_op jit(solution)/shard_map/ppermute | solution.py:218
  111.7 10.3 %collective-permute-start.12 = (f32[2048,128]{1,0:T(8,128)S(1)}, f32[2048,128]{1,0:T(8,128)S(1)}, u32[]{:S(2)}, u32[]{:S(2)}) collective-permute-start(f32[2048,128]{1,0:T(8,128)S(1)} %pad_maximum_fusion.refs_6_), channel_id=1, source_target_pairs={{0,1},{1,0},{2,3},{3,2},{4,5},{5,4},{6,7},{7,6},{8,9},{9,8},{10,11... | collective-permute-start | bytes 3145736 | tf_op jit(solution)/shard_map/ppermute | solution.py:218
  131.9 14.2 %collective-permute-start.14 = (f32[1024,128]{1,0:T(8,128)}, f32[1024,128]{1,0:T(8,128)S(1)}, u32[]{:S(2)}, u32[]{:S(2)}) collective-permute-start(f32[1024,128]{1,0:T(8,128)} %shard_map.150.refs_6_), channel_id=1, source_target_pairs={{0,16},{16,0},{1,17},{17,1},{2,18},{18,2},{3,19},{19,3},{4,20},{20... | collective-permute-start | bytes 1572872 | tf_op jit(solution)/shard_map/ppermute | solution.py:218
  152.2 13.8 %collective-permute-start.15 = (f32[2048,128]{1,0:T(8,128)}, f32[2048,128]{1,0:T(8,128)S(1)}, u32[]{:S(2)}, u32[]{:S(2)}) collective-permute-start(f32[2048,128]{1,0:T(8,128)} %shard_map.154), channel_id=1, source_target_pairs={{0,1},{1,0},{2,3},{3,2},{4,5},{5,4},{6,7},{7,6},{8,9},{9,8},{10,11... | collective-permute-start | bytes 3145736 | tf_op jit(solution)/shard_map/ppermute | solution.py:218
  167.0 13.7 %collective-permute-start.16 = (f32[672,128]{1,0:T(8,128)S(1)}, f32[672,128]{1,0:T(8,128)S(1)}, u32[]{:S(2)}, u32[]{:S(2)}) collective-permute-start(f32[672,128]{1,0:T(8,128)S(1)} %bitcast.224), channel_id=1, source_target_pairs={{0,2},{1,3},{2,0},{3,1},{4,6},{5,7},{6,4},{7,5},{8,10},{9,11},{10,... | collective-permute-start | bytes 1032200 | tf_op jit(solution)/shard_map/ppermute | solution.py:218
  169.6 9.2 %collective-permute-start.22 = (f32[176,128]{1,0:T(8,128)S(1)}, f32[176,128]{1,0:T(8,128)S(1)}, u32[]{:S(2)}, u32[]{:S(2)}) collective-permute-start(f32[176,128]{1,0:T(8,128)S(1)} %bitcast.234), channel_id=1, source_target_pairs={{0,12},{4,8},{8,4},{12,0},{1,13},{5,9},{9,5},{13,1},{2,14},{6,10},... | collective-permute-start | bytes 270344 | tf_op jit(solution)/shard_map/ppermute | solution.py:218
  195.3 11.5 %collective-permute-start.26 = (f32[256,128]{1,0:T(8,128)S(1)}, f32[256,128]{1,0:T(8,128)S(1)}, u32[]{:S(2)}, u32[]{:S(2)}) collective-permute-start(f32[256,128]{1,0:T(8,128)S(1)} %maximum_subtract_fusion), channel_id=1, source_target_pairs={{0,12},{4,8},{8,4},{12,0},{1,13},{5,9},{9,5},{13,1},{2,14},{6,10},... | collective-permute-start | bytes 393224 | tf_op jit(solution)/shard_map/ppermute | solution.py:218
  196.8 11.0 %collective-permute-start.25 = (f32[256,128]{1,0:T(8,128)S(1)}, f32[256,128]{1,0:T(8,128)S(1)}, u32[]{:S(2)}, u32[]{:S(2)}) collective-permute-start(f32[256,128]{1,0:T(8,128)S(1)} %maximum_subtract_fusion), channel_id=1, source_target_pairs={{0,8},{4,12},{8,0},{12,4},{1,9},{5,13},{9,1},{13,5},{2,10},{6,14},... | collective-permute-start | bytes 393224 | tf_op jit(solution)/shard_map/ppermute | solution.py:218
  198.3 11.8 %collective-permute-start.27 = (f32[256,128]{1,0:T(8,128)S(1)}, f32[256,128]{1,0:T(8,128)S(1)}, u32[]{:S(2)}, u32[]{:S(2)}) collective-permute-start(f32[256,128]{1,0:T(8,128)S(1)} %maximum_subtract_fusion), channel_id=1, source_target_pairs={{0,2},{1,3},{2,0},{3,1},{4,6},{5,7},{6,4},{7,5},{8,10},{9,11},{10,... | collective-permute-start | bytes 393224 | tf_op jit(solution)/shard_map/ppermute | solution.py:218
  199.8 10.3 %collective-permute-start.28 = (f32[256,128]{1,0:T(8,128)S(1)}, f32[256,128]{1,0:T(8,128)S(1)}, u32[]{:S(2)}, u32[]{:S(2)}) collective-permute-start(f32[256,128]{1,0:T(8,128)S(1)} %collective-permute-done.24), channel_id=1, source_target_pairs={{0,2},{1,3},{2,0},{3,1},{4,6},{5,7},{6,4},{7,5},{8,10},{9,11},{10,... | collective-permute-start | bytes 393224 | tf_op jit(solution)/shard_map/ppermute | solution.py:218
  207.9 10.2 %collective-permute-start.31 = (f32[1024,128]{1,0:T(8,128)S(1)}, f32[1024,128]{1,0:T(8,128)S(1)}, u32[]{:S(2)}, u32[]{:S(2)}) collective-permute-start(f32[1024,128]{1,0:T(8,128)S(1)} %pad_maximum_fusion.1.refs_6_), channel_id=1, source_target_pairs={{0,1},{1,0},{2,3},{3,2},{4,5},{5,4},{6,7},{7,6},{8,9},{9,8},{10,11... | collective-permute-start | bytes 1572872 | tf_op jit(solution)/shard_map/ppermute | solution.py:218
  242.9 10.5 %collective-permute-start.35 = (f32[672,128]{1,0:T(8,128)S(1)}, f32[672,128]{1,0:T(8,128)S(1)}, u32[]{:S(2)}, u32[]{:S(2)}) collective-permute-start(f32[672,128]{1,0:T(8,128)S(1)} %bitcast.225), channel_id=1, source_target_pairs={{0,2},{1,3},{2,0},{3,1},{4,6},{5,7},{6,4},{7,5},{8,10},{9,11},{10,... | collective-permute-start | bytes 1032200 | tf_op jit(solution)/shard_map/ppermute | solution.py:218
  245.5 13.7 %collective-permute-start.41 = (f32[176,128]{1,0:T(8,128)S(1)}, f32[176,128]{1,0:T(8,128)S(1)}, u32[]{:S(2)}, u32[]{:S(2)}) collective-permute-start(f32[176,128]{1,0:T(8,128)S(1)} %bitcast.232), channel_id=1, source_target_pairs={{0,12},{4,8},{8,4},{12,0},{1,13},{5,9},{9,5},{13,1},{2,14},{6,10},... | collective-permute-start | bytes 270344 | tf_op jit(solution)/shard_map/ppermute | solution.py:218
  246.2 13.2 %collective-permute-start.40 = (f32[176,128]{1,0:T(8,128)S(1)}, f32[176,128]{1,0:T(8,128)S(1)}, u32[]{:S(2)}, u32[]{:S(2)}) collective-permute-start(f32[176,128]{1,0:T(8,128)S(1)} %bitcast.230), channel_id=1, source_target_pairs={{0,8},{4,12},{8,0},{12,4},{1,9},{5,13},{9,1},{13,5},{2,10},{6,14},... | collective-permute-start | bytes 270344 | tf_op jit(solution)/shard_map/ppermute | solution.py:218
  250.2 9.2 %collective-permute-start.39 = (f32[176,128]{1,0:T(8,128)S(1)}, f32[176,128]{1,0:T(8,128)S(1)}, u32[]{:S(2)}, u32[]{:S(2)}) collective-permute-start(f32[176,128]{1,0:T(8,128)S(1)} %bitcast.229), channel_id=1, source_target_pairs={{0,4},{4,0},{8,12},{12,8},{1,5},{5,1},{9,13},{13,9},{2,6},{6,2},{1... | collective-permute-start | bytes 270344 | tf_op jit(solution)/shard_map/ppermute | solution.py:218
  268.3 10.7 %collective-permute-start.44 = (f32[256,128]{1,0:T(8,128)S(1)}, f32[256,128]{1,0:T(8,128)S(1)}, u32[]{:S(2)}, u32[]{:S(2)}) collective-permute-start(f32[256,128]{1,0:T(8,128)S(1)} %pad_maximum_fusion.3), channel_id=1, source_target_pairs={{0,8},{4,12},{8,0},{12,4},{1,9},{5,13},{9,1},{13,5},{2,10},{6,14},... | collective-permute-start | bytes 393224 | tf_op jit(solution)/shard_map/ppermute | solution.py:218
  269.5 12.4 %collective-permute-start.45 = (f32[256,128]{1,0:T(8,128)S(1)}, f32[256,128]{1,0:T(8,128)S(1)}, u32[]{:S(2)}, u32[]{:S(2)}) collective-permute-start(f32[256,128]{1,0:T(8,128)S(1)} %pad_maximum_fusion.3), channel_id=1, source_target_pairs={{0,12},{4,8},{8,4},{12,0},{1,13},{5,9},{9,5},{13,1},{2,14},{6,10},... | collective-permute-start | bytes 393224 | tf_op jit(solution)/shard_map/ppermute | solution.py:218
  270.6 13.5 %collective-permute-start.46 = (f32[256,128]{1,0:T(8,128)S(1)}, f32[256,128]{1,0:T(8,128)S(1)}, u32[]{:S(2)}, u32[]{:S(2)}) collective-permute-start(f32[256,128]{1,0:T(8,128)S(1)} %pad_maximum_fusion.3), channel_id=1, source_target_pairs={{0,2},{1,3},{2,0},{3,1},{4,6},{5,7},{6,4},{7,5},{8,10},{9,11},{10,... | collective-permute-start | bytes 393224 | tf_op jit(solution)/shard_map/ppermute | solution.py:218
  273.2 10.9 %collective-permute-start.47 = (f32[256,128]{1,0:T(8,128)S(1)}, f32[256,128]{1,0:T(8,128)S(1)}, u32[]{:S(2)}, u32[]{:S(2)}) collective-permute-start(f32[256,128]{1,0:T(8,128)S(1)} %collective-permute-done.43), channel_id=1, source_target_pairs={{0,2},{1,3},{2,0},{3,1},{4,6},{5,7},{6,4},{7,5},{8,10},{9,11},{10,... | collective-permute-start | bytes 393224 | tf_op jit(solution)/shard_map/ppermute | solution.py:218
  301.6 14.2 %collective-permute-start.52 = (f32[1024,128]{1,0:T(8,128)}, f32[1024,128]{1,0:T(8,128)S(1)}, u32[]{:S(2)}, u32[]{:S(2)}) collective-permute-start(f32[1024,128]{1,0:T(8,128)} %get-tuple-element.8.refs_8_), channel_id=1, source_target_pairs={{0,16},{16,0},{1,17},{17,1},{2,18},{18,2},{3,19},{19,3},{4,20},{20... | collective-permute-start | bytes 1572872 | tf_op jit(solution)/shard_map/ppermute | solution.py:218
  331.8 18.3 %collective-permute-start.54 = (f32[1376,128]{1,0:T(8,128)S(1)}, f32[1376,128]{1,0:T(8,128)S(1)}, u32[]{:S(2)}, u32[]{:S(2)}) collective-permute-start(f32[1376,128]{1,0:T(8,128)S(1)} %bitcast.223), channel_id=1, source_target_pairs={{0,2},{1,3},{2,0},{3,1},{4,6},{5,7},{6,4},{7,5},{8,10},{9,11},{10,... | collective-permute-start | bytes 2113544 | tf_op jit(solution)/shard_map/ppermute | solution.py:218
  333.4 19.3 %collective-permute-start.60 = (f32[336,128]{1,0:T(8,128)S(1)}, f32[336,128]{1,0:T(8,128)S(1)}, u32[]{:S(2)}, u32[]{:S(2)}) collective-permute-start(f32[336,128]{1,0:T(8,128)S(1)} %bitcast.228), channel_id=1, source_target_pairs={{0,12},{4,8},{8,4},{12,0},{1,13},{5,9},{9,5},{13,1},{2,14},{6,10},... | collective-permute-start | bytes 516104 | tf_op jit(solution)/shard_map/ppermute | solution.py:218
  335.0 18.7 %collective-permute-start.59 = (f32[336,128]{1,0:T(8,128)S(1)}, f32[336,128]{1,0:T(8,128)S(1)}, u32[]{:S(2)}, u32[]{:S(2)}) collective-permute-start(f32[336,128]{1,0:T(8,128)S(1)} %bitcast.227), channel_id=1, source_target_pairs={{0,8},{4,12},{8,0},{12,4},{1,9},{5,13},{9,1},{13,5},{2,10},{6,14},... | collective-permute-start | bytes 516104 | tf_op jit(solution)/shard_map/ppermute | solution.py:218
  335.9 17.8 %collective-permute-start.58 = (f32[336,128]{1,0:T(8,128)S(1)}, f32[336,128]{1,0:T(8,128)S(1)}, u32[]{:S(2)}, u32[]{:S(2)}) collective-permute-start(f32[336,128]{1,0:T(8,128)S(1)} %bitcast.226), channel_id=1, source_target_pairs={{0,4},{4,0},{8,12},{12,8},{1,5},{5,1},{9,13},{13,9},{2,6},{6,2},{1... | collective-permute-start | bytes 516104 | tf_op jit(solution)/shard_map/ppermute | solution.py:218
  350.1 14.2 %collective-permute-start.57 = (f32[344,128]{1,0:T(8,128)S(1)}, f32[344,128]{1,0:T(8,128)S(1)}, u32[]{:S(2)}, u32[]{:S(2)}) collective-permute-start(f32[344,128]{1,0:T(8,128)S(1)} %get-tuple-element.23), channel_id=1, source_target_pairs={{0,12},{4,8},{8,4},{12,0},{1,13},{5,9},{9,5},{13,1},{2,14},{6,10},... | collective-permute-start | bytes 528392 | tf_op jit(solution)/shard_map/ppermute | solution.py:218
  351.7 14.9 %collective-permute-start.56 = (f32[344,128]{1,0:T(8,128)S(1)}, f32[344,128]{1,0:T(8,128)S(1)}, u32[]{:S(2)}, u32[]{:S(2)}) collective-permute-start(f32[344,128]{1,0:T(8,128)S(1)} %get-tuple-element.24), channel_id=1, source_target_pairs={{0,8},{4,12},{8,0},{12,4},{1,9},{5,13},{9,1},{13,5},{2,10},{6,14},... | collective-permute-start | bytes 528392 | tf_op jit(solution)/shard_map/ppermute | solution.py:218
  352.6 14.0 %collective-permute-start.55 = (f32[344,128]{1,0:T(8,128)S(1)}, f32[344,128]{1,0:T(8,128)S(1)}, u32[]{:S(2)}, u32[]{:S(2)}) collective-permute-start(f32[344,128]{1,0:T(8,128)S(1)} %get-tuple-element.22), channel_id=1, source_target_pairs={{0,4},{4,0},{8,12},{12,8},{1,5},{5,1},{9,13},{13,9},{2,6},{6,2},{1... | collective-permute-start | bytes 528392 | tf_op jit(solution)/shard_map/ppermute | solution.py:218
  353.7 13.0 %collective-permute-start.61 = (f32[168,128]{1,0:T(8,128)S(1)}, f32[168,128]{1,0:T(8,128)S(1)}, u32[]{:S(2)}, u32[]{:S(2)}) collective-permute-start(f32[168,128]{1,0:T(8,128)S(1)} %slice_add_fusion.21), channel_id=1, source_target_pairs={{0,2},{1,3},{2,0},{3,1},{4,6},{5,7},{6,4},{7,5},{8,10},{9,11},{10,... | collective-permute-start | bytes 258056 | tf_op jit(solution)/shard_map/ppermute | solution.py:218
  366.8 12.8 %collective-permute-start.62 = (f32[512,128]{1,0:T(8,128)S(1)}, f32[512,128]{1,0:T(8,128)S(1)}, u32[]{:S(2)}, u32[]{:S(2)}) collective-permute-start(f32[512,128]{1,0:T(8,128)S(1)} %pad_maximum_fusion.2), channel_id=1, source_target_pairs={{0,4},{4,0},{8,12},{12,8},{1,5},{5,1},{9,13},{13,9},{2,6},{6,2},{1... | collective-permute-start | bytes 786440 | tf_op jit(solution)/shard_map/ppermute | solution.py:218
  369.3 19.0 %collective-permute-start.63 = (f32[512,128]{1,0:T(8,128)S(1)}, f32[512,128]{1,0:T(8,128)S(1)}, u32[]{:S(2)}, u32[]{:S(2)}) collective-permute-start(f32[512,128]{1,0:T(8,128)S(1)} %pad_maximum_fusion.2), channel_id=1, source_target_pairs={{0,8},{4,12},{8,0},{12,4},{1,9},{5,13},{9,1},{13,5},{2,10},{6,14},... | collective-permute-start | bytes 786440 | tf_op jit(solution)/shard_map/ppermute | solution.py:218
  370.3 23.6 %collective-permute-start.64 = (f32[512,128]{1,0:T(8,128)S(1)}, f32[512,128]{1,0:T(8,128)S(1)}, u32[]{:S(2)}, u32[]{:S(2)}) collective-permute-start(f32[512,128]{1,0:T(8,128)S(1)} %pad_maximum_fusion.2), channel_id=1, source_target_pairs={{0,12},{4,8},{8,4},{12,0},{1,13},{5,9},{9,5},{13,1},{2,14},{6,10},... | collective-permute-start | bytes 786440 | tf_op jit(solution)/shard_map/ppermute | solution.py:218
  393.9 13.6 %collective-permute-start.65 = (f32[2048,128]{1,0:T(8,128)S(1)}, f32[2048,128]{1,0:T(8,128)S(1)}, u32[]{:S(2)}, u32[]{:S(2)}) collective-permute-start(f32[2048,128]{1,0:T(8,128)S(1)} %constant_dynamic-update-slice_fusion.17.refs_6_), channel_id=1, source_target_pairs={{0,1},{1,0},{2,3},{3,2},{4,5},{5,4},{6,7},{7,6},{8,9},{9,8},{10,11... | collective-permute-start | bytes 3145736 | tf_op jit(solution)/shard_map/ppermute | solution.py:218
  422.3 25.6 %collective-permute-start.66 = (f32[2048,128]{1,0:T(8,128)}, f32[2048,128]{1,0:T(8,128)S(1)}, u32[]{:S(2)}, u32[]{:S(2)}) collective-permute-start(f32[2048,128]{1,0:T(8,128)} %get-tuple-element.10), channel_id=1, source_target_pairs={{0,16},{16,0},{1,17},{17,1},{2,18},{18,2},{3,19},{19,3},{4,20},{20... | collective-permute-start | bytes 3145736 | tf_op jit(solution)/shard_map/ppermute | solution.py:218
  423.7 79.1 %collective-permute-start.73 = (f32[4096,128]{1,0:T(8,128)}, f32[4096,128]{1,0:T(8,128)}, u32[]{:S(2)}, u32[]{:S(2)}) collective-permute-start(f32[4096,128]{1,0:T(8,128)} %get-tuple-element.11), channel_id=1, source_target_pairs={{0,2},{1,3},{2,0},{3,1},{4,6},{5,7},{6,4},{7,5},{8,10},{9,11},{10,... | collective-permute-start | bytes 6291464 | tf_op jit(solution)/shard_map/ppermute | solution.py:218
  455.0 33.4 %collective-permute-start.69 = (f32[1024,128]{1,0:T(8,128)}, f32[1024,128]{1,0:T(8,128)S(1)}, u32[]{:S(2)}, u32[]{:S(2)}) collective-permute-start(f32[1024,128]{1,0:T(8,128)} %shard_map.166), channel_id=1, source_target_pairs={{0,12},{4,8},{8,4},{12,0},{1,13},{5,9},{9,5},{13,1},{2,14},{6,10},... | collective-permute-start | bytes 1572872 | tf_op jit(solution)/shard_map/ppermute | solution.py:218
  461.2 37.5 %collective-permute-start.68 = (f32[1024,128]{1,0:T(8,128)}, f32[1024,128]{1,0:T(8,128)S(1)}, u32[]{:S(2)}, u32[]{:S(2)}) collective-permute-start(f32[1024,128]{1,0:T(8,128)} %shard_map.165), channel_id=1, source_target_pairs={{0,8},{4,12},{8,0},{12,4},{1,9},{5,13},{9,1},{13,5},{2,10},{6,14},... | collective-permute-start | bytes 1572872 | tf_op jit(solution)/shard_map/ppermute | solution.py:218
  466.1 32.6 %collective-permute-start.67 = (f32[1024,128]{1,0:T(8,128)}, f32[1024,128]{1,0:T(8,128)S(1)}, u32[]{:S(2)}, u32[]{:S(2)}) collective-permute-start(f32[1024,128]{1,0:T(8,128)} %shard_map.164), channel_id=1, source_target_pairs={{0,4},{4,0},{8,12},{12,8},{1,5},{5,1},{9,13},{13,9},{2,6},{6,2},{1... | collective-permute-start | bytes 1572872 | tf_op jit(solution)/shard_map/ppermute | solution.py:218
  499.0 24.4 %collective-permute-start.70 = (f32[1024,128]{1,0:T(8,128)S(1)}, f32[1024,128]{1,0:T(8,128)S(1)}, u32[]{:S(2)}, u32[]{:S(2)}) collective-permute-start(f32[1024,128]{1,0:T(8,128)S(1)} %get-tuple-element.13), channel_id=1, source_target_pairs={{0,4},{4,0},{8,12},{12,8},{1,5},{5,1},{9,13},{13,9},{2,6},{6,2},{1... | collective-permute-start | bytes 1572872 | tf_op jit(solution)/shard_map/ppermute | solution.py:218
  501.3 35.9 %collective-permute-start.71 = (f32[1024,128]{1,0:T(8,128)S(1)}, f32[1024,128]{1,0:T(8,128)S(1)}, u32[]{:S(2)}, u32[]{:S(2)}) collective-permute-start(f32[1024,128]{1,0:T(8,128)S(1)} %get-tuple-element.13), channel_id=1, source_target_pairs={{0,8},{4,12},{8,0},{12,4},{1,9},{5,13},{9,1},{13,5},{2,10},{6,14},... | collective-permute-start | bytes 1572872 | tf_op jit(solution)/shard_map/ppermute | solution.py:218
  502.4 46.1 %collective-permute-start.72 = (f32[1024,128]{1,0:T(8,128)S(1)}, f32[1024,128]{1,0:T(8,128)S(1)}, u32[]{:S(2)}, u32[]{:S(2)}) collective-permute-start(f32[1024,128]{1,0:T(8,128)S(1)} %get-tuple-element.13), channel_id=1, source_target_pairs={{0,12},{4,8},{8,4},{12,0},{1,13},{5,9},{9,5},{13,1},{2,14},{6,10},... | collective-permute-start | bytes 1572872 | tf_op jit(solution)/shard_map/ppermute | solution.py:218
  (56 other events, 428.2 us)

commit v3 on v2

--- a/solution.py
+++ b/solution.py
@@ -14,8 +14,9 @@
 def product_kernel(cfg, *refs):
     refs = list(refs)
     tile_p, tile_r, dst, offs, pattern = refs[:5]
-    matrix = refs[5]
-    at = 6
+    streams = cfg["streams"]
+    matrices = refs[5 : 5 + streams]
+    at = 5 + streams
     terms = refs[at : at + len(cfg["signs"])]
     at += len(cfg["signs"])
     pieces = refs[at : at + cfg["pieces"]]
@@ -58,8 +59,8 @@
                     else:
                         value = value + part if sign > 0 else value - part
             if transposed:
-                which, column = base // depth, base % depth
-                vector[pl.ds(which * 128, 128), pl.ds(column, chunk)] = value.T.astype(HALF)
+                slot, column = base // depth, base % depth
+                vector[pl.ds(slot * 128, 128), pl.ds(column, chunk)] = value.T.astype(HALF)
             else:
                 vector[pl.ds(base, chunk), :] = value.astype(HALF)
 
@@ -67,7 +68,9 @@
     blocks_r, blocks_c, other = cfg["blocks_r"], cfg["blocks_c"], cfg["other"]
     for sub in range(tile // block):
         result = None
-        for lead in range(matrix.shape[0]):
+        for lead, which in [(p, n) for p in range(matrices[0].shape[0]) for n in range(streams)]:
+            matrix = matrices[which]
+            share = depth // streams
             index = lead if cfg["sum_p"] else tile_p[step]
             start = 0
             if vectors > 1:
@@ -76,22 +79,26 @@
                 if not cfg["sum_p"]:
                     start = pl.multiple_of(start, stride)
             if transposed:
-                x = vector[pl.ds(start, 128), :]
+                x = vector[pl.ds(start, 128), pl.ds(which * share, share)]
                 a = matrix[lead, :, pl.ds(sub * block, block)]
             else:
-                x = vector[pl.ds(start, depth), :]
+                start = start + which * share
+                if vectors > 1 and not cfg["sum_p"]:
+                    start = pl.multiple_of(start, share)
+                x = vector[pl.ds(start, share), :]
                 a = matrix[lead, pl.ds(sub * block, block), :]
             if cfg["masked"]:
                 here = (tile_r[step] * tile + sub * block) // cfg["pattern_block"]
                 kept = []
-                for n in range(depth // other):
+                for n in range(share // other):
+                    across = which * (share // other) + n
                     if transposed:
-                        flag = pattern[(index * blocks_r + n) * blocks_c + here]
+                        flag = pattern[(index * blocks_r + across) * blocks_c + here]
                         part = x[:, n * other : (n + 1) * other]
                     else:
-                        flag = pattern[(index * blocks_r + here) * blocks_c + n]
+                        flag = pattern[(index * blocks_r + here) * blocks_c + across]
                         part = x[n * other : (n + 1) * other, :]
-                    kept.append((part.astype(FULL) * flag.astype(FULL)).astype(HALF))
+                    kept.append(jnp.where(flag != 0, part, jnp.zeros_like(part)))
                 if len(kept) > 1:
                     x = jnp.concatenate(kept, axis=1 if transposed else 0)
                 else:
@@ -154,6 +161,8 @@
         offs = jnp.zeros((8,), jnp.int32)
     if tile_p is None:
         tile_p = jnp.zeros((tiles,), jnp.int32)
+    least = other if masked else 128
+    streams = max([1] + [n for n in (2, 4) if depth % (n * least) == 0])
     signs = tuple(sign for _, sign in terms)
     term_arrays = [array for array, _ in terms]
     x_rows = vectors * depth
@@ -161,15 +170,16 @@
         transposed=transposed, depth=depth, vectors=vectors, signs=signs, pieces=len(pieces),
         piece=piece, addend=addend is not None, ordered=ordered, tile=tile, granule=granule,
         block=block, other=other, pattern_block=pattern_block, blocks_r=blocks_r,
-        blocks_c=blocks_c, masked=masked, sum_p=sum_p,
+        blocks_c=blocks_c, masked=masked, sum_p=sum_p, streams=streams,
     )
     held = lead if sum_p else 1
+    share = depth // streams
     if transposed:
-        matrix_block = (held, depth, tile)
-        matrix_map = lambda t, tp, tr, *_: (tp[t], 0, tr[t])
+        matrix_block = (held, share, tile)
+        maps = [lambda t, tp, tr, *_, s=s: (tp[t], s, tr[t]) for s in range(streams)]
     else:
-        matrix_block = (held, tile, depth)
-        matrix_map = lambda t, tp, tr, *_: (tp[t], tr[t], 0)
+        matrix_block = (held, tile, share)
+        maps = [lambda t, tp, tr, *_, s=s: (tp[t], tr[t], s) for s in range(streams)]
 
     def whole(array):
         return pl.BlockSpec(array.shape, lambda t, *_: (0, 0), pipeline_mode=pl.Buffered(1))
@@ -191,7 +201,7 @@
         grid_spec=pltpu.PrefetchScalarGridSpec(
             num_scalar_prefetch=5,
             grid=(tiles,),
-            in_specs=[pl.BlockSpec(matrix_block, matrix_map)] + [whole(a) for a in inputs],
+            in_specs=[pl.BlockSpec(matrix_block, m) for m in maps] + [whole(a) for a in inputs],
             out_specs=out_specs,
             scratch_shapes=[pltpu.VMEM(scratch, HALF)],
         ),
@@ -202,8 +212,22 @@
             bytes_accessed=tiles * matrix_bytes + resident + written,
             transcendentals=0,
         ),
-    )(tile_p, tile_r, dst, offs, flags, matrix, *inputs)
+    )(tile_p, tile_r, dst, offs, flags, *[matrix] * streams, *inputs)
     return tuple(result) if ordered else result[0]
+
+
+def tie_kernel(*refs):
+    pass
+
+
+def tie(value, *others):
+    return pl.pallas_call(
+        tie_kernel,
+        in_specs=[pl.BlockSpec(memory_space=pl.ANY)] * (1 + len(others)),
+        out_specs=pl.BlockSpec(memory_space=pl.ANY),
+        out_shape=jax.ShapeDtypeStruct(value.shape, value.dtype),
+        input_output_aliases={0: 0},
+    )(value, *others)
 
 
 def ints(values):
@@ -361,19 +385,6 @@
         own_rhs = lax.dynamic_slice(
             rhs_mid, (owner, parity * split + col * cut_mid, 0), (1, cut_mid, 128)
         )[0]
-        blocks = col_collect(own_rhs - to_mid)
-        across = jnp.concatenate([send(b, "leaf", 2) for b in blocks])
-        near = jnp.concatenate(blocks)
-        mid_pieces = [near, across, send(near, "leaf", 1), send(across, "leaf", 1)]
-        mid_offs = ints(
-            [
-                (owner ^ j) * full + (parity ^ i) * split + (col ^ k) * cut_mid
-                for i in range(2)
-                for j in range(2)
-                for k in range(cols)
-            ]
-        )
-
         def make_leaf_root(i):
             tile = fit(split, 512)
             granule = min(cut_root, unit)
@@ -389,6 +400,19 @@
 
         leaf_root_parts = [make_leaf_root(0), make_leaf_root(1)]
 
+        blocks = col_collect(tie(own_rhs - to_mid, *leaf_root_parts))
+        across = jnp.concatenate([send(b, "leaf", 2) for b in blocks])
+        near = jnp.concatenate(blocks)
+        mid_pieces = [near, across, send(near, "leaf", 1), send(across, "leaf", 1)]
+        mid_offs = ints(
+            [
+                (owner ^ j) * full + (parity ^ i) * split + (col ^ k) * cut_mid
+                for i in range(2)
+                for j in range(2)
+                for k in range(cols)
+            ]
+        )
+
         tile = fit(own, 256)
         mid_part = product(
             inverse_mid,
@@ -403,7 +427,7 @@
         forward_mid = row_terms(mid_part)
 
         def make_root(i):
-            tile = fit(split, 1024)
+            tile = fit(split, 512)
             granule = min(cut_root, unit)
             return product(
                 factor_mid_root,
@@ -481,7 +505,6 @@
 
         here, arrived = pair_sum(make_back_mid)
         mid_piece = plane_reduce(here, arrived, cut_mid)
-        near = jnp.concatenate(col_collect(mid_piece))
         tile = fit(factor_leaf_root.shape[2], 256)
         leaf_tiles = tiles(factor_leaf_root.shape[2] // tile)
         back_part = product(
@@ -492,6 +515,7 @@
             tile_r=leaf_tiles,
             tile=tile,
         )
+        near = jnp.concatenate(col_collect(tie(mid_piece, back_part)))
         back_part, mid_own = product(
             factor_leaf_mid,
             transposed=True,

time: 551 us -> 539 us (0.978)
  waiting for transfers between devices: 272 us -> 245 us
  Pallas kernels: 143 us -> 149 us
    ppermute x74, waiting for transfers between devices: 272 us -> 245 us  [send(): return lax.ppermute(value, axis, [(i, i ^ bit) for i in range(size)])]
    pallas_call x20, Pallas kernels: 143 us -> 149 us  [product(): pl.pallas_call(functools.partial(product_kernel, cfg), grid_spec=pltpu.Pr...]
  transfers between devices with their start and end apart: 74 -> 74, of which waited for: 41 -> 41; matrix products, arithmetic and copies ran while one was open for 5% -> 6% of each run, Pallas kernels for 13% -> 14%
where the time goes in v3:
time: 539 us; the launch traced here: 537 us
  waiting for transfers between devices  245 us (45%)
  Pallas kernels  149 us (28%)
  starting transfers between devices  90.6 us (17%)
  other arithmetic  33.6 us (6%)
  local copies, waits for them, and re-layouts  17.8 us (3%)
    ppermute x74, waiting for transfers between devices, send(): return lax.ppermute(value, axis, [(i, i ^ bit) for i in range(size)])  245 us
    pallas_call x20, Pallas kernels, product(): pl.pallas_call(functools.partial(product_kernel, cfg), grid_spec=pltpu.Pr...  149 us
    ppermute x74, starting transfers between devices, send(): return lax.ppermute(value, axis, [(i, i ^ bit) for i in range(size)])  90.6 us
  transfers between devices with their start and end apart: 74, of which 41 were waited for; matrix products, arithmetic and copies ran while one was open for 6% of the time, Pallas kernels for 14%

profile of v3, /device:TPU:8, one launch (start us, length us, event | category | flops | bytes accessed | tf_op | source)
XLA Modules:
  0.0 536.9 jit_solution(3732897085513505659)
XLA Ops:
  2.3 13.0 %shard_map.147.refs_9_ = f32[2048,128]{1,0:T(8,128)} custom-call(s32[8]{0:T(128)} %broadcast_11_refs_0__refs_3__refs_4_.2.refs_0_.refs_3_.refs_4_, s32[8]{0:T(128)} %iota.77.refs_1_, s32[8]{0:T(128)} %iota_multiply_fusion.1.refs_2_, s32[8]{0:T(128)} %broadcast_11_refs_0__refs_3__refs_4_.2.refs_0_.refs_3_.refs_4_, ...), custom_call_target="tpu_custom_call" | custom-call | flops 2147483648 | bytes 19922944 | tf_op jit(solution)/shard_map/pallas_call | solution.py:199
  18.7 21.6 %collective-permute-done.refs_10_ = f32[2048,128]{1,0:T(8,128)S(1)} collective-permute-done((f32[2048,128]{1,0:T(8,128)}, f32[2048,128]{1,0:T(8,128)S(1)}, u32[]{:S(2)}, u32[]{:S(2)}) %collective-permute-start) | collective-permute-done | bytes 1048608 | tf_op jit(solution)/shard_map/ppermute | solution.py:242
  41.4 8.1 %shard_map.149 = f32[2048,128]{1,0:T(8,128)} custom-call(s32[4]{0:T(128)} %broadcast_9_refs_0_.2.refs_0_, s32[4]{0:T(128)} %iota_add_fusion.4.refs_1_, s32[8]{0:T(128)} %stack.387.refs_2_, s32[8]{0:T(128)} %broadcast_11_refs_0__refs_3__refs_4_.2.refs_0_.refs_3_.refs_4_, s32[128]{0:T(128)} %reshape.118.refs_4_, bf16[1,4096,2048]{2,1,0:T(8,128)(2,1)} %refs_8_.25, ...), custom_call_target="tpu_custom_call" | custom-call | flops 1073741824 | bytes 11534336 | tf_op jit(solution)/shard_map/pallas_call | solution.py:199
  50.0 8.1 %shard_map.148 = f32[2048,128]{1,0:T(8,128)} custom-call(s32[4]{0:T(128)} %broadcast_9_refs_0_.2.refs_0_, s32[4]{0:T(128)} %iota_add_fusion.5.refs_1_, s32[8]{0:T(128)} %stack.387.refs_2_, s32[8]{0:T(128)} %broadcast_11_refs_0__refs_3__refs_4_.2.refs_0_.refs_3_.refs_4_, s32[128]{0:T(128)} %reshape.118.refs_4_, bf16[1,4096,2048]{2,1,0:T(8,128)(2,1)} %refs_8_.25, ...), custom_call_target="tpu_custom_call" | custom-call | flops 1073741824 | bytes 11534336 | tf_op jit(solution)/shard_map/pallas_call | solution.py:199
  65.0 8.1 %shard_map.150.refs_1_.refs_9_ = f32[2048,128]{1,0:T(8,128)} custom-call(s32[4]{0:T(128)} %broadcast_9_refs_0_.2.refs_0_, s32[4]{0:T(128)} %iota_add_fusion.5.refs_1_, s32[8]{0:T(128)} %stack.396.refs_2_, s32[8]{0:T(128)} %broadcast_11_refs_0__refs_3__refs_4_.2.refs_0_.refs_3_.refs_4_, s32[128]{0:T(128)} %reshape.119.refs_4_, ...), custom_call_target="tpu_custom_call" | custom-call | flops 1073741824 | bytes 11534336 | tf_op jit(solution)/shard_map/pallas_call | solution.py:199
  73.1 8.1 %shard_map.151.refs_2_.refs_9_ = f32[2048,128]{1,0:T(8,128)} custom-call(s32[4]{0:T(128)} %broadcast_9_refs_0_.2.refs_0_, s32[4]{0:T(128)} %iota_add_fusion.4.refs_1_, s32[8]{0:T(128)} %stack.396.refs_2_, s32[8]{0:T(128)} %broadcast_11_refs_0__refs_3__refs_4_.2.refs_0_.refs_3_.refs_4_, s32[128]{0:T(128)} %reshape.119.refs_4_, ...), custom_call_target="tpu_custom_call" | custom-call | flops 1073741824 | bytes 11534336 | tf_op jit(solution)/shard_map/pallas_call | solution.py:199
  91.4 7.6 %collective-permute-done.5 = f32[512,128]{1,0:T(8,128)S(1)} collective-permute-done((f32[512,128]{1,0:T(8,128)}, f32[512,128]{1,0:T(8,128)S(1)}, u32[]{:S(2)}, u32[]{:S(2)}) %collective-permute-start.5) | collective-permute-done | bytes 262176 | tf_op jit(solution)/shard_map/ppermute | solution.py:242
  100.4 7.2 %collective-permute-done.6 = f32[512,128]{1,0:T(8,128)S(1)} collective-permute-done((f32[512,128]{1,0:T(8,128)}, f32[512,128]{1,0:T(8,128)S(1)}, u32[]{:S(2)}, u32[]{:S(2)}) %collective-permute-start.6) | collective-permute-done | bytes 262176 | tf_op jit(solution)/shard_map/ppermute | solution.py:242
  109.1 3.8 collective-permute-done.7
  115.7 7.1 %collective-permute-done.11 = f32[512,128]{1,0:T(8,128)S(1)} collective-permute-done((f32[512,128]{1,0:T(8,128)S(1)}, f32[512,128]{1,0:T(8,128)S(1)}, u32[]{:S(2)}, u32[]{:S(2)}) %collective-permute-start.11) | collective-permute-done | bytes 262176 | tf_op jit(solution)/shard_map/ppermute | solution.py:242
  125.7 8.6 %shard_map.153.refs_7_.refs_9_ = f32[1024,128]{1,0:T(8,128)} custom-call(s32[4]{0:T(128)} %constant.62.clone.1.refs_0_, s32[4]{0:T(128)} %constant.65.clone.1.refs_1_, s32[4]{0:T(128)} %iota_multiply_fusion.2.refs_2_, s32[16]{0:T(128)} %stack.378.refs_3_, s32[8]{0:T(128)} %broadcast_11_refs_0__refs_3__refs_4_.2.refs_0_.refs_3_.refs_4_, ...), custom_call_target="tpu_custom_call" | custom-call | flops 1073741824 | bytes 13107200 | tf_op jit(solution)/shard_map/pallas_call | solution.py:199
  136.5 11.9 %collective-permute-done.14.refs_8_.refs_10_ = f32[1024,128]{1,0:T(8,128)S(1)} collective-permute-done((f32[1024,128]{1,0:T(8,128)}, f32[1024,128]{1,0:T(8,128)S(1)}, u32[]{:S(2)}, u32[]{:S(2)}) %collective-permute-start.14) | collective-permute-done | bytes 524320 | tf_op jit(solution)/shard_map/ppermute | solution.py:242
  149.2 6.3 %shard_map.155 = f32[2048,128]{1,0:T(8,128)} custom-call(s32[4]{0:T(128)} %broadcast_9_refs_0_.2.refs_0_, s32[4]{0:T(128)} %iota_add_fusion.4.refs_1_, s32[8]{0:T(128)} %stack.396.refs_2_, s32[8]{0:T(128)} %broadcast_11_refs_0__refs_3__refs_4_.2.refs_0_.refs_3_.refs_4_, s32[64]{0:T(128)} %reshape.120.refs_4_, bf16[2,4096,512]{2,1,0:T(8,128)(2,1)} %refs_8_.21, ...), custom_call_target="tpu_custom_call" | custom-call | flops 536870912 | bytes 7340032 | tf_op jit(solution)/shard_map/pallas_call | solution.py:199
  155.6 6.3 %shard_map.154 = f32[2048,128]{1,0:T(8,128)} custom-call(s32[4]{0:T(128)} %broadcast_9_refs_0_.2.refs_0_, s32[4]{0:T(128)} %iota_add_fusion.5.refs_1_, s32[8]{0:T(128)} %stack.396.refs_2_, s32[8]{0:T(128)} %broadcast_11_refs_0__refs_3__refs_4_.2.refs_0_.refs_3_.refs_4_, s32[64]{0:T(128)} %reshape.120.refs_4_, bf16[2,4096,512]{2,1,0:T(8,128)(2,1)} %refs_8_.21, ...), custom_call_target="tpu_custom_call" | custom-call | flops 536870912 | bytes 7340032 | tf_op jit(solution)/shard_map/pallas_call | solution.py:199
  169.0 4.8 collective-permute-done.22
  177.7 4.3 collective-permute-start.18
  182.8 4.1 collective-permute-done.18
  197.1 6.0 %collective-permute-done.26 = f32[256,128]{1,0:T(8,128)S(1)} collective-permute-done((f32[256,128]{1,0:T(8,128)S(1)}, f32[256,128]{1,0:T(8,128)S(1)}, u32[]{:S(2)}, u32[]{:S(2)}) %collective-permute-start.26) | collective-permute-done | bytes 131104 | tf_op jit(solution)/shard_map/ppermute | solution.py:242
  206.0 4.2 collective-permute-done.29
  215.7 5.4 shard_map.156.refs_9_
  223.1 6.5 %collective-permute-done.33.refs_10_ = f32[512,128]{1,0:T(8,128)S(1)} collective-permute-done((f32[512,128]{1,0:T(8,128)}, f32[512,128]{1,0:T(8,128)S(1)}, u32[]{:S(2)}, u32[]{:S(2)}) %collective-permute-start.33) | collective-permute-done | bytes 262176 | tf_op jit(solution)/shard_map/ppermute | solution.py:242
  230.3 4.4 shard_map.158
  235.2 4.6 shard_map.157
  244.1 4.2 collective-permute-start.40
  253.1 4.2 collective-permute-start.37
  272.8 4.1 collective-permute-done.44
  282.0 4.2 collective-permute-done.48
  291.5 8.1 %shard_map.159 = (f32[1024,128]{1,0:T(8,128)}, f32[4096,128]{1,0:T(8,128)}) custom-call(s32[4]{0:T(128)} %constant.62.clone.1.refs_0_, s32[4]{0:T(128)} %constant.65.clone.1.refs_1_, s32[4]{0:T(128)} %iota_multiply_fusion.2.refs_2_, s32[16]{0:T(128)} %stack.413.refs_3_, s32[64]{0:T(128)} %reshape.120.refs_4_, bf16[2,4096,512]{2,1,0:T(8,128)(2,1)} %refs_8_.21, ...), custom_call_target="tpu_custom_call" | custom-call | flops 1073741824 | bytes 13107200 | tf_op jit(solution)/shard_map/pallas_call | solution.py:199
  302.4 11.4 %collective-permute-done.52.refs_12_ = f32[1024,128]{1,0:T(8,128)S(1)} collective-permute-done((f32[1024,128]{1,0:T(8,128)}, f32[1024,128]{1,0:T(8,128)S(1)}, u32[]{:S(2)}, u32[]{:S(2)}) %collective-permute-start.52) | collective-permute-done | bytes 524320 | tf_op jit(solution)/shard_map/ppermute | solution.py:242
  314.6 7.1 %shard_map.161 = f32[4096,128]{1,0:T(8,128)} custom-call(s32[4]{0:T(128)} %constant.62.clone.1.refs_0_, s32[4]{0:T(128)} %tile.21.refs_1_, s32[16]{0:T(128)} %stack.361.refs_2_, s32[8]{0:T(128)} %broadcast_11_refs_0__refs_3__refs_4_.2.refs_0_.refs_3_.refs_4_, s32[8]{0:T(128)} %broadcast_11_refs_0__refs_3__refs_4_.2.refs_0_.refs_3_.refs_4_, ...), custom_call_target="tpu_custom_call" | custom-call | flops 536870912 | bytes 8388608 | tf_op jit(solution)/shard_map/pallas_call | solution.py:199
  322.3 7.1 %shard_map.160 = f32[4096,128]{1,0:T(8,128)} custom-call(s32[4]{0:T(128)} %constant.62.clone.1.refs_0_, s32[4]{0:T(128)} %tile.9.refs_1_, s32[16]{0:T(128)} %stack.361.refs_2_, s32[8]{0:T(128)} %broadcast_11_refs_0__refs_3__refs_4_.2.refs_0_.refs_3_.refs_4_, s32[8]{0:T(128)} %broadcast_11_refs_0__refs_3__refs_4_.2.refs_0_.refs_3_.refs_4_, ...), custom_call_target="tpu_custom_call" | custom-call | flops 536870912 | bytes 8388608 | tf_op jit(solution)/shard_map/pallas_call | solution.py:199
  336.4 12.3 %shard_map.162.refs_1_.refs_11_ = f32[2048,128]{1,0:T(8,128)} custom-call(s32[8]{0:T(128)} %broadcast_11_refs_0__refs_3__refs_4_.2.refs_0_.refs_3_.refs_4_, s32[8]{0:T(128)} %iota.86.refs_1_, s32[8]{0:T(128)} %iota_multiply_fusion.1.refs_2_, s32[8]{0:T(128)} %broadcast_11_refs_0__refs_3__refs_4_.2.refs_0_.refs_3_.refs_4_, s32[128]{0:T(128)} %reshape.119.refs_4_, ...), custom_call_target="tpu_custom_call" | custom-call | flops 2147483648 | bytes 19922944 | tf_op jit(solution)/shard_map/pallas_call | solution.py:199
  354.8 10.0 %collective-permute-done.57 = f32[344,128]{1,0:T(8,128)S(1)} collective-permute-done((f32[344,128]{1,0:T(8,128)S(1)}, f32[344,128]{1,0:T(8,128)S(1)}, u32[]{:S(2)}, u32[]{:S(2)}) %collective-permute-start.57) | collective-permute-done | bytes 176160 | tf_op jit(solution)/shard_map/ppermute | solution.py:242
  367.7 4.3 collective-permute-start.63
  372.0 16.0 %collective-permute-done.64 = f32[512,128]{1,0:T(8,128)S(1)} collective-permute-done((f32[512,128]{1,0:T(8,128)}, f32[512,128]{1,0:T(8,128)S(1)}, u32[]{:S(2)}, u32[]{:S(2)}) %collective-permute-start.64) | collective-permute-done | bytes 262176 | tf_op jit(solution)/shard_map/ppermute | solution.py:242
  394.9 13.2 %shard_map.164 = (f32[2048,128]{1,0:T(8,128)}, f32[4096,128]{1,0:T(8,128)}) custom-call(s32[8]{0:T(128)} %broadcast_11_refs_0__refs_3__refs_4_.2.refs_0_.refs_3_.refs_4_, s32[8]{0:T(128)} %iota.79.refs_1_, s32[8]{0:T(128)} %iota_multiply_fusion.1.refs_2_, s32[8]{0:T(128)} %stack.344.refs_3_, s32[128]{0:T(128)} %reshape.118.refs_4_, ...), custom_call_target="tpu_custom_call" | custom-call | flops 2147483648 | bytes 23068672 | tf_op jit(solution)/shard_map/pallas_call | solution.py:199
  412.6 20.9 %collective-permute-done.66 = f32[2048,128]{1,0:T(8,128)S(1)} collective-permute-done((f32[2048,128]{1,0:T(8,128)}, f32[2048,128]{1,0:T(8,128)S(1)}, u32[]{:S(2)}, u32[]{:S(2)}) %collective-permute-start.66) | collective-permute-done | bytes 1048608 | tf_op jit(solution)/shard_map/ppermute | solution.py:242
  435.9 5.0 shard_map.168
  442.5 5.0 shard_map.167
  447.4 4.2 collective-permute-start.68
  451.7 5.0 shard_map.166
  458.0 5.0 shard_map.165
  463.0 15.4 %collective-permute-done.69 = f32[1024,128]{1,0:T(8,128)S(1)} collective-permute-done((f32[1024,128]{1,0:T(8,128)}, f32[1024,128]{1,0:T(8,128)S(1)}, u32[]{:S(2)}, u32[]{:S(2)}) %collective-permute-start.69) | collective-permute-done | bytes 524320 | tf_op jit(solution)/shard_map/ppermute | solution.py:242
  478.4 8.9 %collective-permute-done.68 = f32[1024,128]{1,0:T(8,128)S(1)} collective-permute-done((f32[1024,128]{1,0:T(8,128)}, f32[1024,128]{1,0:T(8,128)S(1)}, u32[]{:S(2)}, u32[]{:S(2)}) %collective-permute-start.68) | collective-permute-done | bytes 524320 | tf_op jit(solution)/shard_map/ppermute | solution.py:242
  491.5 4.7 maximum_select_fusion
  496.2 13.3 %collective-permute-done.70 = f32[1024,128]{1,0:T(8,128)S(1)} collective-permute-done((f32[1024,128]{1,0:T(8,128)S(1)}, f32[1024,128]{1,0:T(8,128)S(1)}, u32[]{:S(2)}, u32[]{:S(2)}) %collective-permute-start.70) | collective-permute-done | bytes 524320 | tf_op jit(solution)/shard_map/ppermute | solution.py:242
  509.5 16.3 %collective-permute-done.71 = f32[1024,128]{1,0:T(8,128)S(1)} collective-permute-done((f32[1024,128]{1,0:T(8,128)S(1)}, f32[1024,128]{1,0:T(8,128)S(1)}, u32[]{:S(2)}, u32[]{:S(2)}) %collective-permute-start.71) | collective-permute-done | bytes 524320 | tf_op jit(solution)/shard_map/ppermute | solution.py:242
  525.9 9.6 %collective-permute-done.72 = f32[1024,128]{1,0:T(8,128)S(1)} collective-permute-done((f32[1024,128]{1,0:T(8,128)S(1)}, f32[1024,128]{1,0:T(8,128)S(1)}, u32[]{:S(2)}, u32[]{:S(2)}) %collective-permute-start.72) | collective-permute-done | bytes 524320 | tf_op jit(solution)/shard_map/ppermute | solution.py:242
  (266 shorter events, 146.2 us)
Async XLA Ops:
  15.2 25.1 %collective-permute-start = (f32[2048,128]{1,0:T(8,128)}, f32[2048,128]{1,0:T(8,128)S(1)}, u32[]{:S(2)}, u32[]{:S(2)}) collective-permute-start(f32[2048,128]{1,0:T(8,128)} %shard_map.147.refs_9_), channel_id=1, source_target_pairs={{0,16},{16,0},{1,17},{17,1},{2,18},{18,2},{3,19},{19,3},{4,20},{20... | collective-permute-start | bytes 3145736 | tf_op jit(solution)/shard_map/ppermute | solution.py:242
  59.5 21.7 %collective-permute-start.4 = (f32[512,128]{1,0:T(8,128)S(1)}, f32[512,128]{1,0:T(8,128)S(1)}, u32[]{:S(2)}, u32[]{:S(2)}) collective-permute-start(f32[512,128]{1,0:T(8,128)S(1)} %get-tuple-element.37), channel_id=1, source_target_pairs={{0,12},{4,8},{8,4},{12,0},{1,13},{5,9},{9,5},{13,1},{2,14},{6,10},... | collective-permute-start | bytes 786440 | tf_op jit(solution)/shard_map/ppermute | solution.py:242
  61.1 23.1 %collective-permute-start.3 = (f32[512,128]{1,0:T(8,128)S(1)}, f32[512,128]{1,0:T(8,128)S(1)}, u32[]{:S(2)}, u32[]{:S(2)}) collective-permute-start(f32[512,128]{1,0:T(8,128)S(1)} %get-tuple-element.38), channel_id=1, source_target_pairs={{0,8},{4,12},{8,0},{12,4},{1,9},{5,13},{9,1},{13,5},{2,10},{6,14},... | collective-permute-start | bytes 786440 | tf_op jit(solution)/shard_map/ppermute | solution.py:242
  62.2 22.0 %collective-permute-start.2 = (f32[512,128]{1,0:T(8,128)S(1)}, f32[512,128]{1,0:T(8,128)S(1)}, u32[]{:S(2)}, u32[]{:S(2)}) collective-permute-start(f32[512,128]{1,0:T(8,128)S(1)} %get-tuple-element.36), channel_id=1, source_target_pairs={{0,4},{4,0},{8,12},{12,8},{1,5},{5,1},{9,13},{13,9},{2,6},{6,2},{1... | collective-permute-start | bytes 786440 | tf_op jit(solution)/shard_map/ppermute | solution.py:242
  85.9 13.0 %collective-permute-start.5 = (f32[512,128]{1,0:T(8,128)}, f32[512,128]{1,0:T(8,128)S(1)}, u32[]{:S(2)}, u32[]{:S(2)}) collective-permute-start(f32[512,128]{1,0:T(8,128)} %shard_map.152), channel_id=1, source_target_pairs={{0,4},{4,0},{8,12},{12,8},{1,5},{5,1},{9,13},{13,9},{2,6},{6,2},{1... | collective-permute-start | bytes 786440 | tf_op jit(solution)/shard_map/ppermute | solution.py:242
  88.3 19.3 %collective-permute-start.6 = (f32[512,128]{1,0:T(8,128)}, f32[512,128]{1,0:T(8,128)S(1)}, u32[]{:S(2)}, u32[]{:S(2)}) collective-permute-start(f32[512,128]{1,0:T(8,128)} %shard_map.152), channel_id=1, source_target_pairs={{0,8},{4,12},{8,0},{12,4},{1,9},{5,13},{9,1},{13,5},{2,10},{6,14},... | collective-permute-start | bytes 786440 | tf_op jit(solution)/shard_map/ppermute | solution.py:242
  89.3 23.6 %collective-permute-start.7 = (f32[512,128]{1,0:T(8,128)}, f32[512,128]{1,0:T(8,128)S(1)}, u32[]{:S(2)}, u32[]{:S(2)}) collective-permute-start(f32[512,128]{1,0:T(8,128)} %shard_map.152), channel_id=1, source_target_pairs={{0,12},{4,8},{8,4},{12,0},{1,13},{5,9},{9,5},{13,1},{2,14},{6,10},... | collective-permute-start | bytes 786440 | tf_op jit(solution)/shard_map/ppermute | solution.py:242
  89.9 25.7 %collective-permute-start.8 = (f32[512,128]{1,0:T(8,128)}, f32[512,128]{1,0:T(8,128)S(1)}, u32[]{:S(2)}, u32[]{:S(2)}) collective-permute-start(f32[512,128]{1,0:T(8,128)} %shard_map.152), channel_id=1, source_target_pairs={{0,2},{1,3},{2,0},{3,1},{4,6},{5,7},{6,4},{7,5},{8,10},{9,11},{10,... | collective-permute-start | bytes 786440 | tf_op jit(solution)/shard_map/ppermute | solution.py:242
  98.9 16.7 %collective-permute-start.9 = (f32[512,128]{1,0:T(8,128)S(1)}, f32[512,128]{1,0:T(8,128)S(1)}, u32[]{:S(2)}, u32[]{:S(2)}) collective-permute-start(f32[512,128]{1,0:T(8,128)S(1)} %collective-permute-done.5), channel_id=1, source_target_pairs={{0,2},{1,3},{2,0},{3,1},{4,6},{5,7},{6,4},{7,5},{8,10},{9,11},{10,... | collective-permute-start | bytes 786440 | tf_op jit(solution)/shard_map/ppermute | solution.py:242
  114.0 10.3 %collective-permute-start.12 = (f32[2048,128]{1,0:T(8,128)S(1)}, f32[2048,128]{1,0:T(8,128)S(1)}, u32[]{:S(2)}, u32[]{:S(2)}) collective-permute-start(f32[2048,128]{1,0:T(8,128)S(1)} %pad_maximum_fusion.refs_9_), channel_id=1, source_target_pairs={{0,1},{1,0},{2,3},{3,2},{4,5},{5,4},{6,7},{7,6},{8,9},{9,8},{10,11... | collective-permute-start | bytes 3145736 | tf_op jit(solution)/shard_map/ppermute | solution.py:242
  114.0 8.7 %collective-permute-start.11 = (f32[512,128]{1,0:T(8,128)S(1)}, f32[512,128]{1,0:T(8,128)S(1)}, u32[]{:S(2)}, u32[]{:S(2)}) collective-permute-start(f32[512,128]{1,0:T(8,128)S(1)} %collective-permute-done.7), channel_id=1, source_target_pairs={{0,2},{1,3},{2,0},{3,1},{4,6},{5,7},{6,4},{7,5},{8,10},{9,11},{10,... | collective-permute-start | bytes 786440 | tf_op jit(solution)/shard_map/ppermute | solution.py:242
  134.3 14.2 %collective-permute-start.14 = (f32[1024,128]{1,0:T(8,128)}, f32[1024,128]{1,0:T(8,128)S(1)}, u32[]{:S(2)}, u32[]{:S(2)}) collective-permute-start(f32[1024,128]{1,0:T(8,128)} %shard_map.153.refs_7_.refs_9_), channel_id=1, source_target_pairs={{0,16},{16,0},{1,17},{17,1},{2,18},{18,2},{3,19},{19,3},{4,20},{20... | collective-permute-start | bytes 1572872 | tf_op jit(solution)/shard_map/ppermute | solution.py:242
  162.9 13.1 %collective-permute-start.16 = (f32[672,128]{1,0:T(8,128)S(1)}, f32[672,128]{1,0:T(8,128)S(1)}, u32[]{:S(2)}, u32[]{:S(2)}) collective-permute-start(f32[672,128]{1,0:T(8,128)S(1)} %bitcast.231), channel_id=1, source_target_pairs={{0,2},{1,3},{2,0},{3,1},{4,6},{5,7},{6,4},{7,5},{8,10},{9,11},{10,... | collective-permute-start | bytes 1032200 | tf_op jit(solution)/shard_map/ppermute | solution.py:242
  177.7 9.2 %collective-permute-start.18 = (f32[168,128]{1,0:T(8,128)S(1)}, f32[168,128]{1,0:T(8,128)S(1)}, u32[]{:S(2)}, u32[]{:S(2)}) collective-permute-start(f32[168,128]{1,0:T(8,128)S(1)} %get-tuple-element.29), channel_id=1, source_target_pairs={{0,8},{4,12},{8,0},{12,4},{1,9},{5,13},{9,1},{13,5},{2,10},{6,14},... | collective-permute-start | bytes 258056 | tf_op jit(solution)/shard_map/ppermute | solution.py:242
  191.2 11.8 %collective-permute-start.26 = (f32[256,128]{1,0:T(8,128)S(1)}, f32[256,128]{1,0:T(8,128)S(1)}, u32[]{:S(2)}, u32[]{:S(2)}) collective-permute-start(f32[256,128]{1,0:T(8,128)S(1)} %maximum_subtract_fusion), channel_id=1, source_target_pairs={{0,12},{4,8},{8,4},{12,0},{1,13},{5,9},{9,5},{13,1},{2,14},{6,10},... | collective-permute-start | bytes 393224 | tf_op jit(solution)/shard_map/ppermute | solution.py:242
  192.6 11.1 %collective-permute-start.25 = (f32[256,128]{1,0:T(8,128)S(1)}, f32[256,128]{1,0:T(8,128)S(1)}, u32[]{:S(2)}, u32[]{:S(2)}) collective-permute-start(f32[256,128]{1,0:T(8,128)S(1)} %maximum_subtract_fusion), channel_id=1, source_target_pairs={{0,8},{4,12},{8,0},{12,4},{1,9},{5,13},{9,1},{13,5},{2,10},{6,14},... | collective-permute-start | bytes 393224 | tf_op jit(solution)/shard_map/ppermute | solution.py:242
  194.1 11.8 %collective-permute-start.27 = (f32[256,128]{1,0:T(8,128)S(1)}, f32[256,128]{1,0:T(8,128)S(1)}, u32[]{:S(2)}, u32[]{:S(2)}) collective-permute-start(f32[256,128]{1,0:T(8,128)S(1)} %maximum_subtract_fusion), channel_id=1, source_target_pairs={{0,2},{1,3},{2,0},{3,1},{4,6},{5,7},{6,4},{7,5},{8,10},{9,11},{10,... | collective-permute-start | bytes 393224 | tf_op jit(solution)/shard_map/ppermute | solution.py:242
  195.6 10.3 %collective-permute-start.28 = (f32[256,128]{1,0:T(8,128)S(1)}, f32[256,128]{1,0:T(8,128)S(1)}, u32[]{:S(2)}, u32[]{:S(2)}) collective-permute-start(f32[256,128]{1,0:T(8,128)S(1)} %collective-permute-done.24), channel_id=1, source_target_pairs={{0,2},{1,3},{2,0},{3,1},{4,6},{5,7},{6,4},{7,5},{8,10},{9,11},{10,... | collective-permute-start | bytes 393224 | tf_op jit(solution)/shard_map/ppermute | solution.py:242
  203.8 10.1 %collective-permute-start.31 = (f32[1024,128]{1,0:T(8,128)S(1)}, f32[1024,128]{1,0:T(8,128)S(1)}, u32[]{:S(2)}, u32[]{:S(2)}) collective-permute-start(f32[1024,128]{1,0:T(8,128)S(1)} %pad_maximum_fusion.2.refs_9_), channel_id=1, source_target_pairs={{0,1},{1,0},{2,3},{3,2},{4,5},{5,4},{6,7},{7,6},{8,9},{9,8},{10,11... | collective-permute-start | bytes 1572872 | tf_op jit(solution)/shard_map/ppermute | solution.py:242
  240.8 10.5 %collective-permute-start.35 = (f32[672,128]{1,0:T(8,128)S(1)}, f32[672,128]{1,0:T(8,128)S(1)}, u32[]{:S(2)}, u32[]{:S(2)}) collective-permute-start(f32[672,128]{1,0:T(8,128)S(1)} %bitcast.232), channel_id=1, source_target_pairs={{0,2},{1,3},{2,0},{3,1},{4,6},{5,7},{6,4},{7,5},{8,10},{9,11},{10,... | collective-permute-start | bytes 1032200 | tf_op jit(solution)/shard_map/ppermute | solution.py:242
  243.4 13.9 %collective-permute-start.41 = (f32[176,128]{1,0:T(8,128)S(1)}, f32[176,128]{1,0:T(8,128)S(1)}, u32[]{:S(2)}, u32[]{:S(2)}) collective-permute-start(f32[176,128]{1,0:T(8,128)S(1)} %bitcast.240), channel_id=1, source_target_pairs={{0,12},{4,8},{8,4},{12,0},{1,13},{5,9},{9,5},{13,1},{2,14},{6,10},... | collective-permute-start | bytes 270344 | tf_op jit(solution)/shard_map/ppermute | solution.py:242
  244.1 13.2 %collective-permute-start.40 = (f32[176,128]{1,0:T(8,128)S(1)}, f32[176,128]{1,0:T(8,128)S(1)}, u32[]{:S(2)}, u32[]{:S(2)}) collective-permute-start(f32[176,128]{1,0:T(8,128)S(1)} %bitcast.237), channel_id=1, source_target_pairs={{0,8},{4,12},{8,0},{12,4},{1,9},{5,13},{9,1},{13,5},{2,10},{6,14},... | collective-permute-start | bytes 270344 | tf_op jit(solution)/shard_map/ppermute | solution.py:242
  248.3 9.0 %collective-permute-start.39 = (f32[176,128]{1,0:T(8,128)S(1)}, f32[176,128]{1,0:T(8,128)S(1)}, u32[]{:S(2)}, u32[]{:S(2)}) collective-permute-start(f32[176,128]{1,0:T(8,128)S(1)} %bitcast.236), channel_id=1, source_target_pairs={{0,4},{4,0},{8,12},{12,8},{1,5},{5,1},{9,13},{13,9},{2,6},{6,2},{1... | collective-permute-start | bytes 270344 | tf_op jit(solution)/shard_map/ppermute | solution.py:242
  253.1 9.1 %collective-permute-start.37 = (f32[168,128]{1,0:T(8,128)S(1)}, f32[168,128]{1,0:T(8,128)S(1)}, u32[]{:S(2)}, u32[]{:S(2)}) collective-permute-start(f32[168,128]{1,0:T(8,128)S(1)} %get-tuple-element.26), channel_id=1, source_target_pairs={{0,8},{4,12},{8,0},{12,4},{1,9},{5,13},{9,1},{13,5},{2,10},{6,14},... | collective-permute-start | bytes 258056 | tf_op jit(solution)/shard_map/ppermute | solution.py:242
  266.4 10.5 %collective-permute-start.44 = (f32[256,128]{1,0:T(8,128)S(1)}, f32[256,128]{1,0:T(8,128)S(1)}, u32[]{:S(2)}, u32[]{:S(2)}) collective-permute-start(f32[256,128]{1,0:T(8,128)S(1)} %pad_maximum_fusion.4), channel_id=1, source_target_pairs={{0,8},{4,12},{8,0},{12,4},{1,9},{5,13},{9,1},{13,5},{2,10},{6,14},... | collective-permute-start | bytes 393224 | tf_op jit(solution)/shard_map/ppermute | solution.py:242
  267.4 12.4 %collective-permute-start.45 = (f32[256,128]{1,0:T(8,128)S(1)}, f32[256,128]{1,0:T(8,128)S(1)}, u32[]{:S(2)}, u32[]{:S(2)}) collective-permute-start(f32[256,128]{1,0:T(8,128)S(1)} %pad_maximum_fusion.4), channel_id=1, source_target_pairs={{0,12},{4,8},{8,4},{12,0},{1,13},{5,9},{9,5},{13,1},{2,14},{6,10},... | collective-permute-start | bytes 393224 | tf_op jit(solution)/shard_map/ppermute | solution.py:242
  268.5 13.5 %collective-permute-start.46 = (f32[256,128]{1,0:T(8,128)S(1)}, f32[256,128]{1,0:T(8,128)S(1)}, u32[]{:S(2)}, u32[]{:S(2)}) collective-permute-start(f32[256,128]{1,0:T(8,128)S(1)} %pad_maximum_fusion.4), channel_id=1, source_target_pairs={{0,2},{1,3},{2,0},{3,1},{4,6},{5,7},{6,4},{7,5},{8,10},{9,11},{10,... | collective-permute-start | bytes 393224 | tf_op jit(solution)/shard_map/ppermute | solution.py:242
  271.3 10.7 %collective-permute-start.47 = (f32[256,128]{1,0:T(8,128)S(1)}, f32[256,128]{1,0:T(8,128)S(1)}, u32[]{:S(2)}, u32[]{:S(2)}) collective-permute-start(f32[256,128]{1,0:T(8,128)S(1)} %collective-permute-done.43), channel_id=1, source_target_pairs={{0,2},{1,3},{2,0},{3,1},{4,6},{5,7},{6,4},{7,5},{8,10},{9,11},{10,... | collective-permute-start | bytes 393224 | tf_op jit(solution)/shard_map/ppermute | solution.py:242
  279.8 8.9 %collective-permute-start.50 = (f32[1024,128]{1,0:T(8,128)S(1)}, f32[1024,128]{1,0:T(8,128)S(1)}, u32[]{:S(2)}, u32[]{:S(2)}) collective-permute-start(f32[1024,128]{1,0:T(8,128)S(1)} %constant_dynamic-update-slice_fusion.8.refs_9_), channel_id=1, source_target_pairs={{0,1},{1,0},{2,3},{3,2},{4,5},{5,4},{6,7},{7,6},{8,9},{9,8},{10,11... | collective-permute-start | bytes 1572872 | tf_op jit(solution)/shard_map/ppermute | solution.py:242
  299.6 14.2 %collective-permute-start.52 = (f32[1024,128]{1,0:T(8,128)}, f32[1024,128]{1,0:T(8,128)S(1)}, u32[]{:S(2)}, u32[]{:S(2)}) collective-permute-start(f32[1024,128]{1,0:T(8,128)} %get-tuple-element.8.refs_11_), channel_id=1, source_target_pairs={{0,16},{16,0},{1,17},{17,1},{2,18},{18,2},{3,19},{19,3},{4,20},{20... | collective-permute-start | bytes 1572872 | tf_op jit(solution)/shard_map/ppermute | solution.py:242
  330.7 19.0 %collective-permute-start.54 = (f32[1376,128]{1,0:T(8,128)S(1)}, f32[1376,128]{1,0:T(8,128)S(1)}, u32[]{:S(2)}, u32[]{:S(2)}) collective-permute-start(f32[1376,128]{1,0:T(8,128)S(1)} %bitcast.230), channel_id=1, source_target_pairs={{0,2},{1,3},{2,0},{3,1},{4,6},{5,7},{6,4},{7,5},{8,10},{9,11},{10,... | collective-permute-start | bytes 2113544 | tf_op jit(solution)/shard_map/ppermute | solution.py:242
  332.4 16.4 %collective-permute-start.60 = (f32[336,128]{1,0:T(8,128)S(1)}, f32[336,128]{1,0:T(8,128)S(1)}, u32[]{:S(2)}, u32[]{:S(2)}) collective-permute-start(f32[336,128]{1,0:T(8,128)S(1)} %bitcast.235), channel_id=1, source_target_pairs={{0,12},{4,8},{8,4},{12,0},{1,13},{5,9},{9,5},{13,1},{2,14},{6,10},... | collective-permute-start | bytes 516104 | tf_op jit(solution)/shard_map/ppermute | solution.py:242
  333.9 15.0 %collective-permute-start.59 = (f32[336,128]{1,0:T(8,128)S(1)}, f32[336,128]{1,0:T(8,128)S(1)}, u32[]{:S(2)}, u32[]{:S(2)}) collective-permute-start(f32[336,128]{1,0:T(8,128)S(1)} %bitcast.234), channel_id=1, source_target_pairs={{0,8},{4,12},{8,0},{12,4},{1,9},{5,13},{9,1},{13,5},{2,10},{6,14},... | collective-permute-start | bytes 516104 | tf_op jit(solution)/shard_map/ppermute | solution.py:242
  334.9 14.1 %collective-permute-start.58 = (f32[336,128]{1,0:T(8,128)S(1)}, f32[336,128]{1,0:T(8,128)S(1)}, u32[]{:S(2)}, u32[]{:S(2)}) collective-permute-start(f32[336,128]{1,0:T(8,128)S(1)} %bitcast.233), channel_id=1, source_target_pairs={{0,4},{4,0},{8,12},{12,8},{1,5},{5,1},{9,13},{13,9},{2,6},{6,2},{1... | collective-permute-start | bytes 516104 | tf_op jit(solution)/shard_map/ppermute | solution.py:242
  349.8 14.9 %collective-permute-start.57 = (f32[344,128]{1,0:T(8,128)S(1)}, f32[344,128]{1,0:T(8,128)S(1)}, u32[]{:S(2)}, u32[]{:S(2)}) collective-permute-start(f32[344,128]{1,0:T(8,128)S(1)} %get-tuple-element.19), channel_id=1, source_target_pairs={{0,12},{4,8},{8,4},{12,0},{1,13},{5,9},{9,5},{13,1},{2,14},{6,10},... | collective-permute-start | bytes 528392 | tf_op jit(solution)/shard_map/ppermute | solution.py:242
  351.1 14.5 %collective-permute-start.56 = (f32[344,128]{1,0:T(8,128)S(1)}, f32[344,128]{1,0:T(8,128)S(1)}, u32[]{:S(2)}, u32[]{:S(2)}) collective-permute-start(f32[344,128]{1,0:T(8,128)S(1)} %get-tuple-element.20), channel_id=1, source_target_pairs={{0,8},{4,12},{8,0},{12,4},{1,9},{5,13},{9,1},{13,5},{2,10},{6,14},... | collective-permute-start | bytes 528392 | tf_op jit(solution)/shard_map/ppermute | solution.py:242
  354.8 11.7 %collective-permute-start.55 = (f32[344,128]{1,0:T(8,128)S(1)}, f32[344,128]{1,0:T(8,128)S(1)}, u32[]{:S(2)}, u32[]{:S(2)}) collective-permute-start(f32[344,128]{1,0:T(8,128)S(1)} %get-tuple-element.18), channel_id=1, source_target_pairs={{0,4},{4,0},{8,12},{12,8},{1,5},{5,1},{9,13},{13,9},{2,6},{6,2},{1... | collective-permute-start | bytes 528392 | tf_op jit(solution)/shard_map/ppermute | solution.py:242
  367.3 20.7 %collective-permute-start.64 = (f32[512,128]{1,0:T(8,128)}, f32[512,128]{1,0:T(8,128)S(1)}, u32[]{:S(2)}, u32[]{:S(2)}) collective-permute-start(f32[512,128]{1,0:T(8,128)} %shard_map.163), channel_id=1, source_target_pairs={{0,12},{4,8},{8,4},{12,0},{1,13},{5,9},{9,5},{13,1},{2,14},{6,10},... | collective-permute-start | bytes 786440 | tf_op jit(solution)/shard_map/ppermute | solution.py:242
  367.7 21.9 %collective-permute-start.63 = (f32[512,128]{1,0:T(8,128)}, f32[512,128]{1,0:T(8,128)S(1)}, u32[]{:S(2)}, u32[]{:S(2)}) collective-permute-start(f32[512,128]{1,0:T(8,128)} %shard_map.163), channel_id=1, source_target_pairs={{0,8},{4,12},{8,0},{12,4},{1,9},{5,13},{9,1},{13,5},{2,10},{6,14},... | collective-permute-start | bytes 786440 | tf_op jit(solution)/shard_map/ppermute | solution.py:242
  372.0 17.6 %collective-permute-start.62 = (f32[512,128]{1,0:T(8,128)}, f32[512,128]{1,0:T(8,128)S(1)}, u32[]{:S(2)}, u32[]{:S(2)}) collective-permute-start(f32[512,128]{1,0:T(8,128)} %shard_map.163), channel_id=1, source_target_pairs={{0,4},{4,0},{8,12},{12,8},{1,5},{5,1},{9,13},{13,9},{2,6},{6,2},{1... | collective-permute-start | bytes 786440 | tf_op jit(solution)/shard_map/ppermute | solution.py:242
  408.1 25.4 %collective-permute-start.66 = (f32[2048,128]{1,0:T(8,128)}, f32[2048,128]{1,0:T(8,128)S(1)}, u32[]{:S(2)}, u32[]{:S(2)}) collective-permute-start(f32[2048,128]{1,0:T(8,128)} %get-tuple-element.10), channel_id=1, source_target_pairs={{0,16},{16,0},{1,17},{17,1},{2,18},{18,2},{3,19},{19,3},{4,20},{20... | collective-permute-start | bytes 3145736 | tf_op jit(solution)/shard_map/ppermute | solution.py:242
  409.6 81.9 %collective-permute-start.73 = (f32[4096,128]{1,0:T(8,128)}, f32[4096,128]{1,0:T(8,128)}, u32[]{:S(2)}, u32[]{:S(2)}) collective-permute-start(f32[4096,128]{1,0:T(8,128)} %get-tuple-element.11), channel_id=1, source_target_pairs={{0,2},{1,3},{2,0},{3,1},{4,6},{5,7},{6,4},{7,5},{8,10},{9,11},{10,... | collective-permute-start | bytes 6291464 | tf_op jit(solution)/shard_map/ppermute | solution.py:242
  440.8 37.5 %collective-permute-start.69 = (f32[1024,128]{1,0:T(8,128)}, f32[1024,128]{1,0:T(8,128)S(1)}, u32[]{:S(2)}, u32[]{:S(2)}) collective-permute-start(f32[1024,128]{1,0:T(8,128)} %shard_map.168), channel_id=1, source_target_pairs={{0,12},{4,8},{8,4},{12,0},{1,13},{5,9},{9,5},{13,1},{2,14},{6,10},... | collective-permute-start | bytes 1572872 | tf_op jit(solution)/shard_map/ppermute | solution.py:242
  447.4 39.8 %collective-permute-start.68 = (f32[1024,128]{1,0:T(8,128)}, f32[1024,128]{1,0:T(8,128)S(1)}, u32[]{:S(2)}, u32[]{:S(2)}) collective-permute-start(f32[1024,128]{1,0:T(8,128)} %shard_map.167), channel_id=1, source_target_pairs={{0,8},{4,12},{8,0},{12,4},{1,9},{5,13},{9,1},{13,5},{2,10},{6,14},... | collective-permute-start | bytes 1572872 | tf_op jit(solution)/shard_map/ppermute | solution.py:242
  456.6 30.6 %collective-permute-start.67 = (f32[1024,128]{1,0:T(8,128)}, f32[1024,128]{1,0:T(8,128)S(1)}, u32[]{:S(2)}, u32[]{:S(2)}) collective-permute-start(f32[1024,128]{1,0:T(8,128)} %shard_map.166), channel_id=1, source_target_pairs={{0,4},{4,0},{8,12},{12,8},{1,5},{5,1},{9,13},{13,9},{2,6},{6,2},{1... | collective-permute-start | bytes 1572872 | tf_op jit(solution)/shard_map/ppermute | solution.py:242
  487.6 22.0 %collective-permute-start.70 = (f32[1024,128]{1,0:T(8,128)S(1)}, f32[1024,128]{1,0:T(8,128)S(1)}, u32[]{:S(2)}, u32[]{:S(2)}) collective-permute-start(f32[1024,128]{1,0:T(8,128)S(1)} %get-tuple-element.13), channel_id=1, source_target_pairs={{0,4},{4,0},{8,12},{12,8},{1,5},{5,1},{9,13},{13,9},{2,6},{6,2},{1... | collective-permute-start | bytes 1572872 | tf_op jit(solution)/shard_map/ppermute | solution.py:242
  489.8 36.0 %collective-permute-start.71 = (f32[1024,128]{1,0:T(8,128)S(1)}, f32[1024,128]{1,0:T(8,128)S(1)}, u32[]{:S(2)}, u32[]{:S(2)}) collective-permute-start(f32[1024,128]{1,0:T(8,128)S(1)} %get-tuple-element.13), channel_id=1, source_target_pairs={{0,8},{4,12},{8,0},{12,4},{1,9},{5,13},{9,1},{13,5},{2,10},{6,14},... | collective-permute-start | bytes 1572872 | tf_op jit(solution)/shard_map/ppermute | solution.py:242
  491.0 44.5 %collective-permute-start.72 = (f32[1024,128]{1,0:T(8,128)S(1)}, f32[1024,128]{1,0:T(8,128)S(1)}, u32[]{:S(2)}, u32[]{:S(2)}) collective-permute-start(f32[1024,128]{1,0:T(8,128)S(1)} %get-tuple-element.13), channel_id=1, source_target_pairs={{0,12},{4,8},{8,4},{12,0},{1,13},{5,9},{9,5},{13,1},{2,14},{6,10},... | collective-permute-start | bytes 1572872 | tf_op jit(solution)/shard_map/ppermute | solution.py:242
  (56 other events, 410.6 us)

commit v4 on v3

--- a/solution.py
+++ b/solution.py
@@ -14,36 +14,56 @@
 def product_kernel(cfg, *refs):
     refs = list(refs)
     tile_p, tile_r, dst, offs, pattern = refs[:5]
-    streams = cfg["streams"]
-    matrices = refs[5 : 5 + streams]
-    at = 5 + streams
-    terms = refs[at : at + len(cfg["signs"])]
-    at += len(cfg["signs"])
-    pieces = refs[at : at + cfg["pieces"]]
-    at += cfg["pieces"]
-    addend = refs[at] if cfg["addend"] else None
-    at += 1 if cfg["addend"] else 0
+    matrix = refs[5]
+    count = len(cfg["signs"]) + cfg["pieces"] + (1 if cfg["addend"] else 0)
+    inputs = refs[6 : 6 + count]
+    at = 6 + count
     out = refs[at]
     at += 1
     ordered = refs[at] if cfg["ordered"] else None
     at += 1 if cfg["ordered"] else 0
-    vector = refs[at]
+    vector, buffer, arrived = refs[at : at + 3]
+    local = refs[at + 3 : at + 3 + count]
+    ready = refs[at + 3 + count] if count else None
+    terms = local[: len(cfg["signs"])]
+    pieces = local[len(cfg["signs"]) : len(cfg["signs"]) + cfg["pieces"]]
+    addend = local[-1] if cfg["addend"] else None
     transposed, depth, vectors = cfg["transposed"], cfg["depth"], cfg["vectors"]
     step = pl.program_id(0)
+    tile = cfg["tile"]
+    height = buffer.shape[1]
+
+    def fetch(t):
+        start = pl.multiple_of(tile_r[t] * tile, tile)
+        first = 0 if height > 1 or matrix.shape[0] == 1 else tile_p[t]
+        if transposed:
+            source = matrix.at[pl.ds(first, height), :, pl.ds(start, tile)]
+        else:
+            source = matrix.at[pl.ds(first, height), pl.ds(start, tile), :]
+        return pltpu.make_async_copy(source, buffer.at[t], arrived.at[t])
+
+    def bring(n):
+        return pltpu.make_async_copy(inputs[n], local[n], ready.at[n])
 
     @pl.when(step == 0)
     def _():
+        for n in range(count):
+            bring(n).start()
+        for t in range(cfg["tiles"]):
+            fetch(t).start()
+        for n in range(count):
+            bring(n).wait()
         if pieces:
             target = ordered if transposed else vector
-            count = 0
+            position = 0
             for piece in pieces:
                 size = cfg["piece"]
                 for n in range(piece.shape[0] // size):
-                    row = pl.multiple_of(offs[count], size)
+                    row = pl.multiple_of(offs[position], size)
                     target[pl.ds(row, size), :] = piece[pl.ds(n * size, size), :].astype(
                         target.dtype
                     )
-                    count += 1
+                    position += 1
         chunk = min(512, depth)
         for base in range(0, vectors * depth, chunk):
             if pieces:
@@ -64,13 +84,12 @@
             else:
                 vector[pl.ds(base, chunk), :] = value.astype(HALF)
 
-    tile, granule, block = cfg["tile"], cfg["granule"], cfg["block"]
+    fetch(step).wait()
+    granule, block = cfg["granule"], cfg["block"]
     blocks_r, blocks_c, other = cfg["blocks_r"], cfg["blocks_c"], cfg["other"]
     for sub in range(tile // block):
         result = None
-        for lead, which in [(p, n) for p in range(matrices[0].shape[0]) for n in range(streams)]:
-            matrix = matrices[which]
-            share = depth // streams
+        for lead in range(height):
             index = lead if cfg["sum_p"] else tile_p[step]
             start = 0
             if vectors > 1:
@@ -79,24 +98,20 @@
                 if not cfg["sum_p"]:
                     start = pl.multiple_of(start, stride)
             if transposed:
-                x = vector[pl.ds(start, 128), pl.ds(which * share, share)]
-                a = matrix[lead, :, pl.ds(sub * block, block)]
+                x = vector[pl.ds(start, 128), :]
+                a = buffer[step, lead, :, pl.ds(sub * block, block)]
             else:
-                start = start + which * share
-                if vectors > 1 and not cfg["sum_p"]:
-                    start = pl.multiple_of(start, share)
-                x = vector[pl.ds(start, share), :]
-                a = matrix[lead, pl.ds(sub * block, block), :]
+                x = vector[pl.ds(start, depth), :]
+                a = buffer[step, lead, pl.ds(sub * block, block), :]
             if cfg["masked"]:
                 here = (tile_r[step] * tile + sub * block) // cfg["pattern_block"]
                 kept = []
-                for n in range(share // other):
-                    across = which * (share // other) + n
+                for n in range(depth // other):
                     if transposed:
-                        flag = pattern[(index * blocks_r + across) * blocks_c + here]
+                        flag = pattern[(index * blocks_r + n) * blocks_c + here]
                         part = x[:, n * other : (n + 1) * other]
                     else:
-                        flag = pattern[(index * blocks_r + here) * blocks_c + across]
+                        flag = pattern[(index * blocks_r + here) * blocks_c + n]
                         part = x[n * other : (n + 1) * other, :]
                     kept.append(jnp.where(flag != 0, part, jnp.zeros_like(part)))
                 if len(kept) > 1:
@@ -161,8 +176,6 @@
         offs = jnp.zeros((8,), jnp.int32)
     if tile_p is None:
         tile_p = jnp.zeros((tiles,), jnp.int32)
-    least = other if masked else 128
-    streams = max([1] + [n for n in (2, 4) if depth % (n * least) == 0])
     signs = tuple(sign for _, sign in terms)
     term_arrays = [array for array, _ in terms]
     x_rows = vectors * depth
@@ -170,20 +183,10 @@
         transposed=transposed, depth=depth, vectors=vectors, signs=signs, pieces=len(pieces),
         piece=piece, addend=addend is not None, ordered=ordered, tile=tile, granule=granule,
         block=block, other=other, pattern_block=pattern_block, blocks_r=blocks_r,
-        blocks_c=blocks_c, masked=masked, sum_p=sum_p, streams=streams,
+        blocks_c=blocks_c, masked=masked, sum_p=sum_p, tiles=tiles,
     )
     held = lead if sum_p else 1
-    share = depth // streams
-    if transposed:
-        matrix_block = (held, share, tile)
-        maps = [lambda t, tp, tr, *_, s=s: (tp[t], s, tr[t]) for s in range(streams)]
-    else:
-        matrix_block = (held, tile, share)
-        maps = [lambda t, tp, tr, *_, s=s: (tp[t], tr[t], s) for s in range(streams)]
-
-    def whole(array):
-        return pl.BlockSpec(array.shape, lambda t, *_: (0, 0), pipeline_mode=pl.Buffered(1))
-
+    matrix_block = (held, depth, tile) if transposed else (held, tile, depth)
     inputs = term_arrays + list(pieces) + ([addend] if addend is not None else [])
     out_shape = [jax.ShapeDtypeStruct((out_rows, 128), FULL)]
     out_specs = [pl.BlockSpec((out_rows, 128), lambda t, *_: (0, 0))]
@@ -194,16 +197,22 @@
     matrix_bytes = held * depth * tile * 2
     resident = sum(a.size * a.dtype.itemsize for a in inputs)
     written = sum(s.size * 4 for s in out_shape)
-    budget = 2 * matrix_bytes + resident + 2 * written + x_rows * 256 + (12 << 20)
+    budget = tiles * matrix_bytes + resident + 2 * written + x_rows * 256 + (12 << 20)
     budget = max(budget, 57 << 20)
     result = pl.pallas_call(
         functools.partial(product_kernel, cfg),
         grid_spec=pltpu.PrefetchScalarGridSpec(
             num_scalar_prefetch=5,
             grid=(tiles,),
-            in_specs=[pl.BlockSpec(matrix_block, m) for m in maps] + [whole(a) for a in inputs],
+            in_specs=[pl.BlockSpec(memory_space=pl.ANY)] * (1 + len(inputs)),
             out_specs=out_specs,
-            scratch_shapes=[pltpu.VMEM(scratch, HALF)],
+            scratch_shapes=[
+                pltpu.VMEM(scratch, HALF),
+                pltpu.VMEM((tiles,) + matrix_block, HALF),
+                pltpu.SemaphoreType.DMA((tiles,)),
+            ]
+            + [pltpu.VMEM(a.shape, a.dtype) for a in inputs]
+            + ([pltpu.SemaphoreType.DMA((len(inputs),))] if inputs else []),
         ),
         out_shape=out_shape,
         compiler_params=pltpu.CompilerParams(vmem_limit_bytes=int(budget)),
@@ -212,7 +221,7 @@
             bytes_accessed=tiles * matrix_bytes + resident + written,
             transcendentals=0,
         ),
-    )(tile_p, tile_r, dst, offs, flags, *[matrix] * streams, *inputs)
+    )(tile_p, tile_r, dst, offs, flags, matrix, *inputs)
     return tuple(result) if ordered else result[0]
 
 

time: 539 us -> 536 us (level)
  transfers between devices with their start and end apart: 74 -> 74, of which waited for: 41 -> 41; matrix products, arithmetic and copies ran while one was open for 6% -> 6% of each run, Pallas kernels for 14% -> 13%
where the time goes in v4:
time: 536 us; the launch traced here: 535 us
  waiting for transfers between devices  246 us (46%)
  Pallas kernels  144 us (27%)
  starting transfers between devices  91.2 us (17%)
  other arithmetic  33.6 us (6%)
  local copies, waits for them, and re-layouts  17.8 us (3%)
    ppermute x74, waiting for transfers between devices, send(): return lax.ppermute(value, axis, [(i, i ^ bit) for i in range(size)])  246 us
    pallas_call x20, Pallas kernels, product(): pl.pallas_call(functools.partial(product_kernel, cfg), grid_spec=pltpu.Pr...  144 us
    ppermute x74, starting transfers between devices, send(): return lax.ppermute(value, axis, [(i, i ^ bit) for i in range(size)])  91.2 us
  transfers between devices with their start and end apart: 74, of which 41 were waited for; matrix products, arithmetic and copies ran while one was open for 6% of the time, Pallas kernels for 13%

profile of v4, /device:TPU:8, one launch (start us, length us, event | category | flops | bytes accessed | tf_op | source)
XLA Modules:
  0.0 534.8 jit_solution(8477586027615093618)
XLA Ops:
  2.3 13.5 %shard_map.147.refs_6_ = f32[2048,128]{1,0:T(8,128)} custom-call(s32[8]{0:T(128)} %broadcast_11_refs_0__refs_3__refs_4_.2.refs_0_.refs_3_.refs_4_, s32[8]{0:T(128)} %iota.77.refs_1_, s32[8]{0:T(128)} %iota_multiply_fusion.1.refs_2_, s32[8]{0:T(128)} %broadcast_11_refs_0__refs_3__refs_4_.2.refs_0_.refs_3_.refs_4_, ...), custom_call_target="tpu_custom_call" | custom-call | flops 2147483648 | bytes 19922944 | tf_op jit(solution)/shard_map/pallas_call | solution.py:202
  19.3 21.6 %collective-permute-done.refs_7_ = f32[2048,128]{1,0:T(8,128)S(1)} collective-permute-done((f32[2048,128]{1,0:T(8,128)}, f32[2048,128]{1,0:T(8,128)S(1)}, u32[]{:S(2)}, u32[]{:S(2)}) %collective-permute-start) | collective-permute-done | bytes 1048608 | tf_op jit(solution)/shard_map/ppermute | solution.py:251
  41.9 8.1 %shard_map.149 = f32[2048,128]{1,0:T(8,128)} custom-call(s32[4]{0:T(128)} %broadcast_9_refs_0_.2.refs_0_, s32[4]{0:T(128)} %iota_add_fusion.4.refs_1_, s32[8]{0:T(128)} %stack.387.refs_2_, s32[8]{0:T(128)} %broadcast_11_refs_0__refs_3__refs_4_.2.refs_0_.refs_3_.refs_4_, s32[128]{0:T(128)} %reshape.118.refs_4_, bf16[1,4096,2048]{2,1,0:T(8,128)(2,1)} %refs_5_.29, ...), custom_call_target="tpu_custom_call" | custom-call | flops 1073741824 | bytes 11534336 | tf_op jit(solution)/shard_map/pallas_call | solution.py:202
  50.7 8.1 %shard_map.148 = f32[2048,128]{1,0:T(8,128)} custom-call(s32[4]{0:T(128)} %broadcast_9_refs_0_.2.refs_0_, s32[4]{0:T(128)} %iota_add_fusion.5.refs_1_, s32[8]{0:T(128)} %stack.387.refs_2_, s32[8]{0:T(128)} %broadcast_11_refs_0__refs_3__refs_4_.2.refs_0_.refs_3_.refs_4_, s32[128]{0:T(128)} %reshape.118.refs_4_, bf16[1,4096,2048]{2,1,0:T(8,128)(2,1)} %refs_5_.29, ...), custom_call_target="tpu_custom_call" | custom-call | flops 1073741824 | bytes 11534336 | tf_op jit(solution)/shard_map/pallas_call | solution.py:202
  65.7 8.1 %shard_map.150.refs_1_.refs_8_ = f32[2048,128]{1,0:T(8,128)} custom-call(s32[4]{0:T(128)} %broadcast_9_refs_0_.2.refs_0_, s32[4]{0:T(128)} %iota_add_fusion.5.refs_1_, s32[8]{0:T(128)} %stack.396.refs_2_, s32[8]{0:T(128)} %broadcast_11_refs_0__refs_3__refs_4_.2.refs_0_.refs_3_.refs_4_, s32[128]{0:T(128)} %reshape.119.refs_4_, ...), custom_call_target="tpu_custom_call" | custom-call | flops 1073741824 | bytes 11534336 | tf_op jit(solution)/shard_map/pallas_call | solution.py:202
  73.8 8.1 %shard_map.151.refs_2_.refs_8_ = f32[2048,128]{1,0:T(8,128)} custom-call(s32[4]{0:T(128)} %broadcast_9_refs_0_.2.refs_0_, s32[4]{0:T(128)} %iota_add_fusion.4.refs_1_, s32[8]{0:T(128)} %stack.396.refs_2_, s32[8]{0:T(128)} %broadcast_11_refs_0__refs_3__refs_4_.2.refs_0_.refs_3_.refs_4_, s32[128]{0:T(128)} %reshape.119.refs_4_, ...), custom_call_target="tpu_custom_call" | custom-call | flops 1073741824 | bytes 11534336 | tf_op jit(solution)/shard_map/pallas_call | solution.py:202
  92.1 7.5 %collective-permute-done.5 = f32[512,128]{1,0:T(8,128)S(1)} collective-permute-done((f32[512,128]{1,0:T(8,128)}, f32[512,128]{1,0:T(8,128)S(1)}, u32[]{:S(2)}, u32[]{:S(2)}) %collective-permute-start.5) | collective-permute-done | bytes 262176 | tf_op jit(solution)/shard_map/ppermute | solution.py:251
  101.1 7.2 %collective-permute-done.6 = f32[512,128]{1,0:T(8,128)S(1)} collective-permute-done((f32[512,128]{1,0:T(8,128)}, f32[512,128]{1,0:T(8,128)S(1)}, u32[]{:S(2)}, u32[]{:S(2)}) %collective-permute-start.6) | collective-permute-done | bytes 262176 | tf_op jit(solution)/shard_map/ppermute | solution.py:251
  116.4 7.1 %collective-permute-done.11 = f32[512,128]{1,0:T(8,128)S(1)} collective-permute-done((f32[512,128]{1,0:T(8,128)S(1)}, f32[512,128]{1,0:T(8,128)S(1)}, u32[]{:S(2)}, u32[]{:S(2)}) %collective-permute-start.11) | collective-permute-done | bytes 262176 | tf_op jit(solution)/shard_map/ppermute | solution.py:251
  126.3 8.6 %shard_map.153.refs_6_ = f32[1024,128]{1,0:T(8,128)} custom-call(s32[4]{0:T(128)} %constant.62.clone.1.refs_0_, s32[4]{0:T(128)} %constant.65.clone.1.refs_1_, s32[4]{0:T(128)} %iota_multiply_fusion.2.refs_2_, s32[16]{0:T(128)} %stack.378.refs_3_, s32[8]{0:T(128)} %broadcast_11_refs_0__refs_3__refs_4_.2.refs_0_.refs_3_.refs_4_, ...), custom_call_target="tpu_custom_call" | custom-call | flops 1073741824 | bytes 13107200 | tf_op jit(solution)/shard_map/pallas_call | solution.py:202
  137.2 11.9 %collective-permute-done.14.refs_7_ = f32[1024,128]{1,0:T(8,128)S(1)} collective-permute-done((f32[1024,128]{1,0:T(8,128)}, f32[1024,128]{1,0:T(8,128)S(1)}, u32[]{:S(2)}, u32[]{:S(2)}) %collective-permute-start.14) | collective-permute-done | bytes 524320 | tf_op jit(solution)/shard_map/ppermute | solution.py:251
  150.0 6.1 %shard_map.155 = f32[2048,128]{1,0:T(8,128)} custom-call(s32[4]{0:T(128)} %broadcast_9_refs_0_.2.refs_0_, s32[4]{0:T(128)} %iota_add_fusion.4.refs_1_, s32[8]{0:T(128)} %stack.396.refs_2_, s32[8]{0:T(128)} %broadcast_11_refs_0__refs_3__refs_4_.2.refs_0_.refs_3_.refs_4_, s32[64]{0:T(128)} %reshape.120.refs_4_, bf16[2,4096,512]{2,1,0:T(8,128)(2,1)} %refs_5_.25, ...), custom_call_target="tpu_custom_call" | custom-call | flops 536870912 | bytes 7340032 | tf_op jit(solution)/shard_map/pallas_call | solution.py:202
  156.1 6.1 %shard_map.154 = f32[2048,128]{1,0:T(8,128)} custom-call(s32[4]{0:T(128)} %broadcast_9_refs_0_.2.refs_0_, s32[4]{0:T(128)} %iota_add_fusion.5.refs_1_, s32[8]{0:T(128)} %stack.396.refs_2_, s32[8]{0:T(128)} %broadcast_11_refs_0__refs_3__refs_4_.2.refs_0_.refs_3_.refs_4_, s32[64]{0:T(128)} %reshape.120.refs_4_, bf16[2,4096,512]{2,1,0:T(8,128)(2,1)} %refs_5_.25, ...), custom_call_target="tpu_custom_call" | custom-call | flops 536870912 | bytes 7340032 | tf_op jit(solution)/shard_map/pallas_call | solution.py:202
  169.3 4.8 collective-permute-done.22
  178.0 4.3 collective-permute-start.18
  183.1 4.1 collective-permute-done.18
  197.4 6.0 %collective-permute-done.26 = f32[256,128]{1,0:T(8,128)S(1)} collective-permute-done((f32[256,128]{1,0:T(8,128)S(1)}, f32[256,128]{1,0:T(8,128)S(1)}, u32[]{:S(2)}, u32[]{:S(2)}) %collective-permute-start.26) | collective-permute-done | bytes 131104 | tf_op jit(solution)/shard_map/ppermute | solution.py:251
  206.3 4.2 collective-permute-done.29
  216.0 5.1 shard_map.156.refs_6_
  223.2 6.5 %collective-permute-done.33.refs_7_ = f32[512,128]{1,0:T(8,128)S(1)} collective-permute-done((f32[512,128]{1,0:T(8,128)}, f32[512,128]{1,0:T(8,128)S(1)}, u32[]{:S(2)}, u32[]{:S(2)}) %collective-permute-start.33) | collective-permute-done | bytes 262176 | tf_op jit(solution)/shard_map/ppermute | solution.py:251
  230.4 4.0 shard_map.158
  235.1 4.0 shard_map.157
  243.4 4.2 collective-permute-start.40
  252.4 4.2 collective-permute-start.37
  272.1 4.2 collective-permute-done.44
  281.3 4.2 collective-permute-done.48
  290.8 8.0 %shard_map.159 = (f32[1024,128]{1,0:T(8,128)}, f32[4096,128]{1,0:T(8,128)}) custom-call(s32[4]{0:T(128)} %constant.62.clone.1.refs_0_, s32[4]{0:T(128)} %constant.65.clone.1.refs_1_, s32[4]{0:T(128)} %iota_multiply_fusion.2.refs_2_, s32[16]{0:T(128)} %stack.413.refs_3_, s32[64]{0:T(128)} %reshape.120.refs_4_, bf16[2,4096,512]{2,1,0:T(8,128)(2,1)} %refs_5_.25, ...), custom_call_target="tpu_custom_call" | custom-call | flops 1073741824 | bytes 13107200 | tf_op jit(solution)/shard_map/pallas_call | solution.py:202
  301.6 11.4 %collective-permute-done.52.refs_9_ = f32[1024,128]{1,0:T(8,128)S(1)} collective-permute-done((f32[1024,128]{1,0:T(8,128)}, f32[1024,128]{1,0:T(8,128)S(1)}, u32[]{:S(2)}, u32[]{:S(2)}) %collective-permute-start.52) | collective-permute-done | bytes 524320 | tf_op jit(solution)/shard_map/ppermute | solution.py:251
  313.8 6.4 %shard_map.161 = f32[4096,128]{1,0:T(8,128)} custom-call(s32[4]{0:T(128)} %constant.62.clone.1.refs_0_, s32[4]{0:T(128)} %tile.21.refs_1_, s32[16]{0:T(128)} %stack.361.refs_2_, s32[8]{0:T(128)} %broadcast_11_refs_0__refs_3__refs_4_.2.refs_0_.refs_3_.refs_4_, s32[8]{0:T(128)} %broadcast_11_refs_0__refs_3__refs_4_.2.refs_0_.refs_3_.refs_4_, ...), custom_call_target="tpu_custom_call" | custom-call | flops 536870912 | bytes 8388608 | tf_op jit(solution)/shard_map/pallas_call | solution.py:202
  320.9 6.4 %shard_map.160 = f32[4096,128]{1,0:T(8,128)} custom-call(s32[4]{0:T(128)} %constant.62.clone.1.refs_0_, s32[4]{0:T(128)} %tile.9.refs_1_, s32[16]{0:T(128)} %stack.361.refs_2_, s32[8]{0:T(128)} %broadcast_11_refs_0__refs_3__refs_4_.2.refs_0_.refs_3_.refs_4_, s32[8]{0:T(128)} %broadcast_11_refs_0__refs_3__refs_4_.2.refs_0_.refs_3_.refs_4_, ...), custom_call_target="tpu_custom_call" | custom-call | flops 536870912 | bytes 8388608 | tf_op jit(solution)/shard_map/pallas_call | solution.py:202
  334.4 11.6 %shard_map.162.refs_1_.refs_8_ = f32[2048,128]{1,0:T(8,128)} custom-call(s32[8]{0:T(128)} %broadcast_11_refs_0__refs_3__refs_4_.2.refs_0_.refs_3_.refs_4_, s32[8]{0:T(128)} %iota.86.refs_1_, s32[8]{0:T(128)} %iota_multiply_fusion.1.refs_2_, s32[8]{0:T(128)} %broadcast_11_refs_0__refs_3__refs_4_.2.refs_0_.refs_3_.refs_4_, s32[128]{0:T(128)} %reshape.119.refs_4_, ...), custom_call_target="tpu_custom_call" | custom-call | flops 2147483648 | bytes 19922944 | tf_op jit(solution)/shard_map/pallas_call | solution.py:202
  348.6 4.1 collective-permute-start.56
  352.8 10.0 %collective-permute-done.57 = f32[344,128]{1,0:T(8,128)S(1)} collective-permute-done((f32[344,128]{1,0:T(8,128)S(1)}, f32[344,128]{1,0:T(8,128)S(1)}, u32[]{:S(2)}, u32[]{:S(2)}) %collective-permute-start.57) | collective-permute-done | bytes 176160 | tf_op jit(solution)/shard_map/ppermute | solution.py:251
  365.7 4.3 collective-permute-start.63
  369.9 16.0 %collective-permute-done.64 = f32[512,128]{1,0:T(8,128)S(1)} collective-permute-done((f32[512,128]{1,0:T(8,128)}, f32[512,128]{1,0:T(8,128)S(1)}, u32[]{:S(2)}, u32[]{:S(2)}) %collective-permute-start.64) | collective-permute-done | bytes 262176 | tf_op jit(solution)/shard_map/ppermute | solution.py:251
  392.8 13.3 %shard_map.164 = (f32[2048,128]{1,0:T(8,128)}, f32[4096,128]{1,0:T(8,128)}) custom-call(s32[8]{0:T(128)} %broadcast_11_refs_0__refs_3__refs_4_.2.refs_0_.refs_3_.refs_4_, s32[8]{0:T(128)} %iota.79.refs_1_, s32[8]{0:T(128)} %iota_multiply_fusion.1.refs_2_, s32[8]{0:T(128)} %stack.344.refs_3_, s32[128]{0:T(128)} %reshape.118.refs_4_, ...), custom_call_target="tpu_custom_call" | custom-call | flops 2147483648 | bytes 23068672 | tf_op jit(solution)/shard_map/pallas_call | solution.py:202
  410.7 20.9 %collective-permute-done.66 = f32[2048,128]{1,0:T(8,128)S(1)} collective-permute-done((f32[2048,128]{1,0:T(8,128)}, f32[2048,128]{1,0:T(8,128)S(1)}, u32[]{:S(2)}, u32[]{:S(2)}) %collective-permute-start.66) | collective-permute-done | bytes 1048608 | tf_op jit(solution)/shard_map/ppermute | solution.py:251
  434.0 4.7 shard_map.168
  440.4 4.7 shard_map.167
  445.1 4.2 collective-permute-start.68
  449.4 4.7 shard_map.166
  455.6 4.8 shard_map.165
  460.3 16.0 %collective-permute-done.69 = f32[1024,128]{1,0:T(8,128)S(1)} collective-permute-done((f32[1024,128]{1,0:T(8,128)}, f32[1024,128]{1,0:T(8,128)S(1)}, u32[]{:S(2)}, u32[]{:S(2)}) %collective-permute-start.69) | collective-permute-done | bytes 524320 | tf_op jit(solution)/shard_map/ppermute | solution.py:251
  476.3 8.9 %collective-permute-done.68 = f32[1024,128]{1,0:T(8,128)S(1)} collective-permute-done((f32[1024,128]{1,0:T(8,128)}, f32[1024,128]{1,0:T(8,128)S(1)}, u32[]{:S(2)}, u32[]{:S(2)}) %collective-permute-start.68) | collective-permute-done | bytes 524320 | tf_op jit(solution)/shard_map/ppermute | solution.py:251
  489.4 4.7 maximum_select_fusion
  494.1 13.3 %collective-permute-done.70 = f32[1024,128]{1,0:T(8,128)S(1)} collective-permute-done((f32[1024,128]{1,0:T(8,128)S(1)}, f32[1024,128]{1,0:T(8,128)S(1)}, u32[]{:S(2)}, u32[]{:S(2)}) %collective-permute-start.70) | collective-permute-done | bytes 524320 | tf_op jit(solution)/shard_map/ppermute | solution.py:251
  507.5 16.3 %collective-permute-done.71 = f32[1024,128]{1,0:T(8,128)S(1)} collective-permute-done((f32[1024,128]{1,0:T(8,128)S(1)}, f32[1024,128]{1,0:T(8,128)S(1)}, u32[]{:S(2)}, u32[]{:S(2)}) %collective-permute-start.71) | collective-permute-done | bytes 524320 | tf_op jit(solution)/shard_map/ppermute | solution.py:251
  523.8 9.6 %collective-permute-done.72 = f32[1024,128]{1,0:T(8,128)S(1)} collective-permute-done((f32[1024,128]{1,0:T(8,128)S(1)}, f32[1024,128]{1,0:T(8,128)S(1)}, u32[]{:S(2)}, u32[]{:S(2)}) %collective-permute-start.72) | collective-permute-done | bytes 524320 | tf_op jit(solution)/shard_map/ppermute | solution.py:251
  (266 shorter events, 147.2 us)
Async XLA Ops:
  15.8 25.2 %collective-permute-start = (f32[2048,128]{1,0:T(8,128)}, f32[2048,128]{1,0:T(8,128)S(1)}, u32[]{:S(2)}, u32[]{:S(2)}) collective-permute-start(f32[2048,128]{1,0:T(8,128)} %shard_map.147.refs_6_), channel_id=1, source_target_pairs={{0,16},{16,0},{1,17},{17,1},{2,18},{18,2},{3,19},{19,3},{4,20},{20... | collective-permute-start | bytes 3145736 | tf_op jit(solution)/shard_map/ppermute | solution.py:251
  50.0 8.7 %collective-permute-start.1 = (f32[2048,128]{1,0:T(8,128)}, f32[2048,128]{1,0:T(8,128)S(1)}, u32[]{:S(2)}, u32[]{:S(2)}) collective-permute-start(f32[2048,128]{1,0:T(8,128)} %shard_map.149), channel_id=1, source_target_pairs={{0,1},{1,0},{2,3},{3,2},{4,5},{5,4},{6,7},{7,6},{8,9},{9,8},{10,11... | collective-permute-start | bytes 3145736 | tf_op jit(solution)/shard_map/ppermute | solution.py:251
  60.2 21.7 %collective-permute-start.4 = (f32[512,128]{1,0:T(8,128)S(1)}, f32[512,128]{1,0:T(8,128)S(1)}, u32[]{:S(2)}, u32[]{:S(2)}) collective-permute-start(f32[512,128]{1,0:T(8,128)S(1)} %get-tuple-element.37), channel_id=1, source_target_pairs={{0,12},{4,8},{8,4},{12,0},{1,13},{5,9},{9,5},{13,1},{2,14},{6,10},... | collective-permute-start | bytes 786440 | tf_op jit(solution)/shard_map/ppermute | solution.py:251
  61.8 23.1 %collective-permute-start.3 = (f32[512,128]{1,0:T(8,128)S(1)}, f32[512,128]{1,0:T(8,128)S(1)}, u32[]{:S(2)}, u32[]{:S(2)}) collective-permute-start(f32[512,128]{1,0:T(8,128)S(1)} %get-tuple-element.38), channel_id=1, source_target_pairs={{0,8},{4,12},{8,0},{12,4},{1,9},{5,13},{9,1},{13,5},{2,10},{6,14},... | collective-permute-start | bytes 786440 | tf_op jit(solution)/shard_map/ppermute | solution.py:251
  62.9 22.0 %collective-permute-start.2 = (f32[512,128]{1,0:T(8,128)S(1)}, f32[512,128]{1,0:T(8,128)S(1)}, u32[]{:S(2)}, u32[]{:S(2)}) collective-permute-start(f32[512,128]{1,0:T(8,128)S(1)} %get-tuple-element.36), channel_id=1, source_target_pairs={{0,4},{4,0},{8,12},{12,8},{1,5},{5,1},{9,13},{13,9},{2,6},{6,2},{1... | collective-permute-start | bytes 786440 | tf_op jit(solution)/shard_map/ppermute | solution.py:251
  86.6 13.0 %collective-permute-start.5 = (f32[512,128]{1,0:T(8,128)}, f32[512,128]{1,0:T(8,128)S(1)}, u32[]{:S(2)}, u32[]{:S(2)}) collective-permute-start(f32[512,128]{1,0:T(8,128)} %shard_map.152), channel_id=1, source_target_pairs={{0,4},{4,0},{8,12},{12,8},{1,5},{5,1},{9,13},{13,9},{2,6},{6,2},{1... | collective-permute-start | bytes 786440 | tf_op jit(solution)/shard_map/ppermute | solution.py:251
  89.0 19.3 %collective-permute-start.6 = (f32[512,128]{1,0:T(8,128)}, f32[512,128]{1,0:T(8,128)S(1)}, u32[]{:S(2)}, u32[]{:S(2)}) collective-permute-start(f32[512,128]{1,0:T(8,128)} %shard_map.152), channel_id=1, source_target_pairs={{0,8},{4,12},{8,0},{12,4},{1,9},{5,13},{9,1},{13,5},{2,10},{6,14},... | collective-permute-start | bytes 786440 | tf_op jit(solution)/shard_map/ppermute | solution.py:251
  90.0 23.6 %collective-permute-start.7 = (f32[512,128]{1,0:T(8,128)}, f32[512,128]{1,0:T(8,128)S(1)}, u32[]{:S(2)}, u32[]{:S(2)}) collective-permute-start(f32[512,128]{1,0:T(8,128)} %shard_map.152), channel_id=1, source_target_pairs={{0,12},{4,8},{8,4},{12,0},{1,13},{5,9},{9,5},{13,1},{2,14},{6,10},... | collective-permute-start | bytes 786440 | tf_op jit(solution)/shard_map/ppermute | solution.py:251
  90.6 25.7 %collective-permute-start.8 = (f32[512,128]{1,0:T(8,128)}, f32[512,128]{1,0:T(8,128)S(1)}, u32[]{:S(2)}, u32[]{:S(2)}) collective-permute-start(f32[512,128]{1,0:T(8,128)} %shard_map.152), channel_id=1, source_target_pairs={{0,2},{1,3},{2,0},{3,1},{4,6},{5,7},{6,4},{7,5},{8,10},{9,11},{10,... | collective-permute-start | bytes 786440 | tf_op jit(solution)/shard_map/ppermute | solution.py:251
  99.6 16.7 %collective-permute-start.9 = (f32[512,128]{1,0:T(8,128)S(1)}, f32[512,128]{1,0:T(8,128)S(1)}, u32[]{:S(2)}, u32[]{:S(2)}) collective-permute-start(f32[512,128]{1,0:T(8,128)S(1)} %collective-permute-done.5), channel_id=1, source_target_pairs={{0,2},{1,3},{2,0},{3,1},{4,6},{5,7},{6,4},{7,5},{8,10},{9,11},{10,... | collective-permute-start | bytes 786440 | tf_op jit(solution)/shard_map/ppermute | solution.py:251
  114.6 10.3 %collective-permute-start.12 = (f32[2048,128]{1,0:T(8,128)S(1)}, f32[2048,128]{1,0:T(8,128)S(1)}, u32[]{:S(2)}, u32[]{:S(2)}) collective-permute-start(f32[2048,128]{1,0:T(8,128)S(1)} %pad_maximum_fusion.refs_6_), channel_id=1, source_target_pairs={{0,1},{1,0},{2,3},{3,2},{4,5},{5,4},{6,7},{7,6},{8,9},{9,8},{10,11... | collective-permute-start | bytes 3145736 | tf_op jit(solution)/shard_map/ppermute | solution.py:251
  134.9 14.2 %collective-permute-start.14 = (f32[1024,128]{1,0:T(8,128)}, f32[1024,128]{1,0:T(8,128)S(1)}, u32[]{:S(2)}, u32[]{:S(2)}) collective-permute-start(f32[1024,128]{1,0:T(8,128)} %shard_map.153.refs_6_), channel_id=1, source_target_pairs={{0,16},{16,0},{1,17},{17,1},{2,18},{18,2},{3,19},{19,3},{4,20},{20... | collective-permute-start | bytes 1572872 | tf_op jit(solution)/shard_map/ppermute | solution.py:251
  163.2 13.1 %collective-permute-start.16 = (f32[672,128]{1,0:T(8,128)S(1)}, f32[672,128]{1,0:T(8,128)S(1)}, u32[]{:S(2)}, u32[]{:S(2)}) collective-permute-start(f32[672,128]{1,0:T(8,128)S(1)} %bitcast.222), channel_id=1, source_target_pairs={{0,2},{1,3},{2,0},{3,1},{4,6},{5,7},{6,4},{7,5},{8,10},{9,11},{10,... | collective-permute-start | bytes 1032200 | tf_op jit(solution)/shard_map/ppermute | solution.py:251
  178.0 9.2 %collective-permute-start.18 = (f32[168,128]{1,0:T(8,128)S(1)}, f32[168,128]{1,0:T(8,128)S(1)}, u32[]{:S(2)}, u32[]{:S(2)}) collective-permute-start(f32[168,128]{1,0:T(8,128)S(1)} %get-tuple-element.29), channel_id=1, source_target_pairs={{0,8},{4,12},{8,0},{12,4},{1,9},{5,13},{9,1},{13,5},{2,10},{6,14},... | collective-permute-start | bytes 258056 | tf_op jit(solution)/shard_map/ppermute | solution.py:251
  191.5 11.8 %collective-permute-start.26 = (f32[256,128]{1,0:T(8,128)S(1)}, f32[256,128]{1,0:T(8,128)S(1)}, u32[]{:S(2)}, u32[]{:S(2)}) collective-permute-start(f32[256,128]{1,0:T(8,128)S(1)} %maximum_subtract_fusion), channel_id=1, source_target_pairs={{0,12},{4,8},{8,4},{12,0},{1,13},{5,9},{9,5},{13,1},{2,14},{6,10},... | collective-permute-start | bytes 393224 | tf_op jit(solution)/shard_map/ppermute | solution.py:251
  193.0 11.1 %collective-permute-start.25 = (f32[256,128]{1,0:T(8,128)S(1)}, f32[256,128]{1,0:T(8,128)S(1)}, u32[]{:S(2)}, u32[]{:S(2)}) collective-permute-start(f32[256,128]{1,0:T(8,128)S(1)} %maximum_subtract_fusion), channel_id=1, source_target_pairs={{0,8},{4,12},{8,0},{12,4},{1,9},{5,13},{9,1},{13,5},{2,10},{6,14},... | collective-permute-start | bytes 393224 | tf_op jit(solution)/shard_map/ppermute | solution.py:251
  194.5 11.8 %collective-permute-start.27 = (f32[256,128]{1,0:T(8,128)S(1)}, f32[256,128]{1,0:T(8,128)S(1)}, u32[]{:S(2)}, u32[]{:S(2)}) collective-permute-start(f32[256,128]{1,0:T(8,128)S(1)} %maximum_subtract_fusion), channel_id=1, source_target_pairs={{0,2},{1,3},{2,0},{3,1},{4,6},{5,7},{6,4},{7,5},{8,10},{9,11},{10,... | collective-permute-start | bytes 393224 | tf_op jit(solution)/shard_map/ppermute | solution.py:251
  196.0 10.3 %collective-permute-start.28 = (f32[256,128]{1,0:T(8,128)S(1)}, f32[256,128]{1,0:T(8,128)S(1)}, u32[]{:S(2)}, u32[]{:S(2)}) collective-permute-start(f32[256,128]{1,0:T(8,128)S(1)} %collective-permute-done.24), channel_id=1, source_target_pairs={{0,2},{1,3},{2,0},{3,1},{4,6},{5,7},{6,4},{7,5},{8,10},{9,11},{10,... | collective-permute-start | bytes 393224 | tf_op jit(solution)/shard_map/ppermute | solution.py:251
  204.1 10.1 %collective-permute-start.31 = (f32[1024,128]{1,0:T(8,128)S(1)}, f32[1024,128]{1,0:T(8,128)S(1)}, u32[]{:S(2)}, u32[]{:S(2)}) collective-permute-start(f32[1024,128]{1,0:T(8,128)S(1)} %pad_maximum_fusion.2.refs_6_), channel_id=1, source_target_pairs={{0,1},{1,0},{2,3},{3,2},{4,5},{5,4},{6,7},{7,6},{8,9},{9,8},{10,11... | collective-permute-start | bytes 1572872 | tf_op jit(solution)/shard_map/ppermute | solution.py:251
  240.1 10.5 %collective-permute-start.35 = (f32[672,128]{1,0:T(8,128)S(1)}, f32[672,128]{1,0:T(8,128)S(1)}, u32[]{:S(2)}, u32[]{:S(2)}) collective-permute-start(f32[672,128]{1,0:T(8,128)S(1)} %bitcast.223), channel_id=1, source_target_pairs={{0,2},{1,3},{2,0},{3,1},{4,6},{5,7},{6,4},{7,5},{8,10},{9,11},{10,... | collective-permute-start | bytes 1032200 | tf_op jit(solution)/shard_map/ppermute | solution.py:251
  242.7 13.9 %collective-permute-start.41 = (f32[176,128]{1,0:T(8,128)S(1)}, f32[176,128]{1,0:T(8,128)S(1)}, u32[]{:S(2)}, u32[]{:S(2)}) collective-permute-start(f32[176,128]{1,0:T(8,128)S(1)} %bitcast.231), channel_id=1, source_target_pairs={{0,12},{4,8},{8,4},{12,0},{1,13},{5,9},{9,5},{13,1},{2,14},{6,10},... | collective-permute-start | bytes 270344 | tf_op jit(solution)/shard_map/ppermute | solution.py:251
  243.4 13.2 %collective-permute-start.40 = (f32[176,128]{1,0:T(8,128)S(1)}, f32[176,128]{1,0:T(8,128)S(1)}, u32[]{:S(2)}, u32[]{:S(2)}) collective-permute-start(f32[176,128]{1,0:T(8,128)S(1)} %bitcast.228), channel_id=1, source_target_pairs={{0,8},{4,12},{8,0},{12,4},{1,9},{5,13},{9,1},{13,5},{2,10},{6,14},... | collective-permute-start | bytes 270344 | tf_op jit(solution)/shard_map/ppermute | solution.py:251
  247.6 9.0 %collective-permute-start.39 = (f32[176,128]{1,0:T(8,128)S(1)}, f32[176,128]{1,0:T(8,128)S(1)}, u32[]{:S(2)}, u32[]{:S(2)}) collective-permute-start(f32[176,128]{1,0:T(8,128)S(1)} %bitcast.227), channel_id=1, source_target_pairs={{0,4},{4,0},{8,12},{12,8},{1,5},{5,1},{9,13},{13,9},{2,6},{6,2},{1... | collective-permute-start | bytes 270344 | tf_op jit(solution)/shard_map/ppermute | solution.py:251
  252.4 9.1 %collective-permute-start.37 = (f32[168,128]{1,0:T(8,128)S(1)}, f32[168,128]{1,0:T(8,128)S(1)}, u32[]{:S(2)}, u32[]{:S(2)}) collective-permute-start(f32[168,128]{1,0:T(8,128)S(1)} %get-tuple-element.26), channel_id=1, source_target_pairs={{0,8},{4,12},{8,0},{12,4},{1,9},{5,13},{9,1},{13,5},{2,10},{6,14},... | collective-permute-start | bytes 258056 | tf_op jit(solution)/shard_map/ppermute | solution.py:251
  265.7 10.5 %collective-permute-start.44 = (f32[256,128]{1,0:T(8,128)S(1)}, f32[256,128]{1,0:T(8,128)S(1)}, u32[]{:S(2)}, u32[]{:S(2)}) collective-permute-start(f32[256,128]{1,0:T(8,128)S(1)} %pad_maximum_fusion.4), channel_id=1, source_target_pairs={{0,8},{4,12},{8,0},{12,4},{1,9},{5,13},{9,1},{13,5},{2,10},{6,14},... | collective-permute-start | bytes 393224 | tf_op jit(solution)/shard_map/ppermute | solution.py:251
  266.7 12.4 %collective-permute-start.45 = (f32[256,128]{1,0:T(8,128)S(1)}, f32[256,128]{1,0:T(8,128)S(1)}, u32[]{:S(2)}, u32[]{:S(2)}) collective-permute-start(f32[256,128]{1,0:T(8,128)S(1)} %pad_maximum_fusion.4), channel_id=1, source_target_pairs={{0,12},{4,8},{8,4},{12,0},{1,13},{5,9},{9,5},{13,1},{2,14},{6,10},... | collective-permute-start | bytes 393224 | tf_op jit(solution)/shard_map/ppermute | solution.py:251
  267.8 13.5 %collective-permute-start.46 = (f32[256,128]{1,0:T(8,128)S(1)}, f32[256,128]{1,0:T(8,128)S(1)}, u32[]{:S(2)}, u32[]{:S(2)}) collective-permute-start(f32[256,128]{1,0:T(8,128)S(1)} %pad_maximum_fusion.4), channel_id=1, source_target_pairs={{0,2},{1,3},{2,0},{3,1},{4,6},{5,7},{6,4},{7,5},{8,10},{9,11},{10,... | collective-permute-start | bytes 393224 | tf_op jit(solution)/shard_map/ppermute | solution.py:251
  270.6 10.7 %collective-permute-start.47 = (f32[256,128]{1,0:T(8,128)S(1)}, f32[256,128]{1,0:T(8,128)S(1)}, u32[]{:S(2)}, u32[]{:S(2)}) collective-permute-start(f32[256,128]{1,0:T(8,128)S(1)} %collective-permute-done.43), channel_id=1, source_target_pairs={{0,2},{1,3},{2,0},{3,1},{4,6},{5,7},{6,4},{7,5},{8,10},{9,11},{10,... | collective-permute-start | bytes 393224 | tf_op jit(solution)/shard_map/ppermute | solution.py:251
  279.1 8.9 %collective-permute-start.50 = (f32[1024,128]{1,0:T(8,128)S(1)}, f32[1024,128]{1,0:T(8,128)S(1)}, u32[]{:S(2)}, u32[]{:S(2)}) collective-permute-start(f32[1024,128]{1,0:T(8,128)S(1)} %constant_dynamic-update-slice_fusion.8.refs_6_), channel_id=1, source_target_pairs={{0,1},{1,0},{2,3},{3,2},{4,5},{5,4},{6,7},{7,6},{8,9},{9,8},{10,11... | collective-permute-start | bytes 1572872 | tf_op jit(solution)/shard_map/ppermute | solution.py:251
  298.7 14.2 %collective-permute-start.52 = (f32[1024,128]{1,0:T(8,128)}, f32[1024,128]{1,0:T(8,128)S(1)}, u32[]{:S(2)}, u32[]{:S(2)}) collective-permute-start(f32[1024,128]{1,0:T(8,128)} %get-tuple-element.8.refs_8_), channel_id=1, source_target_pairs={{0,16},{16,0},{1,17},{17,1},{2,18},{18,2},{3,19},{19,3},{4,20},{20... | collective-permute-start | bytes 1572872 | tf_op jit(solution)/shard_map/ppermute | solution.py:251
  328.7 19.0 %collective-permute-start.54 = (f32[1376,128]{1,0:T(8,128)S(1)}, f32[1376,128]{1,0:T(8,128)S(1)}, u32[]{:S(2)}, u32[]{:S(2)}) collective-permute-start(f32[1376,128]{1,0:T(8,128)S(1)} %bitcast.221), channel_id=1, source_target_pairs={{0,2},{1,3},{2,0},{3,1},{4,6},{5,7},{6,4},{7,5},{8,10},{9,11},{10,... | collective-permute-start | bytes 2113544 | tf_op jit(solution)/shard_map/ppermute | solution.py:251
  330.3 15.7 %collective-permute-start.60 = (f32[336,128]{1,0:T(8,128)S(1)}, f32[336,128]{1,0:T(8,128)S(1)}, u32[]{:S(2)}, u32[]{:S(2)}) collective-permute-start(f32[336,128]{1,0:T(8,128)S(1)} %bitcast.226), channel_id=1, source_target_pairs={{0,12},{4,8},{8,4},{12,0},{1,13},{5,9},{9,5},{13,1},{2,14},{6,10},... | collective-permute-start | bytes 516104 | tf_op jit(solution)/shard_map/ppermute | solution.py:251
  331.9 15.0 %collective-permute-start.59 = (f32[336,128]{1,0:T(8,128)S(1)}, f32[336,128]{1,0:T(8,128)S(1)}, u32[]{:S(2)}, u32[]{:S(2)}) collective-permute-start(f32[336,128]{1,0:T(8,128)S(1)} %bitcast.225), channel_id=1, source_target_pairs={{0,8},{4,12},{8,0},{12,4},{1,9},{5,13},{9,1},{13,5},{2,10},{6,14},... | collective-permute-start | bytes 516104 | tf_op jit(solution)/shard_map/ppermute | solution.py:251
  332.8 14.1 %collective-permute-start.58 = (f32[336,128]{1,0:T(8,128)S(1)}, f32[336,128]{1,0:T(8,128)S(1)}, u32[]{:S(2)}, u32[]{:S(2)}) collective-permute-start(f32[336,128]{1,0:T(8,128)S(1)} %bitcast.224), channel_id=1, source_target_pairs={{0,4},{4,0},{8,12},{12,8},{1,5},{5,1},{9,13},{13,9},{2,6},{6,2},{1... | collective-permute-start | bytes 516104 | tf_op jit(solution)/shard_map/ppermute | solution.py:251
  347.8 14.9 %collective-permute-start.57 = (f32[344,128]{1,0:T(8,128)S(1)}, f32[344,128]{1,0:T(8,128)S(1)}, u32[]{:S(2)}, u32[]{:S(2)}) collective-permute-start(f32[344,128]{1,0:T(8,128)S(1)} %get-tuple-element.19), channel_id=1, source_target_pairs={{0,12},{4,8},{8,4},{12,0},{1,13},{5,9},{9,5},{13,1},{2,14},{6,10},... | collective-permute-start | bytes 528392 | tf_op jit(solution)/shard_map/ppermute | solution.py:251
  348.6 15.0 %collective-permute-start.56 = (f32[344,128]{1,0:T(8,128)S(1)}, f32[344,128]{1,0:T(8,128)S(1)}, u32[]{:S(2)}, u32[]{:S(2)}) collective-permute-start(f32[344,128]{1,0:T(8,128)S(1)} %get-tuple-element.20), channel_id=1, source_target_pairs={{0,8},{4,12},{8,0},{12,4},{1,9},{5,13},{9,1},{13,5},{2,10},{6,14},... | collective-permute-start | bytes 528392 | tf_op jit(solution)/shard_map/ppermute | solution.py:251
  352.7 11.7 %collective-permute-start.55 = (f32[344,128]{1,0:T(8,128)S(1)}, f32[344,128]{1,0:T(8,128)S(1)}, u32[]{:S(2)}, u32[]{:S(2)}) collective-permute-start(f32[344,128]{1,0:T(8,128)S(1)} %get-tuple-element.18), channel_id=1, source_target_pairs={{0,4},{4,0},{8,12},{12,8},{1,5},{5,1},{9,13},{13,9},{2,6},{6,2},{1... | collective-permute-start | bytes 528392 | tf_op jit(solution)/shard_map/ppermute | solution.py:251
  365.2 20.7 %collective-permute-start.64 = (f32[512,128]{1,0:T(8,128)}, f32[512,128]{1,0:T(8,128)S(1)}, u32[]{:S(2)}, u32[]{:S(2)}) collective-permute-start(f32[512,128]{1,0:T(8,128)} %shard_map.163), channel_id=1, source_target_pairs={{0,12},{4,8},{8,4},{12,0},{1,13},{5,9},{9,5},{13,1},{2,14},{6,10},... | collective-permute-start | bytes 786440 | tf_op jit(solution)/shard_map/ppermute | solution.py:251
  365.7 21.9 %collective-permute-start.63 = (f32[512,128]{1,0:T(8,128)}, f32[512,128]{1,0:T(8,128)S(1)}, u32[]{:S(2)}, u32[]{:S(2)}) collective-permute-start(f32[512,128]{1,0:T(8,128)} %shard_map.163), channel_id=1, source_target_pairs={{0,8},{4,12},{8,0},{12,4},{1,9},{5,13},{9,1},{13,5},{2,10},{6,14},... | collective-permute-start | bytes 786440 | tf_op jit(solution)/shard_map/ppermute | solution.py:251
  369.9 17.6 %collective-permute-start.62 = (f32[512,128]{1,0:T(8,128)}, f32[512,128]{1,0:T(8,128)S(1)}, u32[]{:S(2)}, u32[]{:S(2)}) collective-permute-start(f32[512,128]{1,0:T(8,128)} %shard_map.163), channel_id=1, source_target_pairs={{0,4},{4,0},{8,12},{12,8},{1,5},{5,1},{9,13},{13,9},{2,6},{6,2},{1... | collective-permute-start | bytes 786440 | tf_op jit(solution)/shard_map/ppermute | solution.py:251
  406.1 25.5 %collective-permute-start.66 = (f32[2048,128]{1,0:T(8,128)}, f32[2048,128]{1,0:T(8,128)S(1)}, u32[]{:S(2)}, u32[]{:S(2)}) collective-permute-start(f32[2048,128]{1,0:T(8,128)} %get-tuple-element.10), channel_id=1, source_target_pairs={{0,16},{16,0},{1,17},{17,1},{2,18},{18,2},{3,19},{19,3},{4,20},{20... | collective-permute-start | bytes 3145736 | tf_op jit(solution)/shard_map/ppermute | solution.py:251
  407.7 81.7 %collective-permute-start.73 = (f32[4096,128]{1,0:T(8,128)}, f32[4096,128]{1,0:T(8,128)}, u32[]{:S(2)}, u32[]{:S(2)}) collective-permute-start(f32[4096,128]{1,0:T(8,128)} %get-tuple-element.11), channel_id=1, source_target_pairs={{0,2},{1,3},{2,0},{3,1},{4,6},{5,7},{6,4},{7,5},{8,10},{9,11},{10,... | collective-permute-start | bytes 6291464 | tf_op jit(solution)/shard_map/ppermute | solution.py:251
  438.7 37.6 %collective-permute-start.69 = (f32[1024,128]{1,0:T(8,128)}, f32[1024,128]{1,0:T(8,128)S(1)}, u32[]{:S(2)}, u32[]{:S(2)}) collective-permute-start(f32[1024,128]{1,0:T(8,128)} %shard_map.168), channel_id=1, source_target_pairs={{0,12},{4,8},{8,4},{12,0},{1,13},{5,9},{9,5},{13,1},{2,14},{6,10},... | collective-permute-start | bytes 1572872 | tf_op jit(solution)/shard_map/ppermute | solution.py:251
  445.1 40.0 %collective-permute-start.68 = (f32[1024,128]{1,0:T(8,128)}, f32[1024,128]{1,0:T(8,128)S(1)}, u32[]{:S(2)}, u32[]{:S(2)}) collective-permute-start(f32[1024,128]{1,0:T(8,128)} %shard_map.167), channel_id=1, source_target_pairs={{0,8},{4,12},{8,0},{12,4},{1,9},{5,13},{9,1},{13,5},{2,10},{6,14},... | collective-permute-start | bytes 1572872 | tf_op jit(solution)/shard_map/ppermute | solution.py:251
  454.1 31.1 %collective-permute-start.67 = (f32[1024,128]{1,0:T(8,128)}, f32[1024,128]{1,0:T(8,128)S(1)}, u32[]{:S(2)}, u32[]{:S(2)}) collective-permute-start(f32[1024,128]{1,0:T(8,128)} %shard_map.166), channel_id=1, source_target_pairs={{0,4},{4,0},{8,12},{12,8},{1,5},{5,1},{9,13},{13,9},{2,6},{6,2},{1... | collective-permute-start | bytes 1572872 | tf_op jit(solution)/shard_map/ppermute | solution.py:251
  485.5 22.0 %collective-permute-start.70 = (f32[1024,128]{1,0:T(8,128)S(1)}, f32[1024,128]{1,0:T(8,128)S(1)}, u32[]{:S(2)}, u32[]{:S(2)}) collective-permute-start(f32[1024,128]{1,0:T(8,128)S(1)} %get-tuple-element.13), channel_id=1, source_target_pairs={{0,4},{4,0},{8,12},{12,8},{1,5},{5,1},{9,13},{13,9},{2,6},{6,2},{1... | collective-permute-start | bytes 1572872 | tf_op jit(solution)/shard_map/ppermute | solution.py:251
  487.7 36.0 %collective-permute-start.71 = (f32[1024,128]{1,0:T(8,128)S(1)}, f32[1024,128]{1,0:T(8,128)S(1)}, u32[]{:S(2)}, u32[]{:S(2)}) collective-permute-start(f32[1024,128]{1,0:T(8,128)S(1)} %get-tuple-element.13), channel_id=1, source_target_pairs={{0,8},{4,12},{8,0},{12,4},{1,9},{5,13},{9,1},{13,5},{2,10},{6,14},... | collective-permute-start | bytes 1572872 | tf_op jit(solution)/shard_map/ppermute | solution.py:251
  488.9 44.5 %collective-permute-start.72 = (f32[1024,128]{1,0:T(8,128)S(1)}, f32[1024,128]{1,0:T(8,128)S(1)}, u32[]{:S(2)}, u32[]{:S(2)}) collective-permute-start(f32[1024,128]{1,0:T(8,128)S(1)} %get-tuple-element.13), channel_id=1, source_target_pairs={{0,12},{4,8},{8,4},{12,0},{1,13},{5,9},{9,5},{13,1},{2,14},{6,10},... | collective-permute-start | bytes 1572872 | tf_op jit(solution)/shard_map/ppermute | solution.py:251
  (56 other events, 410.0 us)
